TPU v7x, 256 devices: a whole 4x4x8 slice. The times are simulated.
256 devices in a mesh: comp: 32 (over y, z), harm: 8 (over x, core).
Axes of the slice: x: 4, y: 4, z: 8, core: 2. Of those that a mesh axis runs over, the one named last changes fastest.
Arguments:
- load: float32 [128, 131072], P('harm', 'comp'), may hold values from -6 to 6
- stiff_blocks: bfloat16 [1024, 8, 128, 128], P('comp'), as said below
- mass_blocks: bfloat16 [1024, 8, 128, 128], P('comp'), as said below
- block_cols: int32 [1024, 8], P('comp'), may hold values from -8 to 1031, as said below
- contact_rows: int32 [32, 256], P('comp'), may hold values from 0 to 4095, as said below
- partner_slot: int32 [32, 256], P('comp'), may hold values from 0 to 255, each once within a row
- contact_count: int32 [32], P('comp'), may hold values from 32 to 256, as said below
- normal_load: float32 [32, 256], P('comp'), may hold values from 0.3 to 3
- contact_stiffness: float32 [32, 256], P('comp'), may hold values from 0.3 to 3
- frequency: float32 [1], replicated, may hold values from 0.2 to 1
Outputs:
- displacement: float32 [128, 131072], P('harm', 'comp')
- residual: float32 [128, 131072], P('harm', 'comp')
Inputs may be any that keep to these rules, and one draw needn't show every extreme that they name: `block_cols`: entry 0 of block row r is r; its other 7 entries are distinct, differ from r by 1 to 8, and include r - 8 and r + 8; columns outside 0 .. 1023 refer to zero parts of the field. `contact_rows`: the 256 entries of one group are distinct. Slots 0 .. contact_count[d]-1 of group d are live; the others carry no force. `stiff_blocks`: slot 0 of every block row is the block on the diagonal. `mass_blocks`: slot 0 of every block row is the block on the diagonal.
All inputs are finite; a program needn't handle non-finite values.
Results may differ from a plain program's by a relative error of at most 0.015.
The roundings to bfloat16 on the way count: a program that leaves them out, or rounds other values in their place, can miss the bound.
Values may be sent and summed in bfloat16 or wider, within the bound.
No kernel may reach another device: no remote copies, remote signals or barrier semaphores. Data moves between devices by JAX's collectives and lax.ppermute only.
A program may use at most 64 MiB of HBM per device.

v0:
```python
import math

import jax
import jax.numpy as jnp
from jax import lax
from jax.sharding import PartitionSpec as P

H = 128
TIME_POINTS = 1024
BLK = 128
BAND = 8
ITERS = 3


def with_halo(value, sides, width):
    for axis, dim in sides:
        size, length = (lax.axis_size(axis), value.shape[dim])
        up = [(i, (i + 1) % size) for i in range(size - 1)]
        down = [(j, i) for i, j in up]
        last = lax.slice_in_dim(value, length - width, length, axis=dim)
        leading = lax.slice_in_dim(value, 0, width, axis=dim)
        before = lax.ppermute(last, axis, up)
        after = lax.ppermute(leading, axis, down)
        value = jnp.concatenate([before, value, after], axis=dim)
    return value


def swapped(block, axis, apart):
    count = lax.axis_size(axis)
    route = []
    for low in range(count):
        high = low | 1 << apart
        if high != low and high < count:
            route += [(low, high), (high, low)]
    return lax.ppermute(block, axis, route)


def harmonic_tables():
    column_list = jnp.arange(H, dtype=jnp.int32)
    harmonic_orders = jnp.where(column_list <= H // 2, column_list, column_list - H // 2)
    time_points = jnp.arange(TIME_POINTS, dtype=jnp.int32)
    phase_values = time_points[:, None] * harmonic_orders[None, :] % TIME_POINTS
    phase_angles = phase_values.astype(jnp.float32) * (2.0 * math.pi / TIME_POINTS)
    instant_table = jnp.where(
        column_list[None, :] <= H // 2, jnp.cos(phase_angles), jnp.sin(phase_angles)
    )
    weight_factors = jnp.where(column_list == 0, 1.0, 2.0).astype(jnp.float32) / TIME_POINTS
    return (instant_table, weight_factors, harmonic_orders)


def time_force(time_values, load_part, stiff_part, live_mask):
    return jnp.where(live_mask, load_part * jnp.tanh(stiff_part * time_values / load_part), 0.0)


def local(
    load,
    stiff_blocks,
    mass_blocks,
    block_cols,
    contact_rows,
    partner_slot,
    contact_count,
    normal_load,
    contact_stiffness,
    frequency,
):
    local_harm, local_dofs = load.shape
    block_rows = stiff_blocks.shape[0]
    harm_index = lax.axis_index("harm")
    first_harm = harm_index * local_harm
    first_row = lax.axis_index("comp") * block_rows
    partner_bit = lax.axis_size("comp").bit_length() - 2
    instant_table, weight_factors, harmonic_orders = harmonic_tables()
    own_waves = lax.dynamic_slice_in_dim(harmonic_orders, first_harm, local_harm)
    own_weights = lax.dynamic_slice_in_dim(weight_factors, first_harm, local_harm)
    factor = frequency[0] * own_waves.astype(jnp.float32) * (2.0 / H)
    factor = factor * factor
    stiff_diag = (
        jnp.diagonal(stiff_blocks[:, 0], axis1=1, axis2=2).astype(jnp.float32).reshape(local_dofs)
    )
    mass_diag = (
        jnp.diagonal(mass_blocks[:, 0], axis1=1, axis2=2).astype(jnp.float32).reshape(local_dofs)
    )
    dynamic = stiff_diag[None, :] - factor[:, None] * mass_diag[None, :]
    local_cols = block_cols - first_row + BAND
    slot_rows = contact_rows[0]
    slot_partner = partner_slot[0]
    slot_count = contact_count[0]
    slot_loads = normal_load[0]
    slot_stiffs = contact_stiffness[0]
    slot_ids = jnp.arange(slot_rows.shape[0], dtype=jnp.int32)
    displacement = load / dynamic
    residual = jnp.zeros_like(displacement)
    for sweep_index in range(ITERS):
        rounded = displacement.astype(jnp.bfloat16)
        gap = displacement - lax.optimization_barrier(rounded).astype(jnp.float32)
        extended = with_halo(rounded, (("comp", 1),), BAND * BLK)
        blocked = extended.reshape(local_harm, block_rows + 2 * BAND, BLK)
        picked = blocked[:, local_cols, :]
        stiff_part = jnp.einsum(
            "rsij,hrsj->hri", stiff_blocks, picked, preferred_element_type=jnp.float32
        ).reshape(local_harm, local_dofs)
        mass_part = jnp.einsum(
            "rsij,hrsj->hri", mass_blocks, picked, preferred_element_type=jnp.float32
        ).reshape(local_harm, local_dofs)
        stiff_part = stiff_part + stiff_diag[None, :] * gap
        mass_part = mass_part + mass_diag[None, :] * gap
        listed = displacement[:, slot_rows]
        mirrored = swapped(listed, "comp", partner_bit)
        relative = listed - mirrored[:, slot_partner]
        gathered = lax.all_gather(relative, "harm", axis=0, tiled=True)
        time_values = jnp.dot(instant_table, gathered, precision=lax.Precision.HIGHEST)
        live_mask = (slot_ids < slot_count)[None, :]
        forces = time_force(time_values, slot_loads[None, :], slot_stiffs[None, :], live_mask)
        own_table = lax.dynamic_slice_in_dim(instant_table, first_harm, local_harm, 1)
        own_force = (
            lax.dot_general(
                own_table, forces, (((0,), (0,)), ((), ())), precision=lax.Precision.HIGHEST
            )
            * own_weights[:, None]
        )
        residual = (
            load
            - (stiff_part - factor[:, None] * mass_part)
            - jnp.zeros_like(displacement).at[:, slot_rows].add(own_force)
        )
        displacement = displacement + residual / dynamic
    return (displacement, residual)


def solution(mesh):
    placed = (
        P("harm", "comp"),
        P("comp", None, None, None),
        P("comp", None, None, None),
        P("comp", None),
        P("comp", None),
        P("comp", None),
        P("comp"),
        P("comp", None),
        P("comp", None),
        P(),
    )
    return jax.shard_map(
        local,
        mesh=mesh,
        in_specs=placed,
        out_specs=(P("harm", "comp"), P("harm", "comp")),
        check_vma=False,
    )
```

profile of v0, /device:TPU:9, one launch (start us, length us, event | category | flops | bytes accessed | tf_op | source)
XLA Modules:
  0.0 161.0 jit_solution(14914162382840452449)
XLA Ops:
  1.3 1.3 slice.24
  2.6 3.3 %copy.207 = bf16[32,1,128,128]{0,3,2,1:T(8,128)(2,1)} copy(bf16[32,1,128,128]{3,2,1,0:T(8,128)(2,1)S(1)} %slice.24) | data formatting | bytes 2097152
  5.9 1.9 %gather_fusion = bf16[128,32]{1,0:T(8,128)(2,1)S(1)} fusion(bf16[32,128,128]{0,2,1:T(8,128)(2,1)} %bitcast.181, s32[128]{0:T(128)S(1)} %or_bitcast_fusion), kind=kCustom, calls=%fused_computation | custom fusion | bytes 17408 | tf_op jit(solution)/shard_map/jit(diagonal)/gather | solution.py:79
  8.0 3.3 %copy.208 = bf16[32,1,128,128]{0,3,2,1:T(8,128)(2,1)} copy(bf16[32,1,128,128]{3,2,1,0:T(8,128)(2,1)S(1)} %slice-done) | data formatting | bytes 2097152
  11.2 1.9 %gather_fusion.1 = bf16[128,32]{1,0:T(8,128)(2,1)S(1)} fusion(bf16[32,128,128]{0,2,1:T(8,128)(2,1)} %bitcast.180, s32[128]{0:T(128)S(1)} %or_bitcast_fusion), kind=kCustom, calls=%fused_computation.1 | custom fusion | bytes 17408 | tf_op jit(solution)/shard_map/jit(diagonal)/gather | solution.py:82
  14.9 2.1 %collective-permute-start.2 = (f32[16,256]{0,1:T(8,128)S(1)}, f32[16,256]{0,1:T(8,128)S(1)}, u32[]{:S(2)}, u32[]{:S(2)}) collective-permute-start(f32[16,256]{0,1:T(8,128)S(1)} %bitcast.190), channel_id=1, source_target_pairs={{0,128},{128,0},{8,136},{136,8},{16,144},{144,16},{24,152},{152,24... | collective-permute-start | bytes 49160 | tf_op jit(solution)/shard_map/ppermute | solution.py:35
  17.6 3.5 %collective-permute-start = (bf16[16,1024]{1,0:T(8,128)(2,1)}, bf16[16,1024]{1,0:T(8,128)(2,1)S(1)}, u32[]{:S(2)}, u32[]{:S(2)}) collective-permute-start(bf16[16,1024]{1,0:T(8,128)(2,1)} %get-tuple-element.24), channel_id=1, source_target_pairs={{0,8},{8,16},{16,24},{24,32},{32,40},{40,48},{48,56},{56,64},{64,7... | collective-permute-start | bytes 98312 | tf_op jit(solution)/shard_map/ppermute | solution.py:22
  21.1 6.6 %collective-permute-start.1 = (bf16[16,1024]{1,0:T(8,128)(2,1)}, bf16[16,1024]{1,0:T(8,128)(2,1)S(1)}, u32[]{:S(2)}, u32[]{:S(2)}) collective-permute-start(bf16[16,1024]{1,0:T(8,128)(2,1)} %get-tuple-element.25), channel_id=1, source_target_pairs={{8,0},{16,8},{24,16},{32,24},{40,32},{48,40},{56,48},{64,56},{72,6... | collective-permute-start | bytes 98312 | tf_op jit(solution)/shard_map/ppermute | solution.py:23
  28.5 2.1 %sine_select_fusion = f32[1024,128]{1,0:T(8,128)S(1)} fusion(s32[128]{0:T(128)S(1)} %iota_select_fusion, pred[128]{0:T(512)(128)(4,1)S(1)} %iota_compare_fusion.1), kind=kLoop, calls=%fused_computation.53 | loop fusion | flops 1966080 | bytes 524928 | tf_op jit(solution)/shard_map/jit(_where)/select_n | solution.py:44
  31.7 14.3 %all_gather.9 = f32[128,256]{1,0:T(8,128)S(1)} all-gather(f32[16,256]{1,0:T(8,128)S(1)} %copy.184), channel_id=1, replica_groups=mesh['comp'=32,'harm'=8] {'harm'}, dimensions={0}, use_global_device_ids=true | all-gather | bytes 147456 | tf_op jit(solution)/shard_map/all_gather | solution.py:111
  46.0 3.6 %fusion.11 = f32[1024,256]{1,0:T(8,128)S(1)} fusion(f32[128,256]{1,0:T(8,128)S(1)} %all_gather.9, f32[256]{0:T(256)} %bitcast.198, f32[256]{0:T(256)} %bitcast.201, pred[256]{0:T(512)(128)(4,1)S(1)} %iota_compare_fusion, s32[128]{0:T(128)S(1)} %iota_select_fusion, pred[128]{0:T(512)(128)(4,1)S(1)} %iota_compare_fusion.1), kind=kOutput, calls=%fused_computation.28 | convolution fusion | flops 405667840 | bytes 1182592 | tf_op jit(solution)/shard_map/dot_general | solution.py:112
  50.9 1.9 %scatter_custom_fusion = f32[16,4096]{0,1:T(8,128)S(1)} fusion(s32[256]{0:T(256)S(1)} %bitcast.194, f32[256,16]{1,0:T(8,128)S(1)} %copy.185, f32[]{:T(128)} %constant.60.clone.1), kind=kCustom, calls=%fused_computation.45 | custom fusion | flops 4096 | bytes 262148 | tf_op jit(solution)/shard_map/scatter-add | solution.py:125
  52.9 1.3 copy.186
  55.1 5.7 %convolution_bitcast_fusion.4 = f32[32,2,8,128]{3,2,1,0:T(8,128)S(1)} fusion(bf16[16,32,8,128]{3,0,2,1:T(8,128)(2,1)S(1)} %bitcast.176, bf16[32,8,128,128]{3,2,1,0:T(8,128)(2,1)} %param.12), kind=kOutput, calls=%fused_computation.33 | convolution fusion | flops 134217728 | bytes 9699328 | tf_op jit(solution)/shard_map/rsij,hrsj->hri/dot_general | solution.py:103
  60.7 5.7 %convolution_bitcast_fusion.5 = f32[32,2,8,128]{3,2,1,0:T(8,128)S(1)} fusion(bf16[16,32,8,128]{3,0,2,1:T(8,128)(2,1)S(1)} %bitcast.177, bf16[32,8,128,128]{3,2,1,0:T(8,128)(2,1)} %param.11), kind=kOutput, calls=%fused_computation.34 | convolution fusion | flops 134217728 | bytes 9699328 | tf_op jit(solution)/shard_map/rsij,hrsj->hri/dot_general | solution.py:100
  68.8 1.9 %collective-permute-start.3 = (bf16[16,1024]{1,0:T(8,128)(2,1)}, bf16[16,1024]{1,0:T(8,128)(2,1)}, u32[]{:S(2)}, u32[]{:S(2)}) collective-permute-start(bf16[16,1024]{1,0:T(8,128)(2,1)} %get-tuple-element.22), channel_id=1, source_target_pairs={{0,8},{8,16},{16,24},{24,32},{32,40},{40,48},{48,56},{56,64},{64,7... | collective-permute-start | bytes 98312 | tf_op jit(solution)/shard_map/ppermute | solution.py:22
  70.7 5.5 %collective-permute-start.4 = (bf16[16,1024]{1,0:T(8,128)(2,1)}, bf16[16,1024]{1,0:T(8,128)(2,1)}, u32[]{:S(2)}, u32[]{:S(2)}) collective-permute-start(bf16[16,1024]{1,0:T(8,128)(2,1)} %get-tuple-element.23), channel_id=1, source_target_pairs={{8,0},{16,8},{24,16},{32,24},{40,32},{48,40},{56,48},{64,56},{72,6... | collective-permute-start | bytes 98312 | tf_op jit(solution)/shard_map/ppermute | solution.py:23
  77.0 13.5 %all_gather.10 = f32[128,256]{1,0:T(8,128)S(1)} all-gather(f32[16,256]{1,0:T(8,128)S(1)} %copy.191), channel_id=1, replica_groups=mesh['comp'=32,'harm'=8] {'harm'}, dimensions={0}, use_global_device_ids=true | all-gather | bytes 147456 | tf_op jit(solution)/shard_map/all_gather | solution.py:111
  90.5 3.6 %fusion.7 = f32[1024,256]{1,0:T(8,128)S(1)} fusion(f32[128,256]{1,0:T(8,128)S(1)} %all_gather.10, f32[256]{0:T(256)} %bitcast.199, f32[256]{0:T(256)} %bitcast.202, pred[256]{0:T(512)(128)(4,1)} %copy-done.20, s32[128]{0:T(128)} %copy-done.16, pred[128]{0:T(512)(128)(4,1)} %copy-done.19), kind=kOutput, calls=%fused_computation.23 | convolution fusion | flops 405667840 | bytes 1182592 | tf_op jit(solution)/shard_map/dot_general | solution.py:112
  94.2 1.1 fusion.13
  95.4 2.1 %scatter_custom_fusion.1 = f32[16,4096]{0,1:T(8,128)S(1)} fusion(s32[256]{0:T(256)} %bitcast.195, f32[256,16]{1,0:T(8,128)S(1)} %copy.192, f32[]{:T(128)} %constant.60.clone.1), kind=kCustom, calls=%fused_computation.43 | custom fusion | flops 4096 | bytes 262656 | tf_op jit(solution)/shard_map/scatter-add | solution.py:125
  97.5 1.3 copy.193
  100.5 5.7 %convolution_bitcast_fusion.2 = f32[32,2,8,128]{3,2,1,0:T(8,128)S(1)} fusion(bf16[16,32,8,128]{3,0,2,1:T(8,128)(2,1)S(1)} %bitcast.178, bf16[32,8,128,128]{3,2,1,0:T(8,128)(2,1)} %param.12), kind=kOutput, calls=%fused_computation.31 | convolution fusion | flops 134217728 | bytes 9699328 | tf_op jit(solution)/shard_map/rsij,hrsj->hri/dot_general | solution.py:103
  106.1 5.7 %convolution_bitcast_fusion.3 = f32[32,2,8,128]{3,2,1,0:T(8,128)S(1)} fusion(bf16[16,32,8,128]{3,0,2,1:T(8,128)(2,1)S(1)} %bitcast.179, bf16[32,8,128,128]{3,2,1,0:T(8,128)(2,1)} %param.11), kind=kOutput, calls=%fused_computation.32 | convolution fusion | flops 134217728 | bytes 9699328 | tf_op jit(solution)/shard_map/rsij,hrsj->hri/dot_general | solution.py:100
  113.4 3.3 %collective-permute-start.8 = (f32[16,256]{0,1:T(8,128)S(1)}, f32[16,256]{0,1:T(8,128)S(1)}, u32[]{:S(2)}, u32[]{:S(2)}) collective-permute-start(f32[16,256]{0,1:T(8,128)S(1)} %bitcast.191), channel_id=1, source_target_pairs={{0,128},{128,0},{8,136},{136,8},{16,144},{144,16},{24,152},{152,24... | collective-permute-start | bytes 49160 | tf_op jit(solution)/shard_map/ppermute | solution.py:35
  117.4 1.9 %collective-permute-start.6 = (bf16[16,1024]{1,0:T(8,128)(2,1)}, bf16[16,1024]{1,0:T(8,128)(2,1)}, u32[]{:S(2)}, u32[]{:S(2)}) collective-permute-start(bf16[16,1024]{1,0:T(8,128)(2,1)} %get-tuple-element.20), channel_id=1, source_target_pairs={{0,8},{8,16},{16,24},{24,32},{32,40},{40,48},{48,56},{56,64},{64,7... | collective-permute-start | bytes 98312 | tf_op jit(solution)/shard_map/ppermute | solution.py:22
  119.3 5.5 %collective-permute-start.7 = (bf16[16,1024]{1,0:T(8,128)(2,1)}, bf16[16,1024]{1,0:T(8,128)(2,1)}, u32[]{:S(2)}, u32[]{:S(2)}) collective-permute-start(bf16[16,1024]{1,0:T(8,128)(2,1)} %get-tuple-element.21), channel_id=1, source_target_pairs={{8,0},{16,8},{24,16},{32,24},{40,32},{48,40},{56,48},{64,56},{72,6... | collective-permute-start | bytes 98312 | tf_op jit(solution)/shard_map/ppermute | solution.py:23
  125.6 13.9 %all_gather.11 = f32[128,256]{1,0:T(8,128)S(1)} all-gather(f32[16,256]{1,0:T(8,128)S(1)} %copy.198), channel_id=1, replica_groups=mesh['comp'=32,'harm'=8] {'harm'}, dimensions={0}, use_global_device_ids=true | all-gather | bytes 147456 | tf_op jit(solution)/shard_map/all_gather | solution.py:111
  139.4 3.6 %fusion.3 = f32[1024,256]{1,0:T(8,128)S(1)} fusion(f32[128,256]{1,0:T(8,128)S(1)} %all_gather.11, f32[256]{0:T(256)} %bitcast.200, f32[256]{0:T(256)} %bitcast.203, pred[256]{0:T(512)(128)(4,1)} %copy-done.20, s32[128]{0:T(128)} %copy-done.16, pred[128]{0:T(512)(128)(4,1)} %copy-done.19), kind=kOutput, calls=%fused_computation.18 | convolution fusion | flops 405667840 | bytes 1182592 | tf_op jit(solution)/shard_map/dot_general | solution.py:112
  144.3 2.1 %scatter_custom_fusion.2 = f32[16,4096]{0,1:T(8,128)S(1)} fusion(s32[256]{0:T(256)} %bitcast.196, f32[256,16]{1,0:T(8,128)S(1)} %copy.199, f32[]{:T(128)} %constant.60.clone.1), kind=kCustom, calls=%fused_computation.41 | custom fusion | flops 4096 | bytes 262656 | tf_op jit(solution)/shard_map/scatter-add | solution.py:125
  148.7 5.7 %convolution_bitcast_fusion = f32[32,2,8,128]{3,2,1,0:T(8,128)S(1)} fusion(bf16[16,32,8,128]{3,0,2,1:T(8,128)(2,1)S(1)} %bitcast.174, bf16[32,8,128,128]{3,2,1,0:T(8,128)(2,1)} %param.12), kind=kOutput, calls=%fused_computation.29 | convolution fusion | flops 134217728 | bytes 9699328 | tf_op jit(solution)/shard_map/rsij,hrsj->hri/dot_general | solution.py:103
  154.3 5.7 %convolution_bitcast_fusion.1 = f32[32,2,8,128]{3,2,1,0:T(8,128)S(1)} fusion(bf16[16,32,8,128]{3,0,2,1:T(8,128)(2,1)S(1)} %bitcast.175, bf16[32,8,128,128]{3,2,1,0:T(8,128)(2,1)} %param.11), kind=kOutput, calls=%fused_computation.30 | convolution fusion | flops 134217728 | bytes 9699328 | tf_op jit(solution)/shard_map/rsij,hrsj->hri/dot_general | solution.py:100
  (107 shorter events, 17.8 us)
Async XLA Ops:
  0.6 45.4 %copy-start.16 = (s32[128]{0:T(128)}, s32[128]{0:T(128)S(1)}, u32[]{:S(2)}) copy-start(s32[128]{0:T(128)S(1)} %iota_select_fusion) | copy-start | bytes 1540
  2.6 5.3 %slice-start = ((bf16[32,8,128,128]{3,2,1,0:T(8,128)(2,1)}), bf16[32,1,128,128]{3,2,1,0:T(8,128)(2,1)S(1)}, s32[]{:S(2)}) async-start(bf16[32,8,128,128]{3,2,1,0:T(8,128)(2,1)} %param.12), calls=%async_computation | async-start | bytes 2097152 | tf_op jit(solution)/shard_map/slice | solution.py:82
  5.9 7.4 %copy-start = (f32[16,4096]{1,0:T(8,128)S(1)}, f32[16,4096]{1,0:T(8,128)}, u32[]{:S(2)}) copy-start(f32[16,4096]{1,0:T(8,128)} %param.10) | copy-start | bytes 786436
  7.9 58.5 %copy-start.5 = (f32[32,128]{1,0:T(8,128)}, f32[32,128]{1,0:T(8,128)S(1)}, u32[]{:S(2)}) copy-start(f32[32,128]{1,0:T(8,128)S(1)} %copy.176) | copy-start | bytes 49156
  7.9 6.2 %copy-start.17 = (s32[1,256]{1,0:T(1,128)S(1)}, s32[1,256]{1,0:T(1,128)}, u32[]{:S(2)}) copy-start(s32[1,256]{1,0:T(1,128)} %param.14) | copy-start | bytes 3076
  8.0 19.9 %copy-start.18 = (s32[1,256]{1,0:T(1,128)S(1)}, s32[1,256]{1,0:T(1,128)}, u32[]{:S(2)}) copy-start(s32[1,256]{1,0:T(1,128)} %param.15) | copy-start | bytes 3076
  8.0 22.6 %copy-start.15 = (s32[32,8]{0,1:T(8,128)S(1)}, s32[32,8]{0,1:T(8,128)}, u32[]{:S(2)}) copy-start(s32[32,8]{0,1:T(8,128)} %param.13) | copy-start | bytes 3076
  13.3 53.2 %copy-start.8 = (f32[32,128]{1,0:T(8,128)}, f32[32,128]{1,0:T(8,128)S(1)}, u32[]{:S(2)}) copy-start(f32[32,128]{1,0:T(8,128)S(1)} %copy.178) | copy-start | bytes 49156
  14.1 36.8 %copy-start.14 = (s32[256,1]{0,1:T(1,128)}, s32[256,1]{0,1:T(1,128)S(1)}, u32[]{:S(2)}) copy-start(s32[256,1]{0,1:T(1,128)S(1)} %compare_select_fusion.2) | copy-start | bytes 3076
  14.9 16.0 %collective-permute-start.2 = (f32[16,256]{0,1:T(8,128)S(1)}, f32[16,256]{0,1:T(8,128)S(1)}, u32[]{:S(2)}, u32[]{:S(2)}) collective-permute-start(f32[16,256]{0,1:T(8,128)S(1)} %bitcast.190), channel_id=1, source_target_pairs={{0,128},{128,0},{8,136},{136,8},{16,144},{144,16},{24,152},{152,24... | collective-permute-start | bytes 49160 | tf_op jit(solution)/shard_map/ppermute | solution.py:35
  17.6 36.6 %collective-permute-start = (bf16[16,1024]{1,0:T(8,128)(2,1)}, bf16[16,1024]{1,0:T(8,128)(2,1)S(1)}, u32[]{:S(2)}, u32[]{:S(2)}) collective-permute-start(bf16[16,1024]{1,0:T(8,128)(2,1)} %get-tuple-element.24), channel_id=1, source_target_pairs={{0,8},{8,16},{16,24},{24,32},{32,40},{40,48},{48,56},{56,64},{64,7... | collective-permute-start | bytes 98312 | tf_op jit(solution)/shard_map/ppermute | solution.py:22
  21.1 33.0 %collective-permute-start.1 = (bf16[16,1024]{1,0:T(8,128)(2,1)}, bf16[16,1024]{1,0:T(8,128)(2,1)S(1)}, u32[]{:S(2)}, u32[]{:S(2)}) collective-permute-start(bf16[16,1024]{1,0:T(8,128)(2,1)} %get-tuple-element.25), channel_id=1, source_target_pairs={{8,0},{16,8},{24,16},{32,24},{40,32},{48,40},{56,48},{64,56},{72,6... | collective-permute-start | bytes 98312 | tf_op jit(solution)/shard_map/ppermute | solution.py:23
  27.8 21.9 %copy-start.19 = (pred[128]{0:T(512)(128)(4,1)}, pred[128]{0:T(512)(128)(4,1)S(1)}, u32[]{:S(2)}) copy-start(pred[128]{0:T(512)(128)(4,1)S(1)} %iota_compare_fusion.1) | copy-start | bytes 388
  30.8 20.0 %copy-start.20 = (pred[256]{0:T(512)(128)(4,1)}, pred[256]{0:T(512)(128)(4,1)S(1)}, u32[]{:S(2)}) copy-start(pred[256]{0:T(512)(128)(4,1)S(1)} %iota_compare_fusion) | copy-start | bytes 772
  30.9 20.0 %copy-start.11 = (f32[16]{0:T(128)}, f32[16]{0:T(128)S(1)}, u32[]{:S(2)}) copy-start(f32[16]{0:T(128)S(1)} %dynamic_slice.13) | copy-start | bytes 196
  60.7 5.7 %copy-start.4 = (f32[16,4096]{1,0:T(8,128)S(1)}, f32[16,4096]{1,0:T(8,128)}, u32[]{:S(2)}) copy-start(f32[16,4096]{1,0:T(8,128)} %copy.186) | copy-start | bytes 786436
  66.7 32.1 %copy-start.1 = (bf16[16,4096]{1,0:T(8,128)(2,1)}, bf16[16,4096]{1,0:T(8,128)(2,1)S(1)}, u32[]{:S(2)}) copy-start(bf16[16,4096]{1,0:T(8,128)(2,1)S(1)} %get-tuple-element.16) | copy-start | bytes 393220
  68.0 26.1 %copy-start.12 = (f32[16]{0:T(128)S(1)}, f32[16]{0:T(128)}, u32[]{:S(2)}) copy-start(f32[16]{0:T(128)} %copy-done.11) | copy-start | bytes 196
  68.1 8.1 %collective-permute-start.5 = (f32[16,256]{0,1:T(8,128)S(1)}, f32[16,256]{0,1:T(8,128)S(1)}, u32[]{:S(2)}, u32[]{:S(2)}) collective-permute-start(f32[16,256]{0,1:T(8,128)S(1)} %bitcast.192), channel_id=1, source_target_pairs={{0,128},{128,0},{8,136},{136,8},{16,144},{144,16},{24,152},{152,24... | collective-permute-start | bytes 49160 | tf_op jit(solution)/shard_map/ppermute | solution.py:35
  68.8 30.0 %collective-permute-start.3 = (bf16[16,1024]{1,0:T(8,128)(2,1)}, bf16[16,1024]{1,0:T(8,128)(2,1)}, u32[]{:S(2)}, u32[]{:S(2)}) collective-permute-start(bf16[16,1024]{1,0:T(8,128)(2,1)} %get-tuple-element.22), channel_id=1, source_target_pairs={{0,8},{8,16},{16,24},{24,32},{32,40},{40,48},{48,56},{56,64},{64,7... | collective-permute-start | bytes 98312 | tf_op jit(solution)/shard_map/ppermute | solution.py:22
  70.7 28.1 %collective-permute-start.4 = (bf16[16,1024]{1,0:T(8,128)(2,1)}, bf16[16,1024]{1,0:T(8,128)(2,1)}, u32[]{:S(2)}, u32[]{:S(2)}) collective-permute-start(bf16[16,1024]{1,0:T(8,128)(2,1)} %get-tuple-element.23), channel_id=1, source_target_pairs={{8,0},{16,8},{24,16},{32,24},{40,32},{48,40},{56,48},{64,56},{72,6... | collective-permute-start | bytes 98312 | tf_op jit(solution)/shard_map/ppermute | solution.py:23
  106.1 5.7 %copy-start.2 = (bf16[16,4096]{1,0:T(8,128)(2,1)S(1)}, bf16[16,4096]{1,0:T(8,128)(2,1)}, u32[]{:S(2)}) copy-start(bf16[16,4096]{1,0:T(8,128)(2,1)} %copy-done.1) | copy-start | bytes 393220
  106.1 5.7 %copy-start.3 = (f32[16,4096]{1,0:T(8,128)S(1)}, f32[16,4096]{1,0:T(8,128)}, u32[]{:S(2)}) copy-start(f32[16,4096]{1,0:T(8,128)} %copy.193) | copy-start | bytes 786436
  106.1 5.8 %copy-start.6 = (f32[32,128]{1,0:T(8,128)S(1)}, f32[32,128]{1,0:T(8,128)}, u32[]{:S(2)}) copy-start(f32[32,128]{1,0:T(8,128)} %copy-done.5) | copy-start | bytes 49156
  106.1 5.8 %copy-start.9 = (f32[32,128]{1,0:T(8,128)S(1)}, f32[32,128]{1,0:T(8,128)}, u32[]{:S(2)}) copy-start(f32[32,128]{1,0:T(8,128)} %copy-done.8) | copy-start | bytes 49156
  113.4 29.7 %copy-start.13 = (f32[16]{0:T(128)S(1)}, f32[16]{0:T(128)}, u32[]{:S(2)}) copy-start(f32[16]{0:T(128)} %copy-done.11) | copy-start | bytes 196
  113.4 11.4 %collective-permute-start.8 = (f32[16,256]{0,1:T(8,128)S(1)}, f32[16,256]{0,1:T(8,128)S(1)}, u32[]{:S(2)}, u32[]{:S(2)}) collective-permute-start(f32[16,256]{0,1:T(8,128)S(1)} %bitcast.191), channel_id=1, source_target_pairs={{0,128},{128,0},{8,136},{136,8},{16,144},{144,16},{24,152},{152,24... | collective-permute-start | bytes 49160 | tf_op jit(solution)/shard_map/ppermute | solution.py:35
  117.4 29.6 %collective-permute-start.6 = (bf16[16,1024]{1,0:T(8,128)(2,1)}, bf16[16,1024]{1,0:T(8,128)(2,1)}, u32[]{:S(2)}, u32[]{:S(2)}) collective-permute-start(bf16[16,1024]{1,0:T(8,128)(2,1)} %get-tuple-element.20), channel_id=1, source_target_pairs={{0,8},{8,16},{16,24},{24,32},{32,40},{40,48},{48,56},{56,64},{64,7... | collective-permute-start | bytes 98312 | tf_op jit(solution)/shard_map/ppermute | solution.py:22
  119.3 27.7 %collective-permute-start.7 = (bf16[16,1024]{1,0:T(8,128)(2,1)}, bf16[16,1024]{1,0:T(8,128)(2,1)}, u32[]{:S(2)}, u32[]{:S(2)}) collective-permute-start(bf16[16,1024]{1,0:T(8,128)(2,1)} %get-tuple-element.21), channel_id=1, source_target_pairs={{8,0},{16,8},{24,16},{32,24},{40,32},{48,40},{56,48},{64,56},{72,6... | collective-permute-start | bytes 98312 | tf_op jit(solution)/shard_map/ppermute | solution.py:23
  154.3 5.7 %copy-start.7 = (f32[32,128]{1,0:T(8,128)S(1)}, f32[32,128]{1,0:T(8,128)}, u32[]{:S(2)}) copy-start(f32[32,128]{1,0:T(8,128)} %copy-done.5) | copy-start | bytes 49156
  154.3 5.7 %copy-start.10 = (f32[32,128]{1,0:T(8,128)S(1)}, f32[32,128]{1,0:T(8,128)}, u32[]{:S(2)}) copy-start(f32[32,128]{1,0:T(8,128)} %copy-done.8) | copy-start | bytes 49156
where the time goes:
time: 162 us; the launch traced here: 161 us
  matrix products  48.3 us (30%)
  blocking collectives  41.7 us (26%)
  starting transfers between devices  30.5 us (19%)
  local copies, waits for them, and re-layouts  26.5 us (16%)
  other arithmetic  11.5 us (7%)
  between operations  2.49 us (2%)
    all_gather x3, blocking collectives, local(): gathered = lax.all_gather(relative, 'harm', axis=0, tiled=True)  41.7 us
    ppermute x3, starting transfers between devices, with_halo(): after = lax.ppermute(leading, axis, down)  17.6 us
    dot_general x3, matrix products, local(): jnp.einsum('rsij,hrsj->hri', stiff_blocks, picked, preferred_element_type...  17.1 us
    dot_general x3, matrix products, local(): jnp.einsum('rsij,hrsj->hri', mass_blocks, picked, preferred_element_type=...  17 us
    dot_general x3, matrix products, local(): jnp.dot(instant_table, gathered, precision=lax.Precision.HIGHEST)  10.9 us
    ppermute x3, starting transfers between devices, with_halo(): before = lax.ppermute(last, axis, up)  7.35 us
    unnamed x44, local copies, waits for them, and re-layouts  6.69 us
    scatter-add x3, other arithmetic, local(): jnp.zeros_like(displacement).at[:, slot_rows].add(own_force)  6.07 us
  transfers between devices with their start and end apart: 9, of which 0 were waited for; matrix products, arithmetic and copies ran while one was open for 19% of the time, Pallas kernels for 0%

commit v1 on v0

v1 whole, which is shorter than its diff:
```python
import functools
import math

import jax
import jax.numpy as jnp
import ml_dtypes
import numpy as np
from jax import lax
from jax.experimental import pallas as pl
from jax.experimental.pallas import tpu as pltpu
from jax.sharding import PartitionSpec as P

H = 128
TIME_POINTS = 1024
BLK = 128
SLOTS = 8
BAND = 8
ITERS = 3
OWN = 16
ROWS = 32
CMAX = 256
DOFS = ROWS * BLK
F32 = jnp.float32
BF16 = jnp.bfloat16
LAST_LAST = (((1,), (1,)), ((), ()))

VM = pl.BlockSpec(memory_space=pltpu.VMEM)
SM = pl.BlockSpec(memory_space=pltpu.SMEM)
ANY = pl.BlockSpec(memory_space=pl.ANY)


def tables():
    j = np.arange(H)
    waves = np.where(j <= H // 2, j, j - H // 2)
    phase = (np.arange(TIME_POINTS)[:, None] * waves[None, :]) % TIME_POINTS
    angle = phase.astype(np.float64) * (2.0 * math.pi / TIME_POINTS)
    table = np.where(j[None, :] <= H // 2, np.cos(angle), np.sin(angle)).astype(np.float32)
    high = table.astype(ml_dtypes.bfloat16)
    low = (table - high.astype(np.float32)).astype(ml_dtypes.bfloat16)
    forward = np.concatenate([high, high, low], axis=1)
    weights = (np.where(j == 0, 1.0, 2.0) / TIME_POINTS).astype(np.float32)
    back = (table * weights[None, :]).T
    back_high = back.astype(ml_dtypes.bfloat16)
    back_low = (back - back_high.astype(np.float32)).astype(ml_dtypes.bfloat16)
    backward = np.concatenate(
        [
            back_high.reshape(H // OWN, OWN, TIME_POINTS),
            back_low.reshape(H // OWN, OWN, TIME_POINTS),
        ],
        axis=1,
    )
    return forward, backward


def dot(a, b):
    return jnp.dot(a, b, preferred_element_type=F32)


def dot_nt(a, b):
    return lax.dot_general(a, b, LAST_LAST, preferred_element_type=F32)


def split3(x):
    high = x.astype(BF16)
    rest = x - high.astype(F32)
    mid = rest.astype(BF16)
    low = (rest - mid.astype(F32)).astype(BF16)
    return jnp.concatenate([high, mid, low], axis=0)


def sum3(y):
    n = y.shape[0] // 3
    return y[:n] + y[n : 2 * n] + y[2 * n :]


def own_factor(freq, place):
    j = place[0] * OWN + lax.broadcasted_iota(jnp.int32, (OWN, BLK), 0)
    waves = jnp.where(j <= H // 2, j, j - H // 2)
    factor = freq[0] * waves.astype(F32) * (2.0 / H)
    return factor * factor


def cols_of(r):
    return pl.ds(pl.multiple_of(r * BLK, BLK), BLK)


def init_kernel(
    freq, place, load, stiff, mass, rows, pslot, normal, tangent, count,
    disp_o, inner_o, first_o, last_o, dyn_o, inv_o, hot_o, swap_o, listed_o, inv_rows_o, ratio_o, limit_o,
    s_buf, m_buf, sems,
):
    copy_s = pltpu.make_async_copy(stiff.at[:, 0], s_buf, sems.at[0])
    copy_m = pltpu.make_async_copy(mass.at[:, 0], m_buf, sems.at[1])
    copy_s.start()
    copy_m.start()
    factor = own_factor(freq, place)
    in_block = lax.broadcasted_iota(jnp.int32, (BLK, CMAX), 0)
    wanted = rows[...]
    for r in range(ROWS):
        hot_o[r] = jnp.where(in_block + r * BLK == wanted, 1.0, 0.0).astype(BF16)
    swap_o[...] = jnp.where(
        lax.broadcasted_iota(jnp.int32, (CMAX, CMAX), 0) == pslot[...], 1.0, 0.0
    ).astype(BF16)
    ratio_o[...] = tangent[...] / normal[...]
    live = lax.broadcasted_iota(jnp.int32, (1, CMAX), 1) < count[0]
    limit_o[...] = jnp.where(live, normal[...], 0.0)
    eye = lax.broadcasted_iota(jnp.int32, (BLK, BLK), 0) == lax.broadcasted_iota(
        jnp.int32, (BLK, BLK), 1
    )
    ones = jnp.ones((OWN, BLK), BF16)
    zero = jnp.zeros((BLK, BLK), BF16)
    copy_s.wait()
    copy_m.wait()
    listed = jnp.zeros((3 * OWN, CMAX), F32)
    dyn_rows = jnp.zeros((3 * OWN, CMAX), F32)
    for r in range(ROWS):
        s_diag = dot(ones, jnp.where(eye, s_buf[r], zero))
        m_diag = dot(ones, jnp.where(eye, m_buf[r], zero))
        dynamic = s_diag - factor * m_diag
        at = slice(r * BLK, (r + 1) * BLK)
        disp = load[:, at] / dynamic
        rounded = disp.astype(BF16)
        dyn_o[:, at] = dynamic
        inv_o[:, at] = 1.0 / dynamic
        disp_o[:, at] = disp
        inner_o[r] = rounded
        if r < BAND:
            first_o[r] = rounded
        if r >= ROWS - BAND:
            last_o[r - (ROWS - BAND)] = rounded
        listed = listed + dot(split3(disp), hot_o[r])
        dyn_rows = dyn_rows + dot(split3(dynamic), hot_o[r])
    listed_o[...] = sum3(listed)
    inv_rows_o[...] = 1.0 / sum3(dyn_rows)


def relative_kernel(place, own, core, own_far, core_far, swap, ratio, out):
    far = jnp.concatenate([split3(own_far[...]), split3(core_far[...])], axis=0)
    facing = dot(far, swap[...])
    scale = ratio[...]
    side = lax.rem(place[0], 2)
    out[pl.ds(pl.multiple_of(side * OWN, OWN), OWN), :] = (own[...] - sum3(facing[: 3 * OWN])) * scale
    out[pl.ds(pl.multiple_of((1 - side) * OWN, OWN), OWN), :] = (
        core[...] - sum3(facing[3 * OWN :])
    ) * scale


def product_kernel(
    cols, freq, place, inner, before, after, stiff, mass, load, disp, dyn, inv, hot, lin_o, listed_o, field, *, final
):
    field[:BAND] = before[...]
    field[BAND : BAND + ROWS] = inner[...]
    field[BAND + ROWS :] = after[...]
    factor = own_factor(freq, place)

    def row(r, listed):
        picked = jnp.concatenate([field[cols[r, s]] for s in range(SLOTS)], axis=1)
        both = jnp.concatenate(
            [jnp.concatenate([stiff[r, s], mass[r, s]], axis=0) for s in range(SLOTS)], axis=1
        )
        made = dot_nt(picked, both)
        applied = made[:, :BLK] - factor * made[:, BLK:]
        at = cols_of(r)
        rounded = inner[r].astype(F32)
        if final:
            lin_o[:, at] = load[:, at] - (applied + dyn[:, at] * (disp[:, at] - rounded))
            return listed
        lin = rounded + (load[:, at] - applied) * inv[:, at]
        lin_o[:, at] = lin
        return listed + dot(split3(lin), hot[r])

    listed = lax.fori_loop(0, ROWS, row, jnp.zeros((3 * OWN, CMAX), F32), unroll=8)
    listed_o[...] = sum3(listed)


def time_kernel(place, own, one, two, three, forward, backward, limit, lin_rows, inv_rows, force_o, listed_o, rel):
    chunk = place[0] // 2
    for piece, away in ((own, 0), (one, 3), (two, 2), (three, 1)):
        at = lax.rem(chunk + away, 4) * 32
        rel[pl.ds(pl.multiple_of(at, 32), 32), :] = piece[...]
    whole = rel[...]
    high = whole.astype(BF16)
    low = (whole - high.astype(F32)).astype(BF16)
    stacked = jnp.concatenate([high, low, high], axis=0)
    step = 256
    total = jnp.zeros((2 * OWN, CMAX), F32)
    for n in range(0, TIME_POINTS, step):
        values = jnp.tanh(dot(forward[n : n + step, :], stacked)).astype(BF16)
        total = total + dot(backward[:, n : n + step], values)
    force = (total[:OWN] + total[OWN:]) * limit[...]
    force_o[...] = force
    listed_o[...] = lin_rows[...] - force * inv_rows[...]


def spread(force, hot_block):
    high = force.astype(BF16)
    low = (force - high.astype(F32)).astype(BF16)
    both = dot_nt(jnp.concatenate([high, low], axis=0), hot_block)
    return both[:OWN] + both[OWN:]


def update_kernel(force, hot, lin, inv, disp_o, inner_o, first_o, last_o):
    add = force[...]
    for r in range(ROWS):
        at = slice(r * BLK, (r + 1) * BLK)
        disp = lin[:, at] - spread(add, hot[r]) * inv[:, at]
        rounded = disp.astype(BF16)
        disp_o[:, at] = disp
        inner_o[r] = rounded
        if r < BAND:
            first_o[r] = rounded
        if r >= ROWS - BAND:
            last_o[r - (ROWS - BAND)] = rounded


def finish_kernel(force, hot, lin, inv, disp, disp_o, residual_o):
    add = force[...]
    for r in range(ROWS):
        at = slice(r * BLK, (r + 1) * BLK)
        residual = lin[:, at] - spread(add, hot[r])
        residual_o[:, at] = residual
        disp_o[:, at] = disp[:, at] + residual * inv[:, at]


def shape(dims, dtype=F32):
    return jax.ShapeDtypeStruct(dims, dtype)


def params():
    return pltpu.CompilerParams(vmem_limit_bytes=48 << 20)


FULL = (OWN, DOFS)
LIST = (OWN, CMAX)
EDGE = (BAND, OWN, BLK)


def local(
    load,
    stiff_blocks,
    mass_blocks,
    block_cols,
    contact_rows,
    partner_slot,
    contact_count,
    normal_load,
    contact_stiffness,
    frequency,
):
    harm = lax.axis_index("harm").astype(jnp.int32)
    place = harm.reshape(1)
    groups = lax.axis_size("comp")
    devices = lax.axis_size("harm")
    local_cols = block_cols - lax.axis_index("comp") * ROWS + BAND
    forward, backward = tables()
    forward = jnp.asarray(forward)
    backward = lax.dynamic_index_in_dim(jnp.asarray(backward), harm, 0, keepdims=False)

    (
        disp, inner, first, last, dyn, inv, hot, swap, listed, inv_rows, ratio, limit
    ) = pl.pallas_call(
        init_kernel,
        out_shape=(
            shape(FULL), shape((ROWS, OWN, BLK), BF16), shape(EDGE, BF16), shape(EDGE, BF16),
            shape(FULL), shape(FULL), shape((ROWS, BLK, CMAX), BF16), shape((CMAX, CMAX), BF16),
            shape(LIST), shape(LIST), shape((1, CMAX)), shape((1, CMAX)),
        ),
        in_specs=[SM, SM, VM, ANY, ANY, VM, VM, VM, VM, SM],
        out_specs=(VM,) * 12,
        scratch_shapes=[
            pltpu.VMEM((ROWS, BLK, BLK), BF16),
            pltpu.VMEM((ROWS, BLK, BLK), BF16),
            pltpu.SemaphoreType.DMA((2,)),
        ],
        compiler_params=params(),
        name="init",
    )(frequency, place, load, stiff_blocks, mass_blocks, contact_rows, partner_slot, normal_load, contact_stiffness, contact_count)

    across = groups // 2
    far = [(i, i ^ across) for i in range(groups)]
    far_core = [
        (g * devices + d, (g ^ across) * devices + (d ^ 1))
        for g in range(groups)
        for d in range(devices)
    ]
    core = [(i, i ^ 1) for i in range(devices)]
    up = [(i, i + 1) for i in range(groups - 1)]
    down = [(i + 1, i) for i in range(groups - 1)]

    def around(x, steps):
        return lax.ppermute(x, "harm", [(i, (i + steps) % devices) for i in range(devices)])

    for sweep in range(ITERS):
        final = sweep == ITERS - 1
        own_far = lax.ppermute(listed, "comp", far)
        core_far = lax.ppermute(listed, ("comp", "harm"), far_core)
        core_own = lax.ppermute(listed, "harm", core)
        before = lax.ppermute(last, "comp", up)
        after = lax.ppermute(first, "comp", down)
        relative = pl.pallas_call(
            relative_kernel,
            out_shape=shape((2 * OWN, CMAX)),
            in_specs=[SM] + [VM] * 6,
            out_specs=VM,
            compiler_params=params(),
            name="relative",
        )(place, listed, core_own, own_far, core_far, swap, ratio)
        one = around(relative, 2)
        two = around(relative, 4)
        three = around(relative, 6)
        lin, lin_rows = pl.pallas_call(
            functools.partial(product_kernel, final=final),
            out_shape=(shape(FULL), shape(LIST)),
            in_specs=[SM, SM, SM] + [VM] * 10,
            out_specs=(VM, VM),
            scratch_shapes=[pltpu.VMEM((ROWS + 2 * BAND, OWN, BLK), BF16)],
            compiler_params=params(),
            cost_estimate=pl.CostEstimate(flops=270_000_000, bytes_accessed=17_000_000, transcendentals=0),
            name="product",
        )(local_cols, frequency, place, inner, before, after, stiff_blocks, mass_blocks, load, disp, dyn, inv, hot)
        force, listed = pl.pallas_call(
            time_kernel,
            out_shape=(shape(LIST), shape(LIST)),
            in_specs=[SM] + [VM] * 9,
            out_specs=(VM, VM),
            scratch_shapes=[pltpu.VMEM((H, CMAX), F32)],
            compiler_params=params(),
            name="time",
        )(place, relative, one, two, three, forward, backward, limit, lin_rows, inv_rows)
        if final:
            return pl.pallas_call(
                finish_kernel,
                out_shape=(shape(FULL), shape(FULL)),
                in_specs=[VM] * 5,
                out_specs=(VM, VM),
                compiler_params=params(),
                name="finish",
            )(force, hot, lin, inv, disp)
        disp, inner, first, last = pl.pallas_call(
            update_kernel,
            out_shape=(shape(FULL), shape((ROWS, OWN, BLK), BF16), shape(EDGE, BF16), shape(EDGE, BF16)),
            in_specs=[VM] * 4,
            out_specs=(VM,) * 4,
            compiler_params=params(),
            name="update",
        )(force, hot, lin, inv)


def solution(mesh):
    placed = (
        P("harm", "comp"),
        P("comp", None, None, None),
        P("comp", None, None, None),
        P("comp", None),
        P("comp", None),
        P("comp", None),
        P("comp"),
        P("comp", None),
        P("comp", None),
        P(),
    )
    return jax.shard_map(
        local,
        mesh=mesh,
        in_specs=placed,
        out_specs=(P("harm", "comp"), P("harm", "comp")),
        check_vma=False,
    )
```

time: 162 us -> 121 us (0.75)
  the two profiles are of different devices: /device:TPU:9 before, /device:TPU:1 now
where the time goes in v1:
time: 121 us; the launch traced here: 120 us
  Pallas kernels  53.4 us (44%)
  starting transfers between devices  48.9 us (40%)
  waiting for transfers between devices  8.53 us (7%)
  local copies, waits for them, and re-layouts  6.55 us (5%)
  between operations  2.2 us (2%)
    pallas_call x3, Pallas kernels, local(): pl.pallas_call(functools.partial(product_kernel, final=final), out_shape=...  38.8 us
    ppermute x3, starting transfers between devices, local(): core_far = lax.ppermute(listed, ('comp', 'harm'), far_core)  13.2 us
    ppermute x9, starting transfers between devices, around(): lax.ppermute(x, 'harm', [(i, (i + steps) % devices) for i in range(device...  12.3 us
    ppermute x3, starting transfers between devices, local(): before = lax.ppermute(last, 'comp', up)  7.29 us
    pallas_call x1, Pallas kernels, local(): pl.pallas_call(init_kernel, out_shape=(shape(FULL), shape((ROWS, OWN, BLK...  6.9 us
    ppermute x3, starting transfers between devices, local(): own_far = lax.ppermute(listed, 'comp', far)  6.63 us
    unnamed x25, local copies, waits for them, and re-layouts  5.71 us
    ppermute x3, starting transfers between devices, local(): core_own = lax.ppermute(listed, 'harm', core)  5.62 us
  transfers between devices with their start and end apart: 24, of which 4 were waited for; matrix products, arithmetic and copies ran while one was open for 2% of the time, Pallas kernels for 33%

profile of v1, /device:TPU:1, one launch (start us, length us, event | category | flops | bytes accessed | tf_op | source)
XLA Modules:
  0.0 120.3 jit_solution(13399237194579817029)
XLA Ops:
  1.9 0.9 copy-done.1
  5.6 6.9 %init.1 = (f32[16,4096]{1,0:T(8,128)S(1)}, bf16[32,16,128]{2,1,0:T(8,128)(2,1)S(1)}, bf16[8,16,128]{2,1,0:T(8,128)(2,1)}, bf16[8,16,128]{2,1,0:T(8,128)(2,1)}, f...) custom-call(f32[1]{0:T(128)S(6)} %copy.16.freq, ...), custom_call_target="tpu_custom_call" | custom-call | tf_op jit(solution)/shard_map/init/pallas_call | solution.py:261
  12.5 3.3 %collective-permute-start = (f32[16,256]{1,0:T(8,128)S(1)}, f32[16,256]{1,0:T(8,128)S(1)}, u32[]{:S(2)}, u32[]{:S(2)}) collective-permute-start(f32[16,256]{1,0:T(8,128)S(1)} %get-tuple-element.33.own), channel_id=1, source_target_pairs={{0,1},{1,0},{2,3},{3,2},{4,5},{5,4},{6,7},{7,6},{8,9},{9,8},{10,11... | collective-permute-start | bytes 49160 | tf_op jit(solution)/shard_map/ppermute | solution.py:297
  15.8 1.2 collective-permute-start.1
  17.0 2.0 %collective-permute-start.2 = (f32[16,256]{1,0:T(8,128)S(1)}, f32[16,256]{1,0:T(8,128)}, u32[]{:S(2)}, u32[]{:S(2)}) collective-permute-start(f32[16,256]{1,0:T(8,128)S(1)} %get-tuple-element.33.own), channel_id=1, source_target_pairs={{0,129},{1,128},{2,131},{3,130},{4,133},{5,132},{6,135},{7,134},{8... | collective-permute-start | bytes 49160 | tf_op jit(solution)/shard_map/ppermute | solution.py:296
  19.1 1.8 %collective-permute-start.6 = (bf16[8,16,128]{2,1,0:T(8,128)(2,1)}, bf16[8,16,128]{2,1,0:T(8,128)(2,1)S(1)}, u32[]{:S(2)}, u32[]{:S(2)}) collective-permute-start(bf16[8,16,128]{2,1,0:T(8,128)(2,1)} %get-tuple-element.38), channel_id=1, source_target_pairs={{0,8},{8,16},{16,24},{24,32},{32,40},{40,48},{48,56},{56,64},{64,7... | collective-permute-start | bytes 98312 | tf_op jit(solution)/shard_map/ppermute | solution.py:298
  20.9 1.3 %collective-permute-start.7 = (bf16[8,16,128]{2,1,0:T(8,128)(2,1)}, bf16[8,16,128]{2,1,0:T(8,128)(2,1)S(1)}, u32[]{:S(2)}, u32[]{:S(2)}) collective-permute-start(bf16[8,16,128]{2,1,0:T(8,128)(2,1)} %get-tuple-element.39), channel_id=1, source_target_pairs={{8,0},{16,8},{24,16},{32,24},{40,32},{48,40},{56,48},{64,56},{72,6... | collective-permute-start | bytes 98312 | tf_op jit(solution)/shard_map/ppermute | solution.py:299
  22.2 1.4 %copy.14 = s32[32,8]{1,0:T(8,128)} copy(s32[32,8]{0,1:T(8,128)} %param.15) | data formatting | bytes 2048 | tf_op args[3]
  25.8 1.2 %collective-permute-start.3 = (f32[32,256]{1,0:T(8,128)S(1)}, f32[32,256]{1,0:T(8,128)S(1)}, u32[]{:S(2)}, u32[]{:S(2)}) collective-permute-start(f32[32,256]{1,0:T(8,128)S(1)} %relative.3.own), channel_id=1, source_target_pairs={{0,2},{1,3},{2,4},{3,5},{4,6},{5,7},{6,0},{7,1},{8,10},{9,11},{10,... | collective-permute-start | bytes 98312 | tf_op jit(solution)/shard_map/ppermute | solution.py:291
  27.1 2.5 %collective-permute-start.4 = (f32[32,256]{1,0:T(8,128)S(1)}, f32[32,256]{1,0:T(8,128)S(1)}, u32[]{:S(2)}, u32[]{:S(2)}) collective-permute-start(f32[32,256]{1,0:T(8,128)S(1)} %relative.3.own), channel_id=1, source_target_pairs={{0,4},{1,5},{2,6},{3,7},{4,0},{5,1},{6,2},{7,3},{8,12},{9,13},{10,... | collective-permute-start | bytes 98312 | tf_op jit(solution)/shard_map/ppermute | solution.py:291
  29.5 1.2 collective-permute-start.5
  31.6 14.2 %product.3 = (f32[16,4096]{1,0:T(8,128)S(1)}, f32[16,256]{1,0:T(8,128)S(1)}) custom-call(s32[32,8]{1,0:T(8,128)S(1)} %subtract_add_fusion.cols, f32[1]{0:T(128)S(6)} %copy.16.freq, s32[1]{0:T(128)} %bitcast.place, bf16[32,16,128]{2,1,0:T(8,128)(2,1)S(1)} %get-tuple-element.37.inner, bf16[8,16,128]{2,1,0:T(8,128)(2,1)S(1)} %collective-permute-done.6.before, ...), custom_call_target="tpu_custom_call" | custom-call | flops 270000000 | bytes 17000000 | tf_op jit(solution)/shard_map/product/pallas_call | solution.py:311
  45.8 0.9 time.3
  47.5 4.2 %collective-permute-start.14 = (bf16[8,16,128]{2,1,0:T(8,128)(2,1)S(1)}, bf16[8,16,128]{2,1,0:T(8,128)(2,1)S(1)}, u32[]{:S(2)}, u32[]{:S(2)}) collective-permute-start(bf16[8,16,128]{2,1,0:T(8,128)(2,1)S(1)} %get-tuple-element.50), channel_id=1, source_target_pairs={{0,8},{8,16},{16,24},{24,32},{32,40},{40,48},{48,56},{56,64},{64,7... | collective-permute-start | bytes 98312 | tf_op jit(solution)/shard_map/ppermute | solution.py:298
  51.7 1.3 %collective-permute-start.15 = (bf16[8,16,128]{2,1,0:T(8,128)(2,1)S(1)}, bf16[8,16,128]{2,1,0:T(8,128)(2,1)S(1)}, u32[]{:S(2)}, u32[]{:S(2)}) collective-permute-start(bf16[8,16,128]{2,1,0:T(8,128)(2,1)S(1)} %get-tuple-element.51), channel_id=1, source_target_pairs={{8,0},{16,8},{24,16},{32,24},{40,32},{48,40},{56,48},{64,56},{72,6... | collective-permute-start | bytes 98312 | tf_op jit(solution)/shard_map/ppermute | solution.py:299
  53.0 11.1 %collective-permute-start.10 = (f32[16,256]{1,0:T(8,128)S(1)}, f32[16,256]{1,0:T(8,128)S(1)}, u32[]{:S(2)}, u32[]{:S(2)}) collective-permute-start(f32[16,256]{1,0:T(8,128)S(1)} %get-tuple-element.46.own), channel_id=1, source_target_pairs={{0,129},{1,128},{2,131},{3,130},{4,133},{5,132},{6,135},{7,134},{8... | collective-permute-start | bytes 49160 | tf_op jit(solution)/shard_map/ppermute | solution.py:296
  64.3 1.2 collective-permute-done.10.core_far
  65.5 2.7 %collective-permute-done.9.own_far = f32[16,256]{1,0:T(8,128)S(1)} collective-permute-done((f32[16,256]{1,0:T(8,128)S(1)}, f32[16,256]{1,0:T(8,128)S(1)}, u32[]{:S(2)}, u32[]{:S(2)}) %collective-permute-start.9) | collective-permute-done | bytes 16416 | tf_op jit(solution)/shard_map/ppermute | solution.py:295
  69.3 1.9 %collective-permute-start.13 = (f32[32,256]{1,0:T(8,128)S(1)}, f32[32,256]{1,0:T(8,128)S(1)}, u32[]{:S(2)}, u32[]{:S(2)}) collective-permute-start(f32[32,256]{1,0:T(8,128)S(1)} %relative.4.own), channel_id=1, source_target_pairs={{0,6},{1,7},{2,0},{3,1},{4,2},{5,3},{6,4},{7,5},{8,14},{9,15},{10,... | collective-permute-start | bytes 98312 | tf_op jit(solution)/shard_map/ppermute | solution.py:291
  71.2 14.1 %product.4 = (f32[16,4096]{1,0:T(8,128)S(1)}, f32[16,256]{1,0:T(8,128)S(1)}) custom-call(s32[32,8]{1,0:T(8,128)S(1)} %subtract_add_fusion.cols, f32[1]{0:T(128)S(6)} %copy.16.freq, s32[1]{0:T(128)} %bitcast.place, bf16[32,16,128]{2,1,0:T(8,128)(2,1)S(1)} %get-tuple-element.49.inner, bf16[8,16,128]{2,1,0:T(8,128)(2,1)S(1)} %collective-permute-done.14.before, ...), custom_call_target="tpu_custom_call" | custom-call | flops 270000000 | bytes 17000000 | tf_op jit(solution)/shard_map/product/pallas_call | solution.py:311
  85.3 0.9 time.4
  87.0 1.3 %collective-permute-start.22 = (bf16[8,16,128]{2,1,0:T(8,128)(2,1)S(1)}, bf16[8,16,128]{2,1,0:T(8,128)(2,1)S(1)}, u32[]{:S(2)}, u32[]{:S(2)}) collective-permute-start(bf16[8,16,128]{2,1,0:T(8,128)(2,1)S(1)} %get-tuple-element.58), channel_id=1, source_target_pairs={{0,8},{8,16},{16,24},{24,32},{32,40},{40,48},{48,56},{56,64},{64,7... | collective-permute-start | bytes 98312 | tf_op jit(solution)/shard_map/ppermute | solution.py:298
  88.3 1.3 %collective-permute-start.23 = (bf16[8,16,128]{2,1,0:T(8,128)(2,1)S(1)}, bf16[8,16,128]{2,1,0:T(8,128)(2,1)S(1)}, u32[]{:S(2)}, u32[]{:S(2)}) collective-permute-start(bf16[8,16,128]{2,1,0:T(8,128)(2,1)S(1)} %get-tuple-element.59), channel_id=1, source_target_pairs={{8,0},{16,8},{24,16},{32,24},{40,32},{48,40},{56,48},{64,56},{72,6... | collective-permute-start | bytes 98312 | tf_op jit(solution)/shard_map/ppermute | solution.py:299
  89.6 2.3 %collective-permute-start.16 = (f32[16,256]{1,0:T(8,128)S(1)}, f32[16,256]{1,0:T(8,128)S(1)}, u32[]{:S(2)}, u32[]{:S(2)}) collective-permute-start(f32[16,256]{1,0:T(8,128)S(1)} %get-tuple-element.54.own), channel_id=1, source_target_pairs={{0,1},{1,0},{2,3},{3,2},{4,5},{5,4},{6,7},{7,6},{8,9},{9,8},{10,11... | collective-permute-start | bytes 49160 | tf_op jit(solution)/shard_map/ppermute | solution.py:297
  91.9 5.2 %collective-permute-start.17 = (f32[16,256]{1,0:T(8,128)S(1)}, f32[16,256]{1,0:T(8,128)S(1)}, u32[]{:S(2)}, u32[]{:S(2)}) collective-permute-start(f32[16,256]{1,0:T(8,128)S(1)} %get-tuple-element.54.own), channel_id=1, source_target_pairs={{0,128},{8,136},{16,144},{24,152},{32,160},{40,168},{48,176},{56,1... | collective-permute-start | bytes 49160 | tf_op jit(solution)/shard_map/ppermute | solution.py:295
  97.2 1.0 collective-permute-done.17.own_far
  98.2 3.6 %collective-permute-done.18.core_far = f32[16,256]{1,0:T(8,128)S(1)} collective-permute-done((f32[16,256]{1,0:T(8,128)S(1)}, f32[16,256]{1,0:T(8,128)S(1)}, u32[]{:S(2)}, u32[]{:S(2)}) %collective-permute-start.18) | collective-permute-done | bytes 16416 | tf_op jit(solution)/shard_map/ppermute | solution.py:296
  102.4 2.1 %collective-permute-start.20 = (f32[32,256]{1,0:T(8,128)S(1)}, f32[32,256]{1,0:T(8,128)S(1)}, u32[]{:S(2)}, u32[]{:S(2)}) collective-permute-start(f32[32,256]{1,0:T(8,128)S(1)} %relative.5.own), channel_id=1, source_target_pairs={{0,4},{1,5},{2,6},{3,7},{4,0},{5,1},{6,2},{7,3},{8,12},{9,13},{10,... | collective-permute-start | bytes 98312 | tf_op jit(solution)/shard_map/ppermute | solution.py:291
  104.6 2.0 %collective-permute-start.21 = (f32[32,256]{1,0:T(8,128)S(1)}, f32[32,256]{1,0:T(8,128)S(1)}, u32[]{:S(2)}, u32[]{:S(2)}) collective-permute-start(f32[32,256]{1,0:T(8,128)S(1)} %relative.5.own), channel_id=1, source_target_pairs={{0,6},{1,7},{2,0},{3,1},{4,2},{5,3},{6,4},{7,5},{8,14},{9,15},{10,... | collective-permute-start | bytes 98312 | tf_op jit(solution)/shard_map/ppermute | solution.py:291
  106.5 10.6 %product.5 = (f32[16,4096]{1,0:T(8,128)S(1)}, f32[16,256]{1,0:T(8,128)S(1)}) custom-call(s32[32,8]{1,0:T(8,128)S(1)} %subtract_add_fusion.cols, f32[1]{0:T(128)S(6)} %copy.16.freq, s32[1]{0:T(128)} %bitcast.place, bf16[32,16,128]{2,1,0:T(8,128)(2,1)S(1)} %get-tuple-element.57.inner, bf16[8,16,128]{2,1,0:T(8,128)(2,1)S(1)} %collective-permute-done.22.before, ...), custom_call_target="tpu_custom_call" | custom-call | flops 270000000 | bytes 17000000 | tf_op jit(solution)/shard_map/product/pallas_call | solution.py:311
  117.2 1.5 %time.5 = (f32[16,256]{1,0:T(8,128)S(1)}, f32[16,256]{1,0:T(8,128)}) custom-call(s32[1]{0:T(128)} %bitcast.place, f32[32,256]{1,0:T(8,128)S(1)} %relative.5.own, f32[32,256]{1,0:T(8,128)S(1)} %collective-permute-done.19.one, f32[32,256]{1,0:T(8,128)S(1)} %collective-permute-done.20.two, f32[32,256]{1,0:T(8,128)S(1)} %collective-permute-done.21.three, ...), custom_call_target="tpu_custom_call" | custom-call | tf_op jit(solution)/shard_map/time/pallas_call | solution.py:321
  118.7 1.6 %finish.1 = (f32[16,4096]{1,0:T(8,128)}, f32[16,4096]{1,0:T(8,128)}) custom-call(f32[16,256]{1,0:T(8,128)S(1)} %get-tuple-element.62.force, bf16[32,128,256]{2,1,0:T(8,128)(2,1)S(1)} %get-tuple-element.43.hot, f32[16,4096]{1,0:T(8,128)S(1)} %get-tuple-element.63.lin, f32[16,4096]{1,0:T(8,128)S(1)} %get-tuple-element.42.inv, ...), custom_call_target="tpu_custom_call" | custom-call | tf_op jit(solution)/shard_map/finish/pallas_call | solution.py:331
  (56 shorter events, 9.4 us)
Async XLA Ops:
  1.9 1.0 copy-start.1
  2.9 0.7 copy-start.8
  5.6 25.9 %copy-start.2 = (f32[16,4096]{1,0:T(8,128)S(1)}, f32[16,4096]{1,0:T(8,128)}, u32[]{:S(2)}) copy-start(f32[16,4096]{1,0:T(8,128)} %load.7) | copy-start | bytes 786436
  12.5 11.0 %copy-start.3 = (f32[1,256]{1,0:T(1,128)}, f32[1,256]{1,0:T(1,128)S(1)}, u32[]{:S(2)}) copy-start(f32[1,256]{1,0:T(1,128)S(1)} %get-tuple-element.35.ratio) | copy-start | bytes 3076
  12.5 11.0 %copy-start.6 = (f32[1,256]{1,0:T(1,128)}, f32[1,256]{1,0:T(1,128)S(1)}, u32[]{:S(2)}) copy-start(f32[1,256]{1,0:T(1,128)S(1)} %get-tuple-element.36.limit) | copy-start | bytes 3076
  12.5 11.8 %collective-permute-start = (f32[16,256]{1,0:T(8,128)S(1)}, f32[16,256]{1,0:T(8,128)S(1)}, u32[]{:S(2)}, u32[]{:S(2)}) collective-permute-start(f32[16,256]{1,0:T(8,128)S(1)} %get-tuple-element.33.own), channel_id=1, source_target_pairs={{0,1},{1,0},{2,3},{3,2},{4,5},{5,4},{6,7},{7,6},{8,9},{9,8},{10,11... | collective-permute-start | bytes 49160 | tf_op jit(solution)/shard_map/ppermute | solution.py:297
  15.8 8.4 %collective-permute-start.1 = (f32[16,256]{1,0:T(8,128)S(1)}, f32[16,256]{1,0:T(8,128)S(1)}, u32[]{:S(2)}, u32[]{:S(2)}) collective-permute-start(f32[16,256]{1,0:T(8,128)S(1)} %get-tuple-element.33.own), channel_id=1, source_target_pairs={{0,128},{8,136},{16,144},{24,152},{32,160},{40,168},{48,176},{56,1... | collective-permute-start | bytes 49160 | tf_op jit(solution)/shard_map/ppermute | solution.py:295
  17.0 7.2 %collective-permute-start.2 = (f32[16,256]{1,0:T(8,128)S(1)}, f32[16,256]{1,0:T(8,128)}, u32[]{:S(2)}, u32[]{:S(2)}) collective-permute-start(f32[16,256]{1,0:T(8,128)S(1)} %get-tuple-element.33.own), channel_id=1, source_target_pairs={{0,129},{1,128},{2,131},{3,130},{4,133},{5,132},{6,135},{7,134},{8... | collective-permute-start | bytes 49160 | tf_op jit(solution)/shard_map/ppermute | solution.py:296
  19.1 12.4 %collective-permute-start.6 = (bf16[8,16,128]{2,1,0:T(8,128)(2,1)}, bf16[8,16,128]{2,1,0:T(8,128)(2,1)S(1)}, u32[]{:S(2)}, u32[]{:S(2)}) collective-permute-start(bf16[8,16,128]{2,1,0:T(8,128)(2,1)} %get-tuple-element.38), channel_id=1, source_target_pairs={{0,8},{8,16},{16,24},{24,32},{32,40},{40,48},{48,56},{56,64},{64,7... | collective-permute-start | bytes 98312 | tf_op jit(solution)/shard_map/ppermute | solution.py:298
  20.9 10.6 %collective-permute-start.7 = (bf16[8,16,128]{2,1,0:T(8,128)(2,1)}, bf16[8,16,128]{2,1,0:T(8,128)(2,1)S(1)}, u32[]{:S(2)}, u32[]{:S(2)}) collective-permute-start(bf16[8,16,128]{2,1,0:T(8,128)(2,1)} %get-tuple-element.39), channel_id=1, source_target_pairs={{8,0},{16,8},{24,16},{32,24},{40,32},{48,40},{56,48},{64,56},{72,6... | collective-permute-start | bytes 98312 | tf_op jit(solution)/shard_map/ppermute | solution.py:299
  25.8 19.9 %collective-permute-start.3 = (f32[32,256]{1,0:T(8,128)S(1)}, f32[32,256]{1,0:T(8,128)S(1)}, u32[]{:S(2)}, u32[]{:S(2)}) collective-permute-start(f32[32,256]{1,0:T(8,128)S(1)} %relative.3.own), channel_id=1, source_target_pairs={{0,2},{1,3},{2,4},{3,5},{4,6},{5,7},{6,0},{7,1},{8,10},{9,11},{10,... | collective-permute-start | bytes 98312 | tf_op jit(solution)/shard_map/ppermute | solution.py:291
  27.1 18.7 %collective-permute-start.4 = (f32[32,256]{1,0:T(8,128)S(1)}, f32[32,256]{1,0:T(8,128)S(1)}, u32[]{:S(2)}, u32[]{:S(2)}) collective-permute-start(f32[32,256]{1,0:T(8,128)S(1)} %relative.3.own), channel_id=1, source_target_pairs={{0,4},{1,5},{2,6},{3,7},{4,0},{5,1},{6,2},{7,3},{8,12},{9,13},{10,... | collective-permute-start | bytes 98312 | tf_op jit(solution)/shard_map/ppermute | solution.py:291
  29.5 16.2 %collective-permute-start.5 = (f32[32,256]{1,0:T(8,128)S(1)}, f32[32,256]{1,0:T(8,128)S(1)}, u32[]{:S(2)}, u32[]{:S(2)}) collective-permute-start(f32[32,256]{1,0:T(8,128)S(1)} %relative.3.own), channel_id=1, source_target_pairs={{0,6},{1,7},{2,0},{3,1},{4,2},{5,3},{6,4},{7,5},{8,14},{9,15},{10,... | collective-permute-start | bytes 98312 | tf_op jit(solution)/shard_map/ppermute | solution.py:291
  31.5 14.2 %copy-start = (bf16[1024,384]{1,0:T(8,128)(2,1)S(1)}, bf16[1024,384]{1,0:T(8,128)(2,1)}, u32[]{:S(2)}) copy-start(bf16[1024,384]{1,0:T(8,128)(2,1)} %constant.22.clone.forward) | copy-start | bytes 2359300
  31.5 14.2 %copy-start.7 = (f32[1,256]{1,0:T(1,128)S(1)}, f32[1,256]{1,0:T(1,128)}, u32[]{:S(2)}) copy-start(f32[1,256]{1,0:T(1,128)} %copy-done.6) | copy-start | bytes 3076
  31.6 36.6 %copy-start.5 = (f32[1,256]{1,0:T(1,128)S(1)}, f32[1,256]{1,0:T(1,128)}, u32[]{:S(2)}) copy-start(f32[1,256]{1,0:T(1,128)} %copy-done.3) | copy-start | bytes 3076
  47.5 23.7 %collective-permute-start.14 = (bf16[8,16,128]{2,1,0:T(8,128)(2,1)S(1)}, bf16[8,16,128]{2,1,0:T(8,128)(2,1)S(1)}, u32[]{:S(2)}, u32[]{:S(2)}) collective-permute-start(bf16[8,16,128]{2,1,0:T(8,128)(2,1)S(1)} %get-tuple-element.50), channel_id=1, source_target_pairs={{0,8},{8,16},{16,24},{24,32},{32,40},{40,48},{48,56},{56,64},{64,7... | collective-permute-start | bytes 98312 | tf_op jit(solution)/shard_map/ppermute | solution.py:298
  51.7 19.5 %collective-permute-start.15 = (bf16[8,16,128]{2,1,0:T(8,128)(2,1)S(1)}, bf16[8,16,128]{2,1,0:T(8,128)(2,1)S(1)}, u32[]{:S(2)}, u32[]{:S(2)}) collective-permute-start(bf16[8,16,128]{2,1,0:T(8,128)(2,1)S(1)} %get-tuple-element.51), channel_id=1, source_target_pairs={{8,0},{16,8},{24,16},{32,24},{40,32},{48,40},{56,48},{64,56},{72,6... | collective-permute-start | bytes 98312 | tf_op jit(solution)/shard_map/ppermute | solution.py:299
  53.0 12.5 %collective-permute-start.10 = (f32[16,256]{1,0:T(8,128)S(1)}, f32[16,256]{1,0:T(8,128)S(1)}, u32[]{:S(2)}, u32[]{:S(2)}) collective-permute-start(f32[16,256]{1,0:T(8,128)S(1)} %get-tuple-element.46.own), channel_id=1, source_target_pairs={{0,129},{1,128},{2,131},{3,130},{4,133},{5,132},{6,135},{7,134},{8... | collective-permute-start | bytes 49160 | tf_op jit(solution)/shard_map/ppermute | solution.py:296
  64.1 1.4 %collective-permute-start.8 = (f32[16,256]{1,0:T(8,128)S(1)}, f32[16,256]{1,0:T(8,128)S(1)}, u32[]{:S(2)}, u32[]{:S(2)}) collective-permute-start(f32[16,256]{1,0:T(8,128)S(1)} %get-tuple-element.46.own), channel_id=1, source_target_pairs={{0,1},{1,0},{2,3},{3,2},{4,5},{5,4},{6,7},{7,6},{8,9},{9,8},{10,11... | collective-permute-start | bytes 49160 | tf_op jit(solution)/shard_map/ppermute | solution.py:297
  64.1 4.1 %collective-permute-start.9 = (f32[16,256]{1,0:T(8,128)S(1)}, f32[16,256]{1,0:T(8,128)S(1)}, u32[]{:S(2)}, u32[]{:S(2)}) collective-permute-start(f32[16,256]{1,0:T(8,128)S(1)} %get-tuple-element.46.own), channel_id=1, source_target_pairs={{0,128},{8,136},{16,144},{24,152},{32,160},{40,168},{48,176},{56,1... | collective-permute-start | bytes 49160 | tf_op jit(solution)/shard_map/ppermute | solution.py:295
  68.3 16.9 %collective-permute-start.11 = (f32[32,256]{1,0:T(8,128)S(1)}, f32[32,256]{1,0:T(8,128)S(1)}, u32[]{:S(2)}, u32[]{:S(2)}) collective-permute-start(f32[32,256]{1,0:T(8,128)S(1)} %relative.4.own), channel_id=1, source_target_pairs={{0,2},{1,3},{2,4},{3,5},{4,6},{5,7},{6,0},{7,1},{8,10},{9,11},{10,... | collective-permute-start | bytes 98312 | tf_op jit(solution)/shard_map/ppermute | solution.py:291
  68.7 16.6 %collective-permute-start.12 = (f32[32,256]{1,0:T(8,128)S(1)}, f32[32,256]{1,0:T(8,128)S(1)}, u32[]{:S(2)}, u32[]{:S(2)}) collective-permute-start(f32[32,256]{1,0:T(8,128)S(1)} %relative.4.own), channel_id=1, source_target_pairs={{0,4},{1,5},{2,6},{3,7},{4,0},{5,1},{6,2},{7,3},{8,12},{9,13},{10,... | collective-permute-start | bytes 98312 | tf_op jit(solution)/shard_map/ppermute | solution.py:291
  69.3 16.0 %collective-permute-start.13 = (f32[32,256]{1,0:T(8,128)S(1)}, f32[32,256]{1,0:T(8,128)S(1)}, u32[]{:S(2)}, u32[]{:S(2)}) collective-permute-start(f32[32,256]{1,0:T(8,128)S(1)} %relative.4.own), channel_id=1, source_target_pairs={{0,6},{1,7},{2,0},{3,1},{4,2},{5,3},{6,4},{7,5},{8,14},{9,15},{10,... | collective-permute-start | bytes 98312 | tf_op jit(solution)/shard_map/ppermute | solution.py:291
  87.0 19.5 %collective-permute-start.22 = (bf16[8,16,128]{2,1,0:T(8,128)(2,1)S(1)}, bf16[8,16,128]{2,1,0:T(8,128)(2,1)S(1)}, u32[]{:S(2)}, u32[]{:S(2)}) collective-permute-start(bf16[8,16,128]{2,1,0:T(8,128)(2,1)S(1)} %get-tuple-element.58), channel_id=1, source_target_pairs={{0,8},{8,16},{16,24},{24,32},{32,40},{40,48},{48,56},{56,64},{64,7... | collective-permute-start | bytes 98312 | tf_op jit(solution)/shard_map/ppermute | solution.py:298
  88.3 18.2 %collective-permute-start.23 = (bf16[8,16,128]{2,1,0:T(8,128)(2,1)S(1)}, bf16[8,16,128]{2,1,0:T(8,128)(2,1)S(1)}, u32[]{:S(2)}, u32[]{:S(2)}) collective-permute-start(bf16[8,16,128]{2,1,0:T(8,128)(2,1)S(1)} %get-tuple-element.59), channel_id=1, source_target_pairs={{8,0},{16,8},{24,16},{32,24},{40,32},{48,40},{56,48},{64,56},{72,6... | collective-permute-start | bytes 98312 | tf_op jit(solution)/shard_map/ppermute | solution.py:299
  89.6 7.6 %collective-permute-start.16 = (f32[16,256]{1,0:T(8,128)S(1)}, f32[16,256]{1,0:T(8,128)S(1)}, u32[]{:S(2)}, u32[]{:S(2)}) collective-permute-start(f32[16,256]{1,0:T(8,128)S(1)} %get-tuple-element.54.own), channel_id=1, source_target_pairs={{0,1},{1,0},{2,3},{3,2},{4,5},{5,4},{6,7},{7,6},{8,9},{9,8},{10,11... | collective-permute-start | bytes 49160 | tf_op jit(solution)/shard_map/ppermute | solution.py:297
  91.9 6.3 %collective-permute-start.17 = (f32[16,256]{1,0:T(8,128)S(1)}, f32[16,256]{1,0:T(8,128)S(1)}, u32[]{:S(2)}, u32[]{:S(2)}) collective-permute-start(f32[16,256]{1,0:T(8,128)S(1)} %get-tuple-element.54.own), channel_id=1, source_target_pairs={{0,128},{8,136},{16,144},{24,152},{32,160},{40,168},{48,176},{56,1... | collective-permute-start | bytes 49160 | tf_op jit(solution)/shard_map/ppermute | solution.py:295
  97.1 4.7 %collective-permute-start.18 = (f32[16,256]{1,0:T(8,128)S(1)}, f32[16,256]{1,0:T(8,128)S(1)}, u32[]{:S(2)}, u32[]{:S(2)}) collective-permute-start(f32[16,256]{1,0:T(8,128)S(1)} %get-tuple-element.54.own), channel_id=1, source_target_pairs={{0,129},{1,128},{2,131},{3,130},{4,133},{5,132},{6,135},{7,134},{8... | collective-permute-start | bytes 49160 | tf_op jit(solution)/shard_map/ppermute | solution.py:296
  101.9 15.2 %collective-permute-start.19 = (f32[32,256]{1,0:T(8,128)S(1)}, f32[32,256]{1,0:T(8,128)S(1)}, u32[]{:S(2)}, u32[]{:S(2)}) collective-permute-start(f32[32,256]{1,0:T(8,128)S(1)} %relative.5.own), channel_id=1, source_target_pairs={{0,2},{1,3},{2,4},{3,5},{4,6},{5,7},{6,0},{7,1},{8,10},{9,11},{10,... | collective-permute-start | bytes 98312 | tf_op jit(solution)/shard_map/ppermute | solution.py:291
  102.4 14.8 %collective-permute-start.20 = (f32[32,256]{1,0:T(8,128)S(1)}, f32[32,256]{1,0:T(8,128)S(1)}, u32[]{:S(2)}, u32[]{:S(2)}) collective-permute-start(f32[32,256]{1,0:T(8,128)S(1)} %relative.5.own), channel_id=1, source_target_pairs={{0,4},{1,5},{2,6},{3,7},{4,0},{5,1},{6,2},{7,3},{8,12},{9,13},{10,... | collective-permute-start | bytes 98312 | tf_op jit(solution)/shard_map/ppermute | solution.py:291
  104.6 12.6 %collective-permute-start.21 = (f32[32,256]{1,0:T(8,128)S(1)}, f32[32,256]{1,0:T(8,128)S(1)}, u32[]{:S(2)}, u32[]{:S(2)}) collective-permute-start(f32[32,256]{1,0:T(8,128)S(1)} %relative.5.own), channel_id=1, source_target_pairs={{0,6},{1,7},{2,0},{3,1},{4,2},{5,3},{6,4},{7,5},{8,14},{9,15},{10,... | collective-permute-start | bytes 98312 | tf_op jit(solution)/shard_map/ppermute | solution.py:291
  (4 other events, 2.7 us)

commit v2 on v1

v2 whole, which is shorter than its diff:
```python
import functools
import math

import jax
import jax.numpy as jnp
import ml_dtypes
import numpy as np
from jax import lax
from jax.experimental import pallas as pl
from jax.experimental.pallas import tpu as pltpu
from jax.sharding import PartitionSpec as P

H = 128
TIME_POINTS = 1024
BLK = 128
SLOTS = 8
BAND = 8
ITERS = 3
OWN = 16
ROWS = 32
HALF = ROWS // 2
RATIO = 16
LIMIT = 24
CMAX = 256
DOFS = ROWS * BLK
F32 = jnp.float32
BF16 = jnp.bfloat16
LAST_LAST = (((1,), (1,)), ((), ()))

VM = pl.BlockSpec(memory_space=pltpu.VMEM)
SM = pl.BlockSpec(memory_space=pltpu.SMEM)
FAR = pl.BlockSpec(memory_space=pltpu.HBM)


def tables():
    j = np.arange(H)
    waves = np.where(j <= H // 2, j, j - H // 2)
    phase = (np.arange(TIME_POINTS)[:, None] * waves[None, :]) % TIME_POINTS
    angle = phase.astype(np.float64) * (2.0 * math.pi / TIME_POINTS)
    table = np.where(j[None, :] <= H // 2, np.cos(angle), np.sin(angle)).astype(np.float32)
    high = table.astype(ml_dtypes.bfloat16)
    low = (table - high.astype(np.float32)).astype(ml_dtypes.bfloat16)
    forward = np.concatenate([high, high, low], axis=1)
    weights = (np.where(j == 0, 1.0, 2.0) / TIME_POINTS).astype(np.float32)
    back = (table * weights[None, :]).T
    back_high = back.astype(ml_dtypes.bfloat16)
    back_low = (back - back_high.astype(np.float32)).astype(ml_dtypes.bfloat16)
    backward = np.concatenate(
        [
            back_high.reshape(H // OWN, OWN, TIME_POINTS),
            back_low.reshape(H // OWN, OWN, TIME_POINTS),
        ],
        axis=1,
    )
    return forward, backward


def dot(a, b):
    return jnp.dot(a, b, preferred_element_type=F32)


def dot_nt(a, b):
    return lax.dot_general(a, b, LAST_LAST, preferred_element_type=F32)


def split3(x):
    high = x.astype(BF16)
    rest = x - high.astype(F32)
    mid = rest.astype(BF16)
    low = (rest - mid.astype(F32)).astype(BF16)
    return jnp.concatenate([high, mid, low], axis=0)


def sum3(y):
    n = y.shape[0] // 3
    return y[:n] + y[n : 2 * n] + y[2 * n :]


def own_factor(freq, place):
    j = place[0] * OWN + lax.broadcasted_iota(jnp.int32, (OWN, BLK), 0)
    waves = jnp.where(j <= H // 2, j, j - H // 2)
    factor = freq[0] * waves.astype(F32) * (2.0 / H)
    return factor * factor


def cols_of(r):
    return pl.ds(pl.multiple_of(r * BLK, BLK), BLK)


def put_edges(place, inner, even_o, odd_o):
    low, high = slice(0, BAND), slice(ROWS - BAND, ROWS)
    side = lax.rem(place[1], 2)

    @pl.when(side == 0)
    def _():
        even_o[...] = inner[high]
        odd_o[...] = inner[low]

    @pl.when(side == 1)
    def _():
        even_o[...] = inner[low]
        odd_o[...] = inner[high]


def init_kernel(
    freq, place, count, load, stiff, mass, rows, pslot, normal, tangent,
    disp_o, inner_o, even_o, odd_o, dyn_o, inv_o, hot_o, swap_o, listed_o, aux_o,
    s_buf, m_buf, l_buf, small_i, small_f, parts, sems,
):
    moves = [
        pltpu.make_async_copy(rows, small_i.at[0], sems.at[0]),
        pltpu.make_async_copy(pslot, small_i.at[1], sems.at[1]),
        pltpu.make_async_copy(normal, small_f.at[0], sems.at[2]),
        pltpu.make_async_copy(tangent, small_f.at[1], sems.at[3]),
        pltpu.make_async_copy(stiff.at[:, 0], s_buf, sems.at[4]),
        pltpu.make_async_copy(mass.at[:, 0], m_buf, sems.at[5]),
        pltpu.make_async_copy(load, l_buf, sems.at[6]),
    ]
    for move in moves:
        move.start()
    factor = own_factor(freq, place)
    for move in moves[:4]:
        move.wait()
    in_block = lax.broadcasted_iota(jnp.int32, (BLK, CMAX), 0)
    wanted = small_i[0]
    for r in range(ROWS):
        hot_o[r * BLK : (r + 1) * BLK, :] = jnp.where(in_block + r * BLK == wanted, 1.0, 0.0).astype(BF16)
    swap_o[...] = jnp.where(
        lax.broadcasted_iota(jnp.int32, (CMAX, CMAX), 0) == small_i[1], 1.0, 0.0
    ).astype(BF16)
    live = lax.broadcasted_iota(jnp.int32, (1, CMAX), 1) < count[0]
    aux_o[RATIO : RATIO + 1, :] = small_f[1] / small_f[0]
    aux_o[LIMIT : LIMIT + 1, :] = jnp.where(live, small_f[0], 0.0)
    eye = lax.broadcasted_iota(jnp.int32, (BLK, BLK), 0) == lax.broadcasted_iota(
        jnp.int32, (BLK, BLK), 1
    )
    ones = jnp.ones((OWN, BLK), BF16)
    zero = jnp.zeros((BLK, BLK), BF16)
    for move in moves[4:]:
        move.wait()
    for r in range(ROWS):
        s_diag = dot(ones, jnp.where(eye, s_buf[r], zero))
        m_diag = dot(ones, jnp.where(eye, m_buf[r], zero))
        dynamic = s_diag - factor * m_diag
        at = slice(r * BLK, (r + 1) * BLK)
        disp = l_buf[:, at] / dynamic
        dyn_o[:, at] = dynamic
        inv_o[:, at] = 1.0 / dynamic
        disp_o[:, at] = disp
        inner_o[r] = disp.astype(BF16)
        parts[: 3 * OWN, at] = split3(disp)
        parts[3 * OWN :, at] = split3(dynamic)
    listed = dot(parts[...], hot_o[...])
    listed_o[...] = sum3(listed[: 3 * OWN])
    aux_o[:OWN, :] = 1.0 / sum3(listed[3 * OWN :])
    put_edges(place, inner_o, even_o, odd_o)


def relative_kernel(own, far, swap, aux, _, out):
    facing = dot(split3(far[...]), swap[...])
    out[...] = (own[...] - sum3(facing)) * aux[RATIO : RATIO + 1, :]


def fill_field(place, inner, even, odd, field):
    side = lax.rem(place[1], 2)
    field[BAND : BAND + ROWS] = inner[...]
    far_end = BAND + ROWS
    field[pl.ds((1 - side) * far_end, BAND)] = even[...]
    field[pl.ds(side * far_end, BAND)] = odd[...]


def product_kernel(*refs, start, first, final, more):
    refs = list(refs)
    cols, freq, place, inner, even, odd = refs[:6]
    del refs[:6]
    if first:
        stiff, mass = refs[:2]
        del refs[:2]
    else:
        wide = refs.pop(0)
    load, hot, scale = refs[:3]
    del refs[:3]
    if final:
        disp = refs.pop(0)
    if more:
        earlier = refs.pop(0)
    lin_o = refs.pop(0)
    if not final:
        listed_o = refs.pop(0)
    if first:
        wide = refs.pop(0)
    field, parts = refs
    fill_field(place, inner, even, odd, field)
    factor = own_factor(freq, place)
    offset = place[1] * ROWS - BAND

    def row(i, carry):
        r = i + start
        at = cols_of(r)
        here = cols_of(i)
        picked = [field[cols[s, r] - offset] for s in range(SLOTS)]
        if first:
            for s in range(SLOTS):
                wide[i, s * BLK : (s + 1) * BLK, :BLK] = stiff[r, s].T
                wide[i, s * BLK : (s + 1) * BLK, BLK:] = mass[r, s].T
        made = dot(jnp.concatenate(picked, axis=1), wide[i])
        applied = made[:, :BLK] - factor * made[:, BLK:]
        rounded = inner[r].astype(F32)
        if final:
            lin_o[:, here] = load[:, at] - (applied + scale[:, at] * (disp[:, at] - rounded))
            return carry
        lin = rounded + (load[:, at] - applied) * scale[:, at]
        lin_o[:, here] = lin
        parts[:, here] = split3(lin)
        return carry

    lax.fori_loop(0, HALF, row, 0, unroll=HALF // 2 if first else HALF)
    if not final:
        made = sum3(dot(parts[...], hot[start * BLK : (start + HALF) * BLK, :]))
        listed_o[...] = made + earlier[...] if more else made


def time_kernel(place, near, side, across, forward, backward, aux, *rest, final):
    rel = rest[-1]
    me = place[0]
    for ref, at, other in (
        (near, 0, 0), (near, 1, 1), (side, 0, 2), (side, 1, 3),
        (across, 0, 6), (across, 1, 7), (across, 2, 4), (across, 3, 5),
    ):
        to = pl.multiple_of(jnp.bitwise_xor(me, other) * OWN, OWN)
        rel[pl.ds(to, OWN), :] = ref[at * OWN : (at + 1) * OWN, :]
    whole = rel[...]
    high = whole.astype(BF16)
    low = (whole - high.astype(F32)).astype(BF16)
    stacked = jnp.concatenate([high, low, high], axis=0)
    step = 256
    total = jnp.zeros((2 * OWN, CMAX), F32)
    for n in range(0, TIME_POINTS, step):
        values = jnp.tanh(dot(forward[n : n + step, :], stacked)).astype(BF16)
        total = total + dot(backward[me, :, n : n + step], values)
    force = (total[:OWN] + total[OWN:]) * aux[LIMIT : LIMIT + 1, :]
    if final:
        rest[0][...] = force
        return
    lin_rows, force_o, listed_o, _ = rest
    force_o[...] = force
    listed_o[...] = lin_rows[...] - force * aux[:OWN, :]


def spread(force, hot_block):
    high = force.astype(BF16)
    low = (force - high.astype(F32)).astype(BF16)
    both = dot_nt(jnp.concatenate([high, low], axis=0), hot_block)
    return both[:OWN] + both[OWN:]


def update_kernel(place, force, hot, lin_a, lin_b, inv, disp_o, inner_o, even_o, odd_o):
    add = force[...]
    for r in range(ROWS):
        at = slice(r * BLK, (r + 1) * BLK)
        here = slice(r % HALF * BLK, (r % HALF + 1) * BLK)
        lin = (lin_a if r < HALF else lin_b)[:, here]
        disp = lin - spread(add, hot[at, :]) * inv[:, at]
        disp_o[:, at] = disp
        inner_o[r] = disp.astype(BF16)
    put_edges(place, inner_o, even_o, odd_o)


def finish_kernel(force, hot, lin_a, lin_b, inv, disp, disp_o, residual_o):
    add = force[...]
    for r in range(ROWS):
        at = slice(r * BLK, (r + 1) * BLK)
        here = slice(r % HALF * BLK, (r % HALF + 1) * BLK)
        lin = (lin_a if r < HALF else lin_b)[:, here]
        residual = lin - spread(add, hot[at, :])
        residual_o[:, at] = residual
        disp_o[:, at] = disp[:, at] + residual * inv[:, at]


def shape(dims, dtype=F32):
    return jax.ShapeDtypeStruct(dims, dtype)


def held(dims, dtype=F32):
    return pltpu.VMEM(dims, dtype)


def params(limit=16):
    return pltpu.CompilerParams(vmem_limit_bytes=limit << 20)


def cost(us):
    return pl.CostEstimate(flops=int(us * 1.0e9), bytes_accessed=int(us * 3.0e6), transcendentals=0)


FULL = (OWN, DOFS)
PART = (OWN, HALF * BLK)
LIST = (OWN, CMAX)
EDGE = (BAND, OWN, BLK)
BLOCKED = (ROWS, OWN, BLK)
WIDE = (HALF, SLOTS * BLK, 2 * BLK)


def local(
    load,
    stiff_blocks,
    mass_blocks,
    block_cols,
    contact_rows,
    partner_slot,
    contact_count,
    normal_load,
    contact_stiffness,
    frequency,
):
    harm = lax.axis_index("harm").astype(jnp.int32)
    comp = lax.axis_index("comp").astype(jnp.int32)
    place = jnp.stack([harm, comp])
    groups = lax.axis_size("comp")
    devices = lax.axis_size("harm")
    cols = block_cols.T
    forward, backward = (jnp.asarray(t) for t in tables())
    stiff_near = pltpu.with_memory_space_constraint(stiff_blocks, pltpu.VMEM)
    mass_near = pltpu.with_memory_space_constraint(mass_blocks, pltpu.VMEM)

    disp, inner, even, odd, dyn, inv, hot, swap, listed, aux = pl.pallas_call(
        init_kernel,
        out_shape=(
            shape(FULL), shape(BLOCKED, BF16), shape(EDGE, BF16), shape(EDGE, BF16),
            shape(FULL), shape(FULL), shape((DOFS, CMAX), BF16), shape((CMAX, CMAX), BF16),
            shape(LIST), shape((32, CMAX)),
        ),
        in_specs=[SM, SM, SM] + [FAR] * 7,
        out_specs=(VM,) * 10,
        scratch_shapes=[
            pltpu.VMEM((ROWS, BLK, BLK), BF16),
            pltpu.VMEM((ROWS, BLK, BLK), BF16),
            pltpu.VMEM(FULL, F32),
            pltpu.VMEM((2, 1, CMAX), jnp.int32),
            pltpu.VMEM((2, 1, CMAX), F32),
            pltpu.VMEM((6 * OWN, DOFS), BF16),
            pltpu.SemaphoreType.DMA((7,)),
        ],
        compiler_params=params(),
        cost_estimate=cost(3.0),
        name="init",
    )(
        frequency, place, contact_count, *(
            pltpu.with_memory_space_constraint(x, pltpu.HBM)
            for x in (load, stiff_blocks, mass_blocks, contact_rows, partner_slot, normal_load, contact_stiffness)
        )
    )

    across = groups // 2
    far = [(i, i ^ across) for i in range(groups)]
    evens = [(i, i ^ 1) for i in range(groups)]
    odds = [(i, j) for i in range(groups) if 0 <= (j := i - 1 + 2 * (i % 2)) < groups]

    def flipped(x, bits):
        return lax.ppermute(x, "harm", [(i, i ^ bits) for i in range(devices)])

    for sweep in range(ITERS):
        first, final = sweep == 0, sweep == ITERS - 1
        own_far = lax.ppermute(listed, "comp", far)
        even_in = lax.ppermute(even, "comp", evens)
        odd_in = lax.ppermute(odd, "comp", odds)
        relative = pl.pallas_call(
            relative_kernel,
            out_shape=shape(LIST),
            in_specs=[VM] * 5,
            out_specs=VM,
            compiler_params=params(),
            cost_estimate=cost(0.2),
            name="relative",
        )(listed, own_far, swap, aux, even)
        near = jnp.concatenate([relative, flipped(relative, 1)], axis=0)
        side = flipped(near, 2)
        opposite = flipped(jnp.concatenate([near, side], axis=0), 6)
        lins, found = [], []
        for half in range(2):
            take = [cols, frequency, place, inner, even_in, odd_in]
            specs = [SM] * 3 + [VM] * 3
            if first:
                take += [stiff_near, mass_near]
                specs += [VM] * 2
            else:
                take += [wides[half]]
                specs += [VM]
            take += [load, hot, dyn if final else inv]
            specs += [VM] * 3
            if final:
                take += [disp]
                specs += [VM]
            elif half:
                take += [found[0]]
                specs += [VM]
            give = [shape(PART)] + ([] if final else [shape(LIST)])
            given = [VM] * len(give)
            if first:
                give += [held(WIDE, BF16)]
                given += [VM]
            outs = pl.pallas_call(
                functools.partial(
                    product_kernel, start=half * HALF, first=first, final=final, more=half == 1 and not final
                ),
                out_shape=tuple(give),
                in_specs=specs,
                out_specs=tuple(given),
                scratch_shapes=[
                    pltpu.VMEM((ROWS + 2 * BAND, OWN, BLK), BF16),
                    pltpu.VMEM((3 * OWN, HALF * BLK), BF16),
                ],
                compiler_params=params(),
                cost_estimate=cost(3.0 if first else 1.4),
                name="product",
            )(*take)
            lins.append(outs[0])
            if not final:
                found.append(outs[1])
            if first:
                wides = [outs[2]] if half == 0 else wides + [outs[2]]
        timed = pl.pallas_call(
            functools.partial(time_kernel, final=final),
            out_shape=(shape(LIST),) * (1 if final else 2),
            in_specs=[SM] + [VM] * (6 if final else 7),
            out_specs=(VM,) * (1 if final else 2),
            scratch_shapes=[pltpu.VMEM((H, CMAX), F32)],
            compiler_params=params(),
            cost_estimate=cost(1.0),
            name="time",
        )(place, near, side, opposite, forward, backward, aux, *([] if final else found[1:]))
        if final:
            return pl.pallas_call(
                finish_kernel,
                out_shape=(shape(FULL), shape(FULL)),
                in_specs=[VM] * 6,
                out_specs=(VM, VM),
                compiler_params=params(),
                name="finish",
            )(timed[0], hot, *lins, inv, disp)
        force, listed = timed
        disp, inner, even, odd = pl.pallas_call(
            update_kernel,
            out_shape=(shape(FULL), shape(BLOCKED, BF16), shape(EDGE, BF16), shape(EDGE, BF16)),
            in_specs=[SM] + [VM] * 5,
            out_specs=(VM,) * 4,
            compiler_params=params(),
            cost_estimate=cost(0.8),
            name="update",
        )(place, force, hot, *lins, inv)


def solution(mesh):
    placed = (
        P("harm", "comp"),
        P("comp", None, None, None),
        P("comp", None, None, None),
        P("comp", None),
        P("comp", None),
        P("comp", None),
        P("comp"),
        P("comp", None),
        P("comp", None),
        P(),
    )
    return jax.shard_map(
        local,
        mesh=mesh,
        in_specs=placed,
        out_specs=(P("harm", "comp"), P("harm", "comp")),
        check_vma=False,
    )
```

time: 121 us -> 92.8 us (0.77)
  the two profiles are of different devices: /device:TPU:1 before, /device:TPU:24 now
where the time goes in v2:
time: 92.8 us; the launch traced here: 92.5 us
  starting transfers between devices  32 us (34%)
  Pallas kernels  30.3 us (33%)
  waiting for transfers between devices  17.7 us (19%)
  local copies, waits for them, and re-layouts  10.1 us (11%)
  between operations  2.15 us (2%)
    ppermute x3, starting transfers between devices, local(): odd_in = lax.ppermute(odd, 'comp', odds)  19.1 us
    pallas_call x6, Pallas kernels, local(): pl.pallas_call(functools.partial(product_kernel, start=half * HALF, first...  16.4 us
    unnamed x24, local copies, waits for them, and re-layouts  10.1 us
    ppermute x3, waiting for transfers between devices, local(): own_far = lax.ppermute(listed, 'comp', far)  9.28 us
    ppermute x9, starting transfers between devices, flipped(): return lax.ppermute(x, 'harm', [(i, i ^ bits) for i in range(devices)])  7.47 us
    ppermute x9, waiting for transfers between devices, flipped(): return lax.ppermute(x, 'harm', [(i, i ^ bits) for i in range(devices)])  4.83 us
    pallas_call x3, Pallas kernels, local(): pl.pallas_call(functools.partial(time_kernel, final=final), out_shape=(sh...  4.35 us
    pallas_call x1, Pallas kernels, local(): pl.pallas_call(init_kernel, out_shape=(shape(FULL), shape(BLOCKED, BF16),...  4.23 us
  transfers between devices with their start and end apart: 18, of which 8 were waited for; matrix products, arithmetic and copies ran while one was open for 0% of the time, Pallas kernels for 21%

profile of v2, /device:TPU:24, one launch (start us, length us, event | category | flops | bytes accessed | tf_op | source)
XLA Modules:
  0.0 92.5 jit_solution(11756856282710929044)
XLA Ops:
  2.0 4.2 %init.1 = (f32[16,4096]{1,0:T(8,128)}, bf16[32,16,128]{2,1,0:T(8,128)(2,1)S(1)}, bf16[8,16,128]{2,1,0:T(8,128)(2,1)S(1)}, bf16[8,16,128]{2,1,0:T(8,128)(2,1)S(1)...) custom-call(f32[1]{0:T(128)S(6)} %copy.15.freq.refs_1_, ...), custom_call_target="tpu_custom_call" | custom-call | flops 3000000000 | bytes 9000000 | tf_op jit(solution)/shard_map/init/pallas_call | solution.py:326
  6.3 1.3 %collective-permute-start = (f32[16,256]{1,0:T(8,128)S(1)}, f32[16,256]{1,0:T(8,128)S(1)}, u32[]{:S(2)}, u32[]{:S(2)}) collective-permute-start(f32[16,256]{1,0:T(8,128)S(1)} %get-tuple-element.32.own), channel_id=1, source_target_pairs={{0,128},{8,136},{16,144},{24,152},{32,160},{40,168},{48,176},{56,1... | collective-permute-start | bytes 49160 | tf_op jit(solution)/shard_map/ppermute | solution.py:364
  7.6 4.0 %collective-permute-done.far = f32[16,256]{1,0:T(8,128)S(1)} collective-permute-done((f32[16,256]{1,0:T(8,128)S(1)}, f32[16,256]{1,0:T(8,128)S(1)}, u32[]{:S(2)}, u32[]{:S(2)}) %collective-permute-start) | collective-permute-done | bytes 16416 | tf_op jit(solution)/shard_map/ppermute | solution.py:364
  11.8 2.0 %collective-permute-start.4 = (bf16[8,16,128]{2,1,0:T(8,128)(2,1)S(1)}, bf16[8,16,128]{2,1,0:T(8,128)(2,1)S(1)}, u32[]{:S(2)}, u32[]{:S(2)}) collective-permute-start(bf16[8,16,128]{2,1,0:T(8,128)(2,1)S(1)} %get-tuple-element.35._), channel_id=1, source_target_pairs={{0,8},{8,0},{16,24},{24,16},{32,40},{40,32},{48,56},{56,48},{64,72... | collective-permute-start | bytes 98312 | tf_op jit(solution)/shard_map/ppermute | solution.py:365
  13.8 7.0 %collective-permute-start.5 = (bf16[8,16,128]{2,1,0:T(8,128)(2,1)S(1)}, bf16[8,16,128]{2,1,0:T(8,128)(2,1)S(1)}, u32[]{:S(2)}, u32[]{:S(2)}) collective-permute-start(bf16[8,16,128]{2,1,0:T(8,128)(2,1)S(1)} %get-tuple-element.37), channel_id=1, source_target_pairs={{8,16},{16,8},{24,32},{32,24},{40,48},{48,40},{56,64},{64,56},{72,... | collective-permute-start | bytes 98312 | tf_op jit(solution)/shard_map/ppermute | solution.py:366
  20.8 1.6 %collective-permute-start.2 = (f32[32,256]{1,0:T(8,128)S(1)}, f32[32,256]{1,0:T(8,128)S(1)}, u32[]{:S(2)}, u32[]{:S(2)}) collective-permute-start(f32[32,256]{1,0:T(8,128)S(1)} %pad_maximum_fusion.3.near), channel_id=1, source_target_pairs={{0,2},{1,3},{2,0},{3,1},{4,6},{5,7},{6,4},{7,5},{8,10},{9,11},{10,... | collective-permute-start | bytes 98312 | tf_op jit(solution)/shard_map/ppermute | solution.py:360
  22.7 4.3 %product.6 = (f32[16,2048]{1,0:T(8,128)S(1)}, f32[16,256]{1,0:T(8,128)S(1)}, bf16[16,1024,256]{2,1,0:T(8,128)(2,1)S(1)}) custom-call(s32[8,32]{1,0:T(8,128)S(1)} %bitcast.5, f32[1]{0:T(128)S(6)} %copy.15.freq.refs_1_, s32[2]{0:T(128)S(1)} %pad_add_fusion.place.refs_2_, bf16[32,16,128]{2,1,0:T(8,128)(2,1)S(1)} %get-tuple-element.36.refs_3_, ...), custom_call_target="tpu_custom_call" | custom-call | flops 3000000000 | bytes 9000000 | tf_op jit(solution)/shard_map/product/pallas_call | solution.py:402
  27.0 3.3 %copy-done.2 = bf16[16,1024,256]{2,1,0:T(8,128)(2,1)} copy-done((bf16[16,1024,256]{2,1,0:T(8,128)(2,1)}, bf16[16,1024,256]{2,1,0:T(8,128)(2,1)S(1)}, u32[]{:S(2)}) %copy-start.2) | copy-done | bytes 8388632
  30.3 2.8 %collective-permute-start.3 = (f32[64,256]{1,0:T(8,128)S(1)}, f32[64,256]{1,0:T(8,128)S(1)}, u32[]{:S(2)}, u32[]{:S(2)}) collective-permute-start(f32[64,256]{1,0:T(8,128)S(1)} %pad_maximum_fusion), channel_id=1, source_target_pairs={{0,6},{1,7},{2,4},{3,5},{4,2},{5,3},{6,0},{7,1},{8,14},{9,15},{10,... | collective-permute-start | bytes 196616 | tf_op jit(solution)/shard_map/ppermute | solution.py:360
  33.2 4.3 %product.7 = (f32[16,2048]{1,0:T(8,128)S(1)}, f32[16,256]{1,0:T(8,128)S(1)}, bf16[16,1024,256]{2,1,0:T(8,128)(2,1)S(1)}) custom-call(s32[8,32]{1,0:T(8,128)S(1)} %bitcast.6, f32[1]{0:T(128)S(6)} %copy.15.freq.refs_1_, s32[2]{0:T(128)S(1)} %pad_add_fusion.place.refs_2_, bf16[32,16,128]{2,1,0:T(8,128)(2,1)S(1)} %get-tuple-element.36.refs_3_, ...), custom_call_target="tpu_custom_call" | custom-call | flops 3000000000 | bytes 9000000 | tf_op jit(solution)/shard_map/product/pallas_call | solution.py:402
  37.5 1.5 %time.3 = (f32[16,256]{1,0:T(8,128)S(1)}, f32[16,256]{1,0:T(8,128)S(1)}) custom-call(s32[2]{0:T(128)S(1)} %pad_add_fusion.place.refs_2_, f32[32,256]{1,0:T(8,128)S(1)} %pad_maximum_fusion.3.near, f32[32,256]{1,0:T(8,128)S(1)} %collective-permute-done.2.side, f32[64,256]{1,0:T(8,128)S(1)} %collective-permute-done.3.across, bf16[1024,384]{1,0:T(8,128)(2,1)S(1)} %copy-done.8, ...), custom_call_target="tpu_custom_call" | custom-call | flops 1000000000 | bytes 3000000 | tf_op jit(solution)/shard_map/time/pallas_call | solution.py:422
  39.9 2.0 %update.2 = (f32[16,4096]{1,0:T(8,128)}, bf16[32,16,128]{2,1,0:T(8,128)(2,1)S(1)}, bf16[8,16,128]{2,1,0:T(8,128)(2,1)S(1)}, bf16[8,16,128]{2,1,0:T(8,128)(2,1)S(1)}) custom-call(s32[2]{0:T(128)S(1)} %pad_add_fusion.place.refs_2_, f32[16,256]{1,0:T(8,128)S(1)} %get-tuple-element.43.force, bf16[4096,256]{1,0:T(8,128)(2,1)S(1)} %get-tuple-element.38.refs_9_.hot.refs_8_, ...), custom_call_target="tpu_custom_call" | custom-call | flops 800000000 | bytes 2400000 | tf_op jit(solution)/shard_map/update/pallas_call | solution.py:442
  42.0 2.3 %collective-permute-done.6.far = f32[16,256]{1,0:T(8,128)S(1)} collective-permute-done((f32[16,256]{1,0:T(8,128)S(1)}, f32[16,256]{1,0:T(8,128)S(1)}, u32[]{:S(2)}, u32[]{:S(2)}) %collective-permute-start.6) | collective-permute-done | bytes 16416 | tf_op jit(solution)/shard_map/ppermute | solution.py:364
  44.5 6.1 %collective-permute-start.11 = (bf16[8,16,128]{2,1,0:T(8,128)(2,1)S(1)}, bf16[8,16,128]{2,1,0:T(8,128)(2,1)S(1)}, u32[]{:S(2)}, u32[]{:S(2)}) collective-permute-start(bf16[8,16,128]{2,1,0:T(8,128)(2,1)S(1)} %get-tuple-element.48), channel_id=1, source_target_pairs={{8,16},{16,8},{24,32},{32,24},{40,48},{48,40},{56,64},{64,56},{72,... | collective-permute-start | bytes 98312 | tf_op jit(solution)/shard_map/ppermute | solution.py:366
  50.9 1.6 %collective-permute-done.11.refs_5_ = bf16[8,16,128]{2,1,0:T(8,128)(2,1)S(1)} collective-permute-done((bf16[8,16,128]{2,1,0:T(8,128)(2,1)S(1)}, bf16[8,16,128]{2,1,0:T(8,128)(2,1)S(1)}, u32[]{:S(2)}, u32[]{:S(2)}) %collective-permute-start.11) | collective-permute-done | bytes 32800 | tf_op jit(solution)/shard_map/ppermute | solution.py:366
  52.5 3.4 %copy-done.3 = bf16[16,1024,256]{2,1,0:T(8,128)(2,1)S(1)} copy-done((bf16[16,1024,256]{2,1,0:T(8,128)(2,1)S(1)}, bf16[16,1024,256]{2,1,0:T(8,128)(2,1)}, u32[]{:S(2)}) %copy-start.3) | copy-done | bytes 8388632
  55.9 2.1 %product.8 = (f32[16,2048]{1,0:T(8,128)S(1)}, f32[16,256]{1,0:T(8,128)S(1)}) custom-call(s32[8,32]{1,0:T(8,128)S(1)} %bitcast.7, f32[1]{0:T(128)S(6)} %copy.15.freq.refs_1_, s32[2]{0:T(128)S(1)} %pad_add_fusion.place.refs_2_, bf16[32,16,128]{2,1,0:T(8,128)(2,1)S(1)} %get-tuple-element.47.refs_3_, bf16[8,16,128]{2,1,0:T(8,128)(2,1)S(1)} %collective-permute-done.10.refs_4_, ...), custom_call_target="tpu_custom_call" | custom-call | flops 1400000000 | bytes 4200000 | tf_op jit(solution)/shard_map/product/pallas_call | solution.py:402
  58.0 1.4 %collective-permute-start.9 = (f32[64,256]{1,0:T(8,128)S(1)}, f32[64,256]{1,0:T(8,128)S(1)}, u32[]{:S(2)}, u32[]{:S(2)}) collective-permute-start(f32[64,256]{1,0:T(8,128)S(1)} %pad_maximum_fusion.1), channel_id=1, source_target_pairs={{0,6},{1,7},{2,4},{3,5},{4,2},{5,3},{6,0},{7,1},{8,14},{9,15},{10,... | collective-permute-start | bytes 196616 | tf_op jit(solution)/shard_map/ppermute | solution.py:360
  59.4 2.1 %product.9 = (f32[16,2048]{1,0:T(8,128)S(1)}, f32[16,256]{1,0:T(8,128)S(1)}) custom-call(s32[8,32]{1,0:T(8,128)S(1)} %bitcast.8, f32[1]{0:T(128)S(6)} %copy.15.freq.refs_1_, s32[2]{0:T(128)S(1)} %pad_add_fusion.place.refs_2_, bf16[32,16,128]{2,1,0:T(8,128)(2,1)S(1)} %get-tuple-element.47.refs_3_, bf16[8,16,128]{2,1,0:T(8,128)(2,1)S(1)} %collective-permute-done.10.refs_4_, ...), custom_call_target="tpu_custom_call" | custom-call | flops 1400000000 | bytes 4200000 | tf_op jit(solution)/shard_map/product/pallas_call | solution.py:402
  61.5 2.3 %collective-permute-done.9.across = f32[64,256]{1,0:T(8,128)S(1)} collective-permute-done((f32[64,256]{1,0:T(8,128)S(1)}, f32[64,256]{1,0:T(8,128)S(1)}, u32[]{:S(2)}, u32[]{:S(2)}) %collective-permute-start.9) | collective-permute-done | bytes 65568 | tf_op jit(solution)/shard_map/ppermute | solution.py:360
  63.7 1.5 %time.4 = (f32[16,256]{1,0:T(8,128)S(1)}, f32[16,256]{1,0:T(8,128)S(1)}) custom-call(s32[2]{0:T(128)S(1)} %pad_add_fusion.place.refs_2_, f32[32,256]{1,0:T(8,128)S(1)} %pad_maximum_fusion.4.near, f32[32,256]{1,0:T(8,128)S(1)} %collective-permute-done.8.side, f32[64,256]{1,0:T(8,128)S(1)} %collective-permute-done.9.across, bf16[1024,384]{1,0:T(8,128)(2,1)S(1)} %copy-done.8, ...), custom_call_target="tpu_custom_call" | custom-call | flops 1000000000 | bytes 3000000 | tf_op jit(solution)/shard_map/time/pallas_call | solution.py:422
  66.2 1.3 %update.3 = (f32[16,4096]{1,0:T(8,128)S(1)}, bf16[32,16,128]{2,1,0:T(8,128)(2,1)S(1)}, bf16[8,16,128]{2,1,0:T(8,128)(2,1)S(1)}, bf16[8,16,128]{2,1,0:T(8,128)(2,1)S(1)}) custom-call(s32[2]{0:T(128)S(1)} %pad_add_fusion.place.refs_2_, f32[16,256]{1,0:T(8,128)S(1)} %get-tuple-element.54.force, bf16[4096,256]{1,0:T(8,128)(2,1)S(1)} %get-tuple-element.38.refs_9_.hot.refs_8_, ...), custom_call_target="tpu_custom_call" | custom-call | flops 800000000 | bytes 2400000 | tf_op jit(solution)/shard_map/update/pallas_call | solution.py:442
  67.5 3.0 %collective-permute-done.12.far = f32[16,256]{1,0:T(8,128)S(1)} collective-permute-done((f32[16,256]{1,0:T(8,128)S(1)}, f32[16,256]{1,0:T(8,128)S(1)}, u32[]{:S(2)}, u32[]{:S(2)}) %collective-permute-start.12) | collective-permute-done | bytes 16416 | tf_op jit(solution)/shard_map/ppermute | solution.py:364
  70.7 6.0 %collective-permute-start.17 = (bf16[8,16,128]{2,1,0:T(8,128)(2,1)S(1)}, bf16[8,16,128]{2,1,0:T(8,128)(2,1)S(1)}, u32[]{:S(2)}, u32[]{:S(2)}) collective-permute-start(bf16[8,16,128]{2,1,0:T(8,128)(2,1)S(1)} %get-tuple-element.59), channel_id=1, source_target_pairs={{8,16},{16,8},{24,32},{32,24},{40,48},{48,40},{56,64},{64,56},{72,... | collective-permute-start | bytes 98312 | tf_op jit(solution)/shard_map/ppermute | solution.py:366
  76.9 1.8 %collective-permute-done.17.refs_5_ = bf16[8,16,128]{2,1,0:T(8,128)(2,1)S(1)} collective-permute-done((bf16[8,16,128]{2,1,0:T(8,128)(2,1)S(1)}, bf16[8,16,128]{2,1,0:T(8,128)(2,1)S(1)}, u32[]{:S(2)}, u32[]{:S(2)}) %collective-permute-start.17) | collective-permute-done | bytes 32800 | tf_op jit(solution)/shard_map/ppermute | solution.py:366
  78.7 3.4 %copy-done.5 = bf16[16,1024,256]{2,1,0:T(8,128)(2,1)S(1)} copy-done((bf16[16,1024,256]{2,1,0:T(8,128)(2,1)S(1)}, bf16[16,1024,256]{2,1,0:T(8,128)(2,1)}, u32[]{:S(2)}) %copy-start.5) | copy-done | bytes 8388632
  82.1 1.8 %product.11.lin_b = f32[16,2048]{1,0:T(8,128)S(1)} custom-call(s32[8,32]{1,0:T(8,128)S(1)} %bitcast.9, f32[1]{0:T(128)S(6)} %copy.15.freq.refs_1_, s32[2]{0:T(128)S(1)} %pad_add_fusion.place.refs_2_, bf16[32,16,128]{2,1,0:T(8,128)(2,1)S(1)} %get-tuple-element.58.refs_3_, bf16[8,16,128]{2,1,0:T(8,128)(2,1)S(1)} %collective-permute-done.16.refs_4_, ...), custom_call_target="tpu_custom_call" | custom-call | flops 1400000000 | bytes 4200000 | tf_op jit(solution)/shard_map/product/pallas_call | solution.py:402
  83.9 1.2 %collective-permute-start.15 = (f32[64,256]{1,0:T(8,128)S(1)}, f32[64,256]{1,0:T(8,128)S(1)}, u32[]{:S(2)}, u32[]{:S(2)}) collective-permute-start(f32[64,256]{1,0:T(8,128)S(1)} %pad_maximum_fusion.2), channel_id=1, source_target_pairs={{0,6},{1,7},{2,4},{3,5},{4,2},{5,3},{6,0},{7,1},{8,14},{9,15},{10,... | collective-permute-start | bytes 196616 | tf_op jit(solution)/shard_map/ppermute | solution.py:360
  85.1 1.8 %product.10.lin_a = f32[16,2048]{1,0:T(8,128)S(1)} custom-call(s32[8,32]{1,0:T(8,128)S(1)} %bitcast.10, f32[1]{0:T(128)S(6)} %copy.15.freq.refs_1_, s32[2]{0:T(128)S(1)} %pad_add_fusion.place.refs_2_, bf16[32,16,128]{2,1,0:T(8,128)(2,1)S(1)} %get-tuple-element.58.refs_3_, bf16[8,16,128]{2,1,0:T(8,128)(2,1)S(1)} %collective-permute-done.16.refs_4_, ...), custom_call_target="tpu_custom_call" | custom-call | flops 1400000000 | bytes 4200000 | tf_op jit(solution)/shard_map/product/pallas_call | solution.py:402
  86.9 2.5 %collective-permute-done.15.across = f32[64,256]{1,0:T(8,128)S(1)} collective-permute-done((f32[64,256]{1,0:T(8,128)S(1)}, f32[64,256]{1,0:T(8,128)S(1)}, u32[]{:S(2)}, u32[]{:S(2)}) %collective-permute-start.15) | collective-permute-done | bytes 65568 | tf_op jit(solution)/shard_map/ppermute | solution.py:360
  89.5 1.4 %time.5.force = f32[16,256]{1,0:T(8,128)S(1)} custom-call(s32[2]{0:T(128)S(1)} %pad_add_fusion.place.refs_2_, f32[32,256]{1,0:T(8,128)S(1)} %pad_maximum_fusion.5.near, f32[32,256]{1,0:T(8,128)S(1)} %collective-permute-done.14.side, f32[64,256]{1,0:T(8,128)S(1)} %collective-permute-done.15.across, bf16[1024,384]{1,0:T(8,128)(2,1)S(1)} %copy-done.8, ...), custom_call_target="tpu_custom_call" | custom-call | flops 1000000000 | bytes 3000000 | tf_op jit(solution)/shard_map/time/pallas_call | solution.py:422
  90.9 1.6 %finish.1 = (f32[16,4096]{1,0:T(8,128)}, f32[16,4096]{1,0:T(8,128)}) custom-call(f32[16,256]{1,0:T(8,128)S(1)} %time.5.force, bf16[4096,256]{1,0:T(8,128)(2,1)S(1)} %get-tuple-element.38.refs_9_.hot.refs_8_, f32[16,2048]{1,0:T(8,128)S(1)} %product.10.lin_a, f32[16,2048]{1,0:T(8,128)S(1)} %product.11.lin_b, ...), custom_call_target="tpu_custom_call" | custom-call | tf_op jit(solution)/shard_map/finish/pallas_call | solution.py:433
  (52 shorter events, 3.5 us)
Async XLA Ops:
  2.0 20.7 %copy-start = (bf16[32,8,128,128]{3,2,1,0:T(8,128)(2,1)S(1)}, bf16[32,8,128,128]{3,2,1,0:T(8,128)(2,1)}, u32[]{:S(2)}) copy-start(bf16[32,8,128,128]{3,2,1,0:T(8,128)(2,1)} %refs_6_.3) | copy-start | bytes 25165828
  2.0 20.7 %copy-start.1 = (bf16[32,8,128,128]{3,2,1,0:T(8,128)(2,1)S(1)}, bf16[32,8,128,128]{3,2,1,0:T(8,128)(2,1)}, u32[]{:S(2)}) copy-start(bf16[32,8,128,128]{3,2,1,0:T(8,128)(2,1)} %refs_7_.7) | copy-start | bytes 25165828
  2.0 20.7 %copy-start.6 = (f32[16,4096]{1,0:T(8,128)S(1)}, f32[16,4096]{1,0:T(8,128)}, u32[]{:S(2)}) copy-start(f32[16,4096]{1,0:T(8,128)} %refs_7_.11) | copy-start | bytes 786436
  2.0 20.7 %copy-start.7 = (s32[32,8]{0,1:T(8,128)S(1)}, s32[32,8]{0,1:T(8,128)}, u32[]{:S(2)}) copy-start(s32[32,8]{0,1:T(8,128)} %param.15) | copy-start | bytes 3076
  6.3 5.3 %collective-permute-start = (f32[16,256]{1,0:T(8,128)S(1)}, f32[16,256]{1,0:T(8,128)S(1)}, u32[]{:S(2)}, u32[]{:S(2)}) collective-permute-start(f32[16,256]{1,0:T(8,128)S(1)} %get-tuple-element.32.own), channel_id=1, source_target_pairs={{0,128},{8,136},{16,144},{24,152},{32,160},{40,168},{48,176},{56,1... | collective-permute-start | bytes 49160 | tf_op jit(solution)/shard_map/ppermute | solution.py:364
  11.7 9.1 %collective-permute-start.1 = (f32[16,256]{1,0:T(8,128)S(1)}, f32[16,256]{1,0:T(8,128)S(1)}, u32[]{:S(2)}, u32[]{:S(2)}) collective-permute-start(f32[16,256]{1,0:T(8,128)S(1)} %relative.3), channel_id=1, source_target_pairs={{0,1},{1,0},{2,3},{3,2},{4,5},{5,4},{6,7},{7,6},{8,9},{9,8},{10,11... | collective-permute-start | bytes 49160 | tf_op jit(solution)/shard_map/ppermute | solution.py:360
  11.8 10.6 %collective-permute-start.4 = (bf16[8,16,128]{2,1,0:T(8,128)(2,1)S(1)}, bf16[8,16,128]{2,1,0:T(8,128)(2,1)S(1)}, u32[]{:S(2)}, u32[]{:S(2)}) collective-permute-start(bf16[8,16,128]{2,1,0:T(8,128)(2,1)S(1)} %get-tuple-element.35._), channel_id=1, source_target_pairs={{0,8},{8,0},{16,24},{24,16},{32,40},{40,32},{48,56},{56,48},{64,72... | collective-permute-start | bytes 98312 | tf_op jit(solution)/shard_map/ppermute | solution.py:365
  13.8 8.9 %collective-permute-start.5 = (bf16[8,16,128]{2,1,0:T(8,128)(2,1)S(1)}, bf16[8,16,128]{2,1,0:T(8,128)(2,1)S(1)}, u32[]{:S(2)}, u32[]{:S(2)}) collective-permute-start(bf16[8,16,128]{2,1,0:T(8,128)(2,1)S(1)} %get-tuple-element.37), channel_id=1, source_target_pairs={{8,16},{16,8},{24,32},{32,24},{40,48},{48,40},{56,64},{64,56},{72,... | collective-permute-start | bytes 98312 | tf_op jit(solution)/shard_map/ppermute | solution.py:366
  20.8 9.5 %collective-permute-start.2 = (f32[32,256]{1,0:T(8,128)S(1)}, f32[32,256]{1,0:T(8,128)S(1)}, u32[]{:S(2)}, u32[]{:S(2)}) collective-permute-start(f32[32,256]{1,0:T(8,128)S(1)} %pad_maximum_fusion.3.near), channel_id=1, source_target_pairs={{0,2},{1,3},{2,0},{3,1},{4,6},{5,7},{6,4},{7,5},{8,10},{9,11},{10,... | collective-permute-start | bytes 98312 | tf_op jit(solution)/shard_map/ppermute | solution.py:360
  27.0 3.3 %copy-start.2 = (bf16[16,1024,256]{2,1,0:T(8,128)(2,1)}, bf16[16,1024,256]{2,1,0:T(8,128)(2,1)S(1)}, u32[]{:S(2)}) copy-start(bf16[16,1024,256]{2,1,0:T(8,128)(2,1)S(1)} %get-tuple-element.50.refs_6_) | copy-start | bytes 25165828
  30.3 7.2 %collective-permute-start.3 = (f32[64,256]{1,0:T(8,128)S(1)}, f32[64,256]{1,0:T(8,128)S(1)}, u32[]{:S(2)}, u32[]{:S(2)}) collective-permute-start(f32[64,256]{1,0:T(8,128)S(1)} %pad_maximum_fusion), channel_id=1, source_target_pairs={{0,6},{1,7},{2,4},{3,5},{4,2},{5,3},{6,0},{7,1},{8,14},{9,15},{10,... | collective-permute-start | bytes 196616 | tf_op jit(solution)/shard_map/ppermute | solution.py:360
  33.2 4.3 %copy-start.8 = (bf16[1024,384]{1,0:T(8,128)(2,1)S(1)}, bf16[1024,384]{1,0:T(8,128)(2,1)}, u32[]{:S(2)}) copy-start(bf16[1024,384]{1,0:T(8,128)(2,1)} %constant.13.clone.forward) | copy-start | bytes 2359300
  33.2 4.3 %copy-start.9 = (bf16[8,32,1024]{2,1,0:T(8,128)(2,1)S(1)}, bf16[8,32,1024]{2,1,0:T(8,128)(2,1)}, u32[]{:S(2)}) copy-start(bf16[8,32,1024]{2,1,0:T(8,128)(2,1)} %constant.14.clone.backward) | copy-start | bytes 1572868
  37.5 21.9 %copy-start.4 = (bf16[16,1024,256]{2,1,0:T(8,128)(2,1)}, bf16[16,1024,256]{2,1,0:T(8,128)(2,1)S(1)}, u32[]{:S(2)}) copy-start(bf16[16,1024,256]{2,1,0:T(8,128)(2,1)S(1)} %get-tuple-element.49.refs_6_) | copy-start | bytes 25165828
  39.0 5.3 %collective-permute-start.6 = (f32[16,256]{1,0:T(8,128)S(1)}, f32[16,256]{1,0:T(8,128)S(1)}, u32[]{:S(2)}, u32[]{:S(2)}) collective-permute-start(f32[16,256]{1,0:T(8,128)S(1)} %get-tuple-element.42.own), channel_id=1, source_target_pairs={{0,128},{8,136},{16,144},{24,152},{32,160},{40,168},{48,176},{56,1... | collective-permute-start | bytes 49160 | tf_op jit(solution)/shard_map/ppermute | solution.py:364
  44.4 6.2 %collective-permute-start.7 = (f32[16,256]{1,0:T(8,128)S(1)}, f32[16,256]{1,0:T(8,128)S(1)}, u32[]{:S(2)}, u32[]{:S(2)}) collective-permute-start(f32[16,256]{1,0:T(8,128)S(1)} %relative.4), channel_id=1, source_target_pairs={{0,1},{1,0},{2,3},{3,2},{4,5},{5,4},{6,7},{7,6},{8,9},{9,8},{10,11... | collective-permute-start | bytes 49160 | tf_op jit(solution)/shard_map/ppermute | solution.py:360
  44.4 6.5 %collective-permute-start.10 = (bf16[8,16,128]{2,1,0:T(8,128)(2,1)S(1)}, bf16[8,16,128]{2,1,0:T(8,128)(2,1)S(1)}, u32[]{:S(2)}, u32[]{:S(2)}) collective-permute-start(bf16[8,16,128]{2,1,0:T(8,128)(2,1)S(1)} %get-tuple-element.46._), channel_id=1, source_target_pairs={{0,8},{8,0},{16,24},{24,16},{32,40},{40,32},{48,56},{56,48},{64,72... | collective-permute-start | bytes 98312 | tf_op jit(solution)/shard_map/ppermute | solution.py:365
  44.5 8.0 %collective-permute-start.11 = (bf16[8,16,128]{2,1,0:T(8,128)(2,1)S(1)}, bf16[8,16,128]{2,1,0:T(8,128)(2,1)S(1)}, u32[]{:S(2)}, u32[]{:S(2)}) collective-permute-start(bf16[8,16,128]{2,1,0:T(8,128)(2,1)S(1)} %get-tuple-element.48), channel_id=1, source_target_pairs={{8,16},{16,8},{24,32},{32,24},{40,48},{48,40},{56,64},{64,56},{72,... | collective-permute-start | bytes 98312 | tf_op jit(solution)/shard_map/ppermute | solution.py:366
  50.6 7.4 %collective-permute-start.8 = (f32[32,256]{1,0:T(8,128)S(1)}, f32[32,256]{1,0:T(8,128)S(1)}, u32[]{:S(2)}, u32[]{:S(2)}) collective-permute-start(f32[32,256]{1,0:T(8,128)S(1)} %pad_maximum_fusion.4.near), channel_id=1, source_target_pairs={{0,2},{1,3},{2,0},{3,1},{4,6},{5,7},{6,4},{7,5},{8,10},{9,11},{10,... | collective-permute-start | bytes 98312 | tf_op jit(solution)/shard_map/ppermute | solution.py:360
  52.5 3.4 %copy-start.3 = (bf16[16,1024,256]{2,1,0:T(8,128)(2,1)S(1)}, bf16[16,1024,256]{2,1,0:T(8,128)(2,1)}, u32[]{:S(2)}) copy-start(bf16[16,1024,256]{2,1,0:T(8,128)(2,1)} %copy-done.2) | copy-start | bytes 25165828
  58.0 5.7 %collective-permute-start.9 = (f32[64,256]{1,0:T(8,128)S(1)}, f32[64,256]{1,0:T(8,128)S(1)}, u32[]{:S(2)}, u32[]{:S(2)}) collective-permute-start(f32[64,256]{1,0:T(8,128)S(1)} %pad_maximum_fusion.1), channel_id=1, source_target_pairs={{0,6},{1,7},{2,4},{3,5},{4,2},{5,3},{6,0},{7,1},{8,14},{9,15},{10,... | collective-permute-start | bytes 196616 | tf_op jit(solution)/shard_map/ppermute | solution.py:360
  65.2 19.9 %slice-start = ((s8[8388608]{0:T(1024)(128)(4,1)}), s8[4194304]{0:T(1024)(128)(4,1)S(1)}, s32[]{:S(2)}) async-start(s8[8388608]{0:T(1024)(128)(4,1)} %bitcast.3), calls=%async_computation | async-start | bytes 8388608
  65.2 5.3 %collective-permute-start.12 = (f32[16,256]{1,0:T(8,128)S(1)}, f32[16,256]{1,0:T(8,128)S(1)}, u32[]{:S(2)}, u32[]{:S(2)}) collective-permute-start(f32[16,256]{1,0:T(8,128)S(1)} %get-tuple-element.53.own), channel_id=1, source_target_pairs={{0,128},{8,136},{16,144},{24,152},{32,160},{40,168},{48,176},{56,1... | collective-permute-start | bytes 49160 | tf_op jit(solution)/shard_map/ppermute | solution.py:364
  70.6 6.2 %collective-permute-start.13 = (f32[16,256]{1,0:T(8,128)S(1)}, f32[16,256]{1,0:T(8,128)S(1)}, u32[]{:S(2)}, u32[]{:S(2)}) collective-permute-start(f32[16,256]{1,0:T(8,128)S(1)} %relative.5), channel_id=1, source_target_pairs={{0,1},{1,0},{2,3},{3,2},{4,5},{5,4},{6,7},{7,6},{8,9},{9,8},{10,11... | collective-permute-start | bytes 49160 | tf_op jit(solution)/shard_map/ppermute | solution.py:360
  70.6 6.3 %collective-permute-start.16 = (bf16[8,16,128]{2,1,0:T(8,128)(2,1)S(1)}, bf16[8,16,128]{2,1,0:T(8,128)(2,1)S(1)}, u32[]{:S(2)}, u32[]{:S(2)}) collective-permute-start(bf16[8,16,128]{2,1,0:T(8,128)(2,1)S(1)} %get-tuple-element.57._), channel_id=1, source_target_pairs={{0,8},{8,0},{16,24},{24,16},{32,40},{40,32},{48,56},{56,48},{64,72... | collective-permute-start | bytes 98312 | tf_op jit(solution)/shard_map/ppermute | solution.py:365
  70.7 7.9 %collective-permute-start.17 = (bf16[8,16,128]{2,1,0:T(8,128)(2,1)S(1)}, bf16[8,16,128]{2,1,0:T(8,128)(2,1)S(1)}, u32[]{:S(2)}, u32[]{:S(2)}) collective-permute-start(bf16[8,16,128]{2,1,0:T(8,128)(2,1)S(1)} %get-tuple-element.59), channel_id=1, source_target_pairs={{8,16},{16,8},{24,32},{32,24},{40,48},{48,40},{56,64},{64,56},{72,... | collective-permute-start | bytes 98312 | tf_op jit(solution)/shard_map/ppermute | solution.py:366
  76.8 7.1 %collective-permute-start.14 = (f32[32,256]{1,0:T(8,128)S(1)}, f32[32,256]{1,0:T(8,128)S(1)}, u32[]{:S(2)}, u32[]{:S(2)}) collective-permute-start(f32[32,256]{1,0:T(8,128)S(1)} %pad_maximum_fusion.5.near), channel_id=1, source_target_pairs={{0,2},{1,3},{2,0},{3,1},{4,6},{5,7},{6,4},{7,5},{8,10},{9,11},{10,... | collective-permute-start | bytes 98312 | tf_op jit(solution)/shard_map/ppermute | solution.py:360
  78.7 3.4 %copy-start.5 = (bf16[16,1024,256]{2,1,0:T(8,128)(2,1)S(1)}, bf16[16,1024,256]{2,1,0:T(8,128)(2,1)}, u32[]{:S(2)}) copy-start(bf16[16,1024,256]{2,1,0:T(8,128)(2,1)} %copy-done.4) | copy-start | bytes 25165828
  82.1 3.1 %slice-start.1 = ((s8[8388608]{0:T(1024)(128)(4,1)}), s8[4194304]{0:T(1024)(128)(4,1)S(1)}, s32[]{:S(2)}) async-start(s8[8388608]{0:T(1024)(128)(4,1)} %bitcast.3), calls=%async_computation.1 | async-start | bytes 8388608
  83.9 5.6 %collective-permute-start.15 = (f32[64,256]{1,0:T(8,128)S(1)}, f32[64,256]{1,0:T(8,128)S(1)}, u32[]{:S(2)}, u32[]{:S(2)}) collective-permute-start(f32[64,256]{1,0:T(8,128)S(1)} %pad_maximum_fusion.2), channel_id=1, source_target_pairs={{0,6},{1,7},{2,4},{3,5},{4,2},{5,3},{6,0},{7,1},{8,14},{9,15},{10,... | collective-permute-start | bytes 196616 | tf_op jit(solution)/shard_map/ppermute | solution.py:360

commit v3 on v2

--- a/solution.py
+++ b/solution.py
@@ -103,8 +103,8 @@
 
 
 def init_kernel(
-    freq, place, count, load, stiff, mass, rows, pslot, normal, tangent,
-    disp_o, inner_o, even_o, odd_o, dyn_o, inv_o, hot_o, swap_o, listed_o, aux_o,
+    freq, place, count, load, stiff, mass, rows, pslot, normal, tangent, backward, cols,
+    inner_o, even_o, odd_o, dyn_o, inv_o, hot_o, swap_o, listed_o, aux_o, backward_o, place_o, cols_o,
     s_buf, m_buf, l_buf, small_i, small_f, parts, sems,
 ):
     moves = [
@@ -115,6 +115,8 @@
         pltpu.make_async_copy(stiff.at[:, 0], s_buf, sems.at[4]),
         pltpu.make_async_copy(mass.at[:, 0], m_buf, sems.at[5]),
         pltpu.make_async_copy(load, l_buf, sems.at[6]),
+        pltpu.make_async_copy(backward.at[place[0]], backward_o, sems.at[7]),
+        pltpu.make_async_copy(cols, cols_o, sems.at[8]),
     ]
     for move in moves:
         move.start()
@@ -136,7 +138,7 @@
     )
     ones = jnp.ones((OWN, BLK), BF16)
     zero = jnp.zeros((BLK, BLK), BF16)
-    for move in moves[4:]:
+    for move in moves[4:7]:
         move.wait()
     for r in range(ROWS):
         s_diag = dot(ones, jnp.where(eye, s_buf[r], zero))
@@ -146,7 +148,6 @@
         disp = l_buf[:, at] / dynamic
         dyn_o[:, at] = dynamic
         inv_o[:, at] = 1.0 / dynamic
-        disp_o[:, at] = disp
         inner_o[r] = disp.astype(BF16)
         parts[: 3 * OWN, at] = split3(disp)
         parts[3 * OWN :, at] = split3(dynamic)
@@ -154,6 +155,10 @@
     listed_o[...] = sum3(listed[: 3 * OWN])
     aux_o[:OWN, :] = 1.0 / sum3(listed[3 * OWN :])
     put_edges(place, inner_o, even_o, odd_o)
+    place_o[0] = place[0]
+    place_o[1] = place[1]
+    moves[7].wait()
+    moves[8].wait()
 
 
 def relative_kernel(own, far, swap, aux, _, out):
@@ -161,18 +166,17 @@
     out[...] = (own[...] - sum3(facing)) * aux[RATIO : RATIO + 1, :]
 
 
-def fill_field(place, inner, even, odd, field):
-    side = lax.rem(place[1], 2)
-    field[BAND : BAND + ROWS] = inner[...]
-    far_end = BAND + ROWS
-    field[pl.ds((1 - side) * far_end, BAND)] = even[...]
-    field[pl.ds(side * far_end, BAND)] = odd[...]
-
-
-def product_kernel(*refs, start, first, final, more):
+INSIDE = tuple(range(BAND, ROWS - BAND))
+OUTSIDE = tuple(range(BAND)) + tuple(range(ROWS - BAND, ROWS))
+
+
+def product_kernel(*refs, edges, first, final, more):
     refs = list(refs)
-    cols, freq, place, inner, even, odd = refs[:6]
-    del refs[:6]
+    cols, freq, place, inner = refs[:4]
+    del refs[:4]
+    if edges:
+        even, odd = refs[:2]
+        del refs[:2]
     if first:
         stiff, mass = refs[:2]
         del refs[:2]
@@ -190,15 +194,22 @@
     if first:
         wide = refs.pop(0)
     field, parts = refs
-    fill_field(place, inner, even, odd, field)
+    own = place[1] * ROWS
+    if edges:
+        side = lax.rem(place[1], 2)
+        far_end = BAND + ROWS
+        field[BAND:far_end] = inner[...]
+        field[pl.ds((1 - side) * far_end, BAND)] = even[...]
+        field[pl.ds(side * far_end, BAND)] = odd[...]
+        source, offset = field, own - BAND
+    else:
+        source, offset = inner, own
     factor = own_factor(freq, place)
-    offset = place[1] * ROWS - BAND
-
-    def row(i, carry):
-        r = i + start
-        at = cols_of(r)
-        here = cols_of(i)
-        picked = [field[cols[s, r] - offset] for s in range(SLOTS)]
+    chosen = OUTSIDE if edges else INSIDE
+    for i, r in enumerate(chosen):
+        at = slice(r * BLK, (r + 1) * BLK)
+        here = slice(i * BLK, (i + 1) * BLK)
+        picked = [source[cols[s, r] - offset] for s in range(SLOTS)]
         if first:
             for s in range(SLOTS):
                 wide[i, s * BLK : (s + 1) * BLK, :BLK] = stiff[r, s].T
@@ -208,24 +219,34 @@
         rounded = inner[r].astype(F32)
         if final:
             lin_o[:, here] = load[:, at] - (applied + scale[:, at] * (disp[:, at] - rounded))
-            return carry
-        lin = rounded + (load[:, at] - applied) * scale[:, at]
-        lin_o[:, here] = lin
-        parts[:, here] = split3(lin)
-        return carry
-
-    lax.fori_loop(0, HALF, row, 0, unroll=HALF // 2 if first else HALF)
+        else:
+            lin = rounded + (load[:, at] - applied) * scale[:, at]
+            lin_o[:, here] = lin
+            parts[:, here] = split3(lin)
     if not final:
-        made = sum3(dot(parts[...], hot[start * BLK : (start + HALF) * BLK, :]))
+        if edges:
+            cut, tail = BAND * BLK, (ROWS - BAND) * BLK
+            made = dot(parts[:, :cut], hot[:cut, :]) + dot(parts[:, cut:], hot[tail:, :])
+        else:
+            made = dot(parts[...], hot[BAND * BLK : (ROWS - BAND) * BLK, :])
+        made = sum3(made)
         listed_o[...] = made + earlier[...] if more else made
 
 
-def time_kernel(place, near, side, across, forward, backward, aux, *rest, final):
+def lin_block(inside, outside, r):
+    if r in INSIDE:
+        i = INSIDE.index(r)
+        return inside[:, i * BLK : (i + 1) * BLK]
+    i = OUTSIDE.index(r)
+    return outside[:, i * BLK : (i + 1) * BLK]
+
+
+def time_kernel(place, near, opposite, across, forward, backward, aux, *rest, final):
     rel = rest[-1]
     me = place[0]
     for ref, at, other in (
-        (near, 0, 0), (near, 1, 1), (side, 0, 2), (side, 1, 3),
-        (across, 0, 6), (across, 1, 7), (across, 2, 4), (across, 3, 5),
+        (near, 0, 0), (near, 1, 2), (opposite, 0, 6), (opposite, 1, 4),
+        (across, 0, 1), (across, 1, 3), (across, 2, 7), (across, 3, 5),
     ):
         to = pl.multiple_of(jnp.bitwise_xor(me, other) * OWN, OWN)
         rel[pl.ds(to, OWN), :] = ref[at * OWN : (at + 1) * OWN, :]
@@ -237,7 +258,7 @@
     total = jnp.zeros((2 * OWN, CMAX), F32)
     for n in range(0, TIME_POINTS, step):
         values = jnp.tanh(dot(forward[n : n + step, :], stacked)).astype(BF16)
-        total = total + dot(backward[me, :, n : n + step], values)
+        total = total + dot(backward[:, n : n + step], values)
     force = (total[:OWN] + total[OWN:]) * aux[LIMIT : LIMIT + 1, :]
     if final:
         rest[0][...] = force
@@ -254,14 +275,14 @@
     return both[:OWN] + both[OWN:]
 
 
-def update_kernel(place, force, hot, lin_a, lin_b, inv, disp_o, inner_o, even_o, odd_o):
+def update_kernel(place, force, hot, lin_a, lin_b, inv, inner_o, even_o, odd_o, *rest):
     add = force[...]
     for r in range(ROWS):
         at = slice(r * BLK, (r + 1) * BLK)
-        here = slice(r % HALF * BLK, (r % HALF + 1) * BLK)
-        lin = (lin_a if r < HALF else lin_b)[:, here]
+        lin = lin_block(lin_a, lin_b, r)
         disp = lin - spread(add, hot[at, :]) * inv[:, at]
-        disp_o[:, at] = disp
+        if rest:
+            rest[0][:, at] = disp
         inner_o[r] = disp.astype(BF16)
     put_edges(place, inner_o, even_o, odd_o)
 
@@ -270,8 +291,7 @@
     add = force[...]
     for r in range(ROWS):
         at = slice(r * BLK, (r + 1) * BLK)
-        here = slice(r % HALF * BLK, (r % HALF + 1) * BLK)
-        lin = (lin_a if r < HALF else lin_b)[:, here]
+        lin = lin_block(lin_a, lin_b, r)
         residual = lin - spread(add, hot[at, :])
         residual_o[:, at] = residual
         disp_o[:, at] = disp[:, at] + residual * inv[:, at]
@@ -285,7 +305,7 @@
     return pltpu.VMEM(dims, dtype)
 
 
-def params(limit=16):
+def params(limit=4):
     return pltpu.CompilerParams(vmem_limit_bytes=limit << 20)
 
 
@@ -320,18 +340,16 @@
     devices = lax.axis_size("harm")
     cols = block_cols.T
     forward, backward = (jnp.asarray(t) for t in tables())
-    stiff_near = pltpu.with_memory_space_constraint(stiff_blocks, pltpu.VMEM)
-    mass_near = pltpu.with_memory_space_constraint(mass_blocks, pltpu.VMEM)
-
-    disp, inner, even, odd, dyn, inv, hot, swap, listed, aux = pl.pallas_call(
+    inner, even, odd, dyn, inv, hot, swap, listed, aux, backward, place, cols = pl.pallas_call(
         init_kernel,
         out_shape=(
-            shape(FULL), shape(BLOCKED, BF16), shape(EDGE, BF16), shape(EDGE, BF16),
+            shape(BLOCKED, BF16), shape(EDGE, BF16), shape(EDGE, BF16),
             shape(FULL), shape(FULL), shape((DOFS, CMAX), BF16), shape((CMAX, CMAX), BF16),
-            shape(LIST), shape((32, CMAX)),
+            shape(LIST), shape((32, CMAX)), shape((2 * OWN, TIME_POINTS), BF16),
+            pltpu.SMEM((2,), jnp.int32), pltpu.SMEM((SLOTS, ROWS), jnp.int32),
         ),
-        in_specs=[SM, SM, SM] + [FAR] * 7,
-        out_specs=(VM,) * 10,
+        in_specs=[SM, SM, SM] + [FAR] * 9,
+        out_specs=(VM,) * 10 + (SM,) * 2,
         scratch_shapes=[
             pltpu.VMEM((ROWS, BLK, BLK), BF16),
             pltpu.VMEM((ROWS, BLK, BLK), BF16),
@@ -339,7 +357,7 @@
             pltpu.VMEM((2, 1, CMAX), jnp.int32),
             pltpu.VMEM((2, 1, CMAX), F32),
             pltpu.VMEM((6 * OWN, DOFS), BF16),
-            pltpu.SemaphoreType.DMA((7,)),
+            pltpu.SemaphoreType.DMA((9,)),
         ],
         compiler_params=params(),
         cost_estimate=cost(3.0),
@@ -347,9 +365,13 @@
     )(
         frequency, place, contact_count, *(
             pltpu.with_memory_space_constraint(x, pltpu.HBM)
-            for x in (load, stiff_blocks, mass_blocks, contact_rows, partner_slot, normal_load, contact_stiffness)
+            for x in (load, stiff_blocks, mass_blocks, contact_rows, partner_slot, normal_load, contact_stiffness, backward, cols)
         )
     )
+
+    stiff_late, mass_late, _ = lax.optimization_barrier((stiff_blocks, mass_blocks, listed))
+    stiff_near = pltpu.with_memory_space_constraint(stiff_late, pltpu.VMEM)
+    mass_near = pltpu.with_memory_space_constraint(mass_late, pltpu.VMEM)
 
     across = groups // 2
     far = [(i, i ^ across) for i in range(groups)]
@@ -359,11 +381,40 @@
     def flipped(x, bits):
         return lax.ppermute(x, "harm", [(i, i ^ bits) for i in range(devices)])
 
+    wides = []
     for sweep in range(ITERS):
         first, final = sweep == 0, sweep == ITERS - 1
         own_far = lax.ppermute(listed, "comp", far)
         even_in = lax.ppermute(even, "comp", evens)
         odd_in = lax.ppermute(odd, "comp", odds)
+
+        def product(edges, extra):
+            take = [cols, frequency, place, inner] + ([even_in, odd_in] if edges else [])
+            if first:
+                take += [stiff_near, mass_near]
+            else:
+                take += [pltpu.with_memory_space_constraint(wides[int(edges)], pltpu.VMEM)]
+            take += [load, hot, dyn if final else inv]
+            take += ([kept] if final else []) + extra
+            give = [shape(PART)] + ([] if final else [shape(LIST)]) + ([held(WIDE, BF16)] if first else [])
+            outs = pl.pallas_call(
+                functools.partial(product_kernel, edges=edges, first=first, final=final, more=bool(extra)),
+                out_shape=tuple(give),
+                in_specs=[SM] * 3 + [VM] * (len(take) - 3),
+                out_specs=(VM,) * len(give),
+                scratch_shapes=[
+                    pltpu.VMEM((ROWS + 2 * BAND, OWN, BLK), BF16),
+                    pltpu.VMEM((3 * OWN, HALF * BLK), BF16),
+                ],
+                compiler_params=params(),
+                cost_estimate=cost(3.0 if first else 1.5),
+                name="edges" if edges else "inside",
+            )(*take)
+            if first:
+                wides.append(outs[-1])
+            return outs[:1] if final else outs[:2]
+
+        inside = product(False, [])
         relative = pl.pallas_call(
             relative_kernel,
             out_shape=shape(LIST),
@@ -372,53 +423,12 @@
             compiler_params=params(),
             cost_estimate=cost(0.2),
             name="relative",
-        )(listed, own_far, swap, aux, even)
-        near = jnp.concatenate([relative, flipped(relative, 1)], axis=0)
-        side = flipped(near, 2)
-        opposite = flipped(jnp.concatenate([near, side], axis=0), 6)
-        lins, found = [], []
-        for half in range(2):
-            take = [cols, frequency, place, inner, even_in, odd_in]
-            specs = [SM] * 3 + [VM] * 3
-            if first:
-                take += [stiff_near, mass_near]
-                specs += [VM] * 2
-            else:
-                take += [wides[half]]
-                specs += [VM]
-            take += [load, hot, dyn if final else inv]
-            specs += [VM] * 3
-            if final:
-                take += [disp]
-                specs += [VM]
-            elif half:
-                take += [found[0]]
-                specs += [VM]
-            give = [shape(PART)] + ([] if final else [shape(LIST)])
-            given = [VM] * len(give)
-            if first:
-                give += [held(WIDE, BF16)]
-                given += [VM]
-            outs = pl.pallas_call(
-                functools.partial(
-                    product_kernel, start=half * HALF, first=first, final=final, more=half == 1 and not final
-                ),
-                out_shape=tuple(give),
-                in_specs=specs,
-                out_specs=tuple(given),
-                scratch_shapes=[
-                    pltpu.VMEM((ROWS + 2 * BAND, OWN, BLK), BF16),
-                    pltpu.VMEM((3 * OWN, HALF * BLK), BF16),
-                ],
-                compiler_params=params(),
-                cost_estimate=cost(3.0 if first else 1.4),
-                name="product",
-            )(*take)
-            lins.append(outs[0])
-            if not final:
-                found.append(outs[1])
-            if first:
-                wides = [outs[2]] if half == 0 else wides + [outs[2]]
+        )(listed, own_far, swap, aux, inside[0])
+        near = jnp.concatenate([relative, flipped(relative, 2)], axis=0)
+        opposite = flipped(near, 6)
+        across_core = flipped(jnp.concatenate([near, opposite], axis=0), 1)
+        outside = product(True, [] if final else [inside[1]])
+        lins = [inside[0], outside[0]]
         timed = pl.pallas_call(
             functools.partial(time_kernel, final=final),
             out_shape=(shape(LIST),) * (1 if final else 2),
@@ -428,7 +438,7 @@
             compiler_params=params(),
             cost_estimate=cost(1.0),
             name="time",
-        )(place, near, side, opposite, forward, backward, aux, *([] if final else found[1:]))
+        )(place, near, opposite, across_core, forward, backward, aux, *([] if final else [outside[1]]))
         if final:
             return pl.pallas_call(
                 finish_kernel,
@@ -437,17 +447,20 @@
                 out_specs=(VM, VM),
                 compiler_params=params(),
                 name="finish",
-            )(timed[0], hot, *lins, inv, disp)
+            )(timed[0], hot, *lins, inv, kept)
         force, listed = timed
-        disp, inner, even, odd = pl.pallas_call(
+        keep = (shape(FULL),) if sweep == ITERS - 2 else ()
+        inner, even, odd, *rest = pl.pallas_call(
             update_kernel,
-            out_shape=(shape(FULL), shape(BLOCKED, BF16), shape(EDGE, BF16), shape(EDGE, BF16)),
+            out_shape=(shape(BLOCKED, BF16), shape(EDGE, BF16), shape(EDGE, BF16)) + keep,
             in_specs=[SM] + [VM] * 5,
-            out_specs=(VM,) * 4,
+            out_specs=(VM,) * (3 + len(keep)),
             compiler_params=params(),
             cost_estimate=cost(0.8),
             name="update",
         )(place, force, hot, *lins, inv)
+        if rest:
+            kept = rest[0]
 
 
 def solution(mesh):

time: 92.8 us -> 77.9 us (0.84)
  local copies, waits for them, and re-layouts: 10.1 us -> 1.73 us
  Pallas kernels: 30.3 us -> 22.2 us
  starting transfers between devices: 32 us -> 33.2 us
    unnamed x24 -> x8, local copies, waits for them, and re-layouts: 10.1 us -> 1.73 us
    pallas_call x9, Pallas kernels: 24 us -> 17.5 us  [the longest x6 12.4 us: product(): pl.pallas_call(functools.partial(product_kernel, edges=edges, first=first...]
    ppermute x3, waiting for transfers between devices: 9.28 us -> 3.85 us  [local(): own_far = lax.ppermute(listed, 'comp', far)]
    ppermute x9, waiting for transfers between devices: 4.83 us -> 9.24 us  [flipped(): return lax.ppermute(x, 'harm', [(i, i ^ bits) for i in range(devices)])]
    ppermute x3, waiting for transfers between devices: 3.62 us -> 5.24 us  [local(): odd_in = lax.ppermute(odd, 'comp', odds)]
    pallas_call x3, Pallas kernels: 4.35 us -> 2.76 us  [local(): pl.pallas_call(functools.partial(time_kernel, final=final), out_shape=(sh...]
    ppermute x9, starting transfers between devices: 7.47 us -> 8.52 us  [flipped(): return lax.ppermute(x, 'harm', [(i, i ^ bits) for i in range(devices)])]
  transfers between devices with their start and end apart: 18 -> 18, of which waited for: 8 -> 8; matrix products, arithmetic and copies ran while one was open for 0% -> 0% of each run, Pallas kernels for 21% -> 18%
where the time goes in v3:
time: 77.9 us; the launch traced here: 77.7 us
  starting transfers between devices  33.2 us (43%)
  Pallas kernels  22.2 us (28%)
  waiting for transfers between devices  18.3 us (23%)
  between operations  2.1 us (3%)
  local copies, waits for them, and re-layouts  1.73 us (2%)
    ppermute x3, starting transfers between devices, local(): odd_in = lax.ppermute(odd, 'comp', odds)  19.1 us
    pallas_call x6, Pallas kernels, product(): pl.pallas_call(functools.partial(product_kernel, edges=edges, first=first...  12.4 us
    ppermute x9, waiting for transfers between devices, flipped(): return lax.ppermute(x, 'harm', [(i, i ^ bits) for i in range(devices)])  9.24 us
    ppermute x9, starting transfers between devices, flipped(): return lax.ppermute(x, 'harm', [(i, i ^ bits) for i in range(devices)])  8.52 us
    ppermute x3, waiting for transfers between devices, local(): odd_in = lax.ppermute(odd, 'comp', odds)  5.24 us
    ppermute x3, waiting for transfers between devices, local(): own_far = lax.ppermute(listed, 'comp', far)  3.85 us
    ppermute x3, starting transfers between devices, local(): own_far = lax.ppermute(listed, 'comp', far)  3.73 us
    pallas_call x1, Pallas kernels, local(): pl.pallas_call(init_kernel, out_shape=(shape(BLOCKED, BF16), shape(EDGE,...  3.51 us
  transfers between devices with their start and end apart: 18, of which 8 were waited for; matrix products, arithmetic and copies ran while one was open for 0% of the time, Pallas kernels for 18%

profile of v3, /device:TPU:24, one launch (start us, length us, event | category | flops | bytes accessed | tf_op | source)
XLA Modules:
  0.0 77.7 jit_solution(14167853698682561213)
XLA Ops:
  2.0 3.5 %init.1 = (bf16[32,16,128]{2,1,0:T(8,128)(2,1)S(1)}, bf16[8,16,128]{2,1,0:T(8,128)(2,1)S(1)}, bf16[8,16,128]{2,1,0:T(8,128)(2,1)S(1)}, f32[16,4096]{1,0:T(8,128)...) custom-call(f32[1]{0:T(128)S(6)} %copy.15.freq.refs_1_, ...), custom_call_target="tpu_custom_call" | custom-call | flops 3000000000 | bytes 9000000 | tf_op jit(solution)/shard_map/init/pallas_call | solution.py:343
  5.5 1.3 %collective-permute-start = (f32[16,256]{1,0:T(8,128)S(1)}, f32[16,256]{1,0:T(8,128)S(1)}, u32[]{:S(2)}, u32[]{:S(2)}) collective-permute-start(f32[16,256]{1,0:T(8,128)S(1)} %get-tuple-element.38.own), channel_id=1, source_target_pairs={{0,128},{8,136},{16,144},{24,152},{32,160},{40,168},{48,176},{56,1... | collective-permute-start | bytes 49160 | tf_op jit(solution)/shard_map/ppermute | solution.py:387
  6.8 1.7 %copy-done.1 = bf16[32,8,128,128]{3,2,1,0:T(8,128)(2,1)S(1)} copy-done((bf16[32,8,128,128]{3,2,1,0:T(8,128)(2,1)S(1)}, bf16[32,8,128,128]{3,2,1,0:T(8,128)(2,1)}, u32[]{:S(2)}) %copy-start.1) | copy-done | bytes 8388632
  8.6 3.4 %inside.3 = (f32[16,2048]{1,0:T(8,128)S(1)}, f32[16,256]{1,0:T(8,128)S(1)}, bf16[16,1024,256]{2,1,0:T(8,128)(2,1)S(1)}) custom-call(s32[8,32]{1,0:T(8,128)S(4)} %get-tuple-element.41.refs_0_, f32[1]{0:T(128)S(6)} %copy.15.freq.refs_1_, s32[2]{0:T(128)S(4)} %get-tuple-element.37.refs_2_.place, bf16[32,16,128]{2,1,0:T(8,128)(2,1)S(1)} %get-tuple-element.42.refs_3_, ...), custom_call_target="tpu_custom_call" | custom-call | flops 3000000000 | bytes 9000000 | tf_op jit(solution)/shard_map/inside/pallas_call | solution.py:400
  12.1 1.5 %collective-permute-start.1 = (f32[16,256]{1,0:T(8,128)S(1)}, f32[16,256]{1,0:T(8,128)S(1)}, u32[]{:S(2)}, u32[]{:S(2)}) collective-permute-start(f32[16,256]{1,0:T(8,128)S(1)} %relative.3), channel_id=1, source_target_pairs={{0,2},{1,3},{2,0},{3,1},{4,6},{5,7},{6,4},{7,5},{8,10},{9,11},{10,... | collective-permute-start | bytes 49160 | tf_op jit(solution)/shard_map/ppermute | solution.py:382
  13.6 2.2 %collective-permute-done.1 = f32[16,256]{1,0:T(8,128)S(1)} collective-permute-done((f32[16,256]{1,0:T(8,128)S(1)}, f32[16,256]{1,0:T(8,128)S(1)}, u32[]{:S(2)}, u32[]{:S(2)}) %collective-permute-start.1) | collective-permute-done | bytes 16416 | tf_op jit(solution)/shard_map/ppermute | solution.py:382
  15.9 2.8 %collective-permute-start.2 = (f32[32,256]{1,0:T(8,128)S(1)}, f32[32,256]{1,0:T(8,128)S(1)}, u32[]{:S(2)}, u32[]{:S(2)}) collective-permute-start(f32[32,256]{1,0:T(8,128)S(1)} %pad_maximum_fusion.3.near), channel_id=1, source_target_pairs={{0,6},{1,7},{2,4},{3,5},{4,2},{5,3},{6,0},{7,1},{8,14},{9,15},{10,... | collective-permute-start | bytes 98312 | tf_op jit(solution)/shard_map/ppermute | solution.py:382
  18.6 1.9 %collective-permute-start.4 = (bf16[8,16,128]{2,1,0:T(8,128)(2,1)S(1)}, bf16[8,16,128]{2,1,0:T(8,128)(2,1)S(1)}, u32[]{:S(2)}, u32[]{:S(2)}) collective-permute-start(bf16[8,16,128]{2,1,0:T(8,128)(2,1)S(1)} %get-tuple-element.49), channel_id=1, source_target_pairs={{0,8},{8,0},{16,24},{24,16},{32,40},{40,32},{48,56},{56,48},{64,72... | collective-permute-start | bytes 98312 | tf_op jit(solution)/shard_map/ppermute | solution.py:388
  20.5 7.0 %collective-permute-start.5 = (bf16[8,16,128]{2,1,0:T(8,128)(2,1)S(1)}, bf16[8,16,128]{2,1,0:T(8,128)(2,1)S(1)}, u32[]{:S(2)}, u32[]{:S(2)}) collective-permute-start(bf16[8,16,128]{2,1,0:T(8,128)(2,1)S(1)} %get-tuple-element.50), channel_id=1, source_target_pairs={{8,16},{16,8},{24,32},{32,24},{40,48},{48,40},{56,64},{64,56},{72,... | collective-permute-start | bytes 98312 | tf_op jit(solution)/shard_map/ppermute | solution.py:389
  27.7 1.7 %collective-permute-done.5.refs_5_ = bf16[8,16,128]{2,1,0:T(8,128)(2,1)S(1)} collective-permute-done((bf16[8,16,128]{2,1,0:T(8,128)(2,1)S(1)}, bf16[8,16,128]{2,1,0:T(8,128)(2,1)S(1)}, u32[]{:S(2)}, u32[]{:S(2)}) %collective-permute-start.5) | collective-permute-done | bytes 32800 | tf_op jit(solution)/shard_map/ppermute | solution.py:389
  29.4 3.5 %edges.3 = (f32[16,2048]{1,0:T(8,128)S(1)}, f32[16,256]{1,0:T(8,128)S(1)}, bf16[16,1024,256]{2,1,0:T(8,128)(2,1)S(1)}) custom-call(s32[8,32]{1,0:T(8,128)S(4)} %get-tuple-element.41.refs_0_, f32[1]{0:T(128)S(6)} %copy.15.freq.refs_1_, s32[2]{0:T(128)S(4)} %get-tuple-element.37.refs_2_.place, bf16[32,16,128]{2,1,0:T(8,128)(2,1)S(1)} %get-tuple-element.42.refs_3_, ...), custom_call_target="tpu_custom_call" | custom-call | flops 3000000000 | bytes 9000000 | tf_op jit(solution)/shard_map/edges/pallas_call | solution.py:400
  33.0 0.9 %time.3 = (f32[16,256]{1,0:T(8,128)S(1)}, f32[16,256]{1,0:T(8,128)S(1)}) custom-call(s32[2]{0:T(128)S(4)} %get-tuple-element.37.refs_2_.place, f32[32,256]{1,0:T(8,128)S(1)} %pad_maximum_fusion.3.near, f32[32,256]{1,0:T(8,128)S(1)} %collective-permute-done.2.opposite, f32[64,256]{1,0:T(8,128)S(1)} %collective-permute-done.3.across, ...), custom_call_target="tpu_custom_call" | custom-call | flops 1000000000 | bytes 3000000 | tf_op jit(solution)/shard_map/time/pallas_call | solution.py:432
  33.9 1.2 %collective-permute-start.6 = (f32[16,256]{1,0:T(8,128)S(1)}, f32[16,256]{1,0:T(8,128)S(1)}, u32[]{:S(2)}, u32[]{:S(2)}) collective-permute-start(f32[16,256]{1,0:T(8,128)S(1)} %get-tuple-element.53.own), channel_id=1, source_target_pairs={{0,128},{8,136},{16,144},{24,152},{32,160},{40,168},{48,176},{56,1... | collective-permute-start | bytes 49160 | tf_op jit(solution)/shard_map/ppermute | solution.py:387
  35.1 0.8 update.2
  35.8 1.5 %inside.4 = (f32[16,2048]{1,0:T(8,128)S(1)}, f32[16,256]{1,0:T(8,128)S(1)}) custom-call(s32[8,32]{1,0:T(8,128)S(4)} %get-tuple-element.41.refs_0_, f32[1]{0:T(128)S(6)} %copy.15.freq.refs_1_, s32[2]{0:T(128)S(4)} %get-tuple-element.37.refs_2_.place, bf16[32,16,128]{2,1,0:T(8,128)(2,1)S(1)} %get-tuple-element.56.refs_3_, ...), custom_call_target="tpu_custom_call" | custom-call | flops 1500000000 | bytes 4500000 | tf_op jit(solution)/shard_map/inside/pallas_call | solution.py:400
  37.3 1.8 %collective-permute-done.6.far = f32[16,256]{1,0:T(8,128)S(1)} collective-permute-done((f32[16,256]{1,0:T(8,128)S(1)}, f32[16,256]{1,0:T(8,128)S(1)}, u32[]{:S(2)}, u32[]{:S(2)}) %collective-permute-start.6) | collective-permute-done | bytes 16416 | tf_op jit(solution)/shard_map/ppermute | solution.py:387
  39.7 3.5 %collective-permute-done.7 = f32[16,256]{1,0:T(8,128)S(1)} collective-permute-done((f32[16,256]{1,0:T(8,128)S(1)}, f32[16,256]{1,0:T(8,128)S(1)}, u32[]{:S(2)}, u32[]{:S(2)}) %collective-permute-start.7) | collective-permute-done | bytes 16416 | tf_op jit(solution)/shard_map/ppermute | solution.py:382
  43.7 6.0 %collective-permute-start.11 = (bf16[8,16,128]{2,1,0:T(8,128)(2,1)S(1)}, bf16[8,16,128]{2,1,0:T(8,128)(2,1)S(1)}, u32[]{:S(2)}, u32[]{:S(2)}) collective-permute-start(bf16[8,16,128]{2,1,0:T(8,128)(2,1)S(1)} %get-tuple-element.60), channel_id=1, source_target_pairs={{8,16},{16,8},{24,32},{32,24},{40,48},{48,40},{56,64},{64,56},{72,... | collective-permute-start | bytes 98312 | tf_op jit(solution)/shard_map/ppermute | solution.py:389
  49.9 1.7 %collective-permute-done.11.refs_5_ = bf16[8,16,128]{2,1,0:T(8,128)(2,1)S(1)} collective-permute-done((bf16[8,16,128]{2,1,0:T(8,128)(2,1)S(1)}, bf16[8,16,128]{2,1,0:T(8,128)(2,1)S(1)}, u32[]{:S(2)}, u32[]{:S(2)}) %collective-permute-start.11) | collective-permute-done | bytes 32800 | tf_op jit(solution)/shard_map/ppermute | solution.py:389
  51.6 1.6 %edges.4 = (f32[16,2048]{1,0:T(8,128)S(1)}, f32[16,256]{1,0:T(8,128)S(1)}) custom-call(s32[8,32]{1,0:T(8,128)S(4)} %get-tuple-element.41.refs_0_, f32[1]{0:T(128)S(6)} %copy.15.freq.refs_1_, s32[2]{0:T(128)S(4)} %get-tuple-element.37.refs_2_.place, bf16[32,16,128]{2,1,0:T(8,128)(2,1)S(1)} %get-tuple-element.56.refs_3_, ...), custom_call_target="tpu_custom_call" | custom-call | flops 1500000000 | bytes 4500000 | tf_op jit(solution)/shard_map/edges/pallas_call | solution.py:400
  53.2 0.9 %time.4 = (f32[16,256]{1,0:T(8,128)S(1)}, f32[16,256]{1,0:T(8,128)S(1)}) custom-call(s32[2]{0:T(128)S(4)} %get-tuple-element.37.refs_2_.place, f32[32,256]{1,0:T(8,128)S(1)} %pad_maximum_fusion.4.near, f32[32,256]{1,0:T(8,128)S(1)} %collective-permute-done.8.opposite, f32[64,256]{1,0:T(8,128)S(1)} %collective-permute-done.9.across, ...), custom_call_target="tpu_custom_call" | custom-call | flops 1000000000 | bytes 3000000 | tf_op jit(solution)/shard_map/time/pallas_call | solution.py:432
  54.2 1.2 %collective-permute-start.12 = (f32[16,256]{1,0:T(8,128)S(1)}, f32[16,256]{1,0:T(8,128)S(1)}, u32[]{:S(2)}, u32[]{:S(2)}) collective-permute-start(f32[16,256]{1,0:T(8,128)S(1)} %get-tuple-element.64.own), channel_id=1, source_target_pairs={{0,128},{8,136},{16,144},{24,152},{32,160},{40,168},{48,176},{56,1... | collective-permute-start | bytes 49160 | tf_op jit(solution)/shard_map/ppermute | solution.py:387
  55.4 0.8 update.3
  56.1 1.2 %inside.5._.lin_a = f32[16,2048]{1,0:T(8,128)S(1)} custom-call(s32[8,32]{1,0:T(8,128)S(4)} %get-tuple-element.41.refs_0_, f32[1]{0:T(128)S(6)} %copy.15.freq.refs_1_, s32[2]{0:T(128)S(4)} %get-tuple-element.37.refs_2_.place, bf16[32,16,128]{2,1,0:T(8,128)(2,1)S(1)} %get-tuple-element.67.refs_3_, bf16[16,1024,256]{2,1,0:T(8,128)(2,1)S(1)} %get-tuple-element.57.refs_4_, ...), custom_call_target="tpu_custom_call" | custom-call | flops 1500000000 | bytes 4500000 | tf_op jit(solution)/shard_map/inside/pallas_call | solution.py:400
  57.3 2.1 %collective-permute-done.12.far = f32[16,256]{1,0:T(8,128)S(1)} collective-permute-done((f32[16,256]{1,0:T(8,128)S(1)}, f32[16,256]{1,0:T(8,128)S(1)}, u32[]{:S(2)}, u32[]{:S(2)}) %collective-permute-start.12) | collective-permute-done | bytes 16416 | tf_op jit(solution)/shard_map/ppermute | solution.py:387
  59.9 3.5 %collective-permute-done.13 = f32[16,256]{1,0:T(8,128)S(1)} collective-permute-done((f32[16,256]{1,0:T(8,128)S(1)}, f32[16,256]{1,0:T(8,128)S(1)}, u32[]{:S(2)}, u32[]{:S(2)}) %collective-permute-start.13) | collective-permute-done | bytes 16416 | tf_op jit(solution)/shard_map/ppermute | solution.py:382
  63.3 2.8 %collective-permute-start.14 = (f32[32,256]{1,0:T(8,128)S(1)}, f32[32,256]{1,0:T(8,128)S(1)}, u32[]{:S(2)}, u32[]{:S(2)}) collective-permute-start(f32[32,256]{1,0:T(8,128)S(1)} %pad_maximum_fusion.5.near), channel_id=1, source_target_pairs={{0,6},{1,7},{2,4},{3,5},{4,2},{5,3},{6,0},{7,1},{8,14},{9,15},{10,... | collective-permute-start | bytes 98312 | tf_op jit(solution)/shard_map/ppermute | solution.py:382
  66.1 6.0 %collective-permute-start.17 = (bf16[8,16,128]{2,1,0:T(8,128)(2,1)S(1)}, bf16[8,16,128]{2,1,0:T(8,128)(2,1)S(1)}, u32[]{:S(2)}, u32[]{:S(2)}) collective-permute-start(bf16[8,16,128]{2,1,0:T(8,128)(2,1)S(1)} %get-tuple-element.71), channel_id=1, source_target_pairs={{8,16},{16,8},{24,32},{32,24},{40,48},{48,40},{56,64},{64,56},{72,... | collective-permute-start | bytes 98312 | tf_op jit(solution)/shard_map/ppermute | solution.py:389
  72.2 1.7 %collective-permute-done.17.refs_5_ = bf16[8,16,128]{2,1,0:T(8,128)(2,1)S(1)} collective-permute-done((bf16[8,16,128]{2,1,0:T(8,128)(2,1)S(1)}, bf16[8,16,128]{2,1,0:T(8,128)(2,1)S(1)}, u32[]{:S(2)}, u32[]{:S(2)}) %collective-permute-start.17) | collective-permute-done | bytes 32800 | tf_op jit(solution)/shard_map/ppermute | solution.py:389
  74.0 1.2 %edges.5.lin_b = f32[16,2048]{1,0:T(8,128)S(1)} custom-call(s32[8,32]{1,0:T(8,128)S(4)} %get-tuple-element.41.refs_0_, f32[1]{0:T(128)S(6)} %copy.15.freq.refs_1_, s32[2]{0:T(128)S(4)} %get-tuple-element.37.refs_2_.place, bf16[32,16,128]{2,1,0:T(8,128)(2,1)S(1)} %get-tuple-element.67.refs_3_, bf16[8,16,128]{2,1,0:T(8,128)(2,1)S(1)} %collective-permute-done.16.refs_4_, ...), custom_call_target="tpu_custom_call" | custom-call | flops 1500000000 | bytes 4500000 | tf_op jit(solution)/shard_map/edges/pallas_call | solution.py:400
  75.2 0.9 %time.5.force = f32[16,256]{1,0:T(8,128)S(1)} custom-call(s32[2]{0:T(128)S(4)} %get-tuple-element.37.refs_2_.place, f32[32,256]{1,0:T(8,128)S(1)} %pad_maximum_fusion.5.near, f32[32,256]{1,0:T(8,128)S(1)} %collective-permute-done.14.opposite, f32[64,256]{1,0:T(8,128)S(1)} %collective-permute-done.15.across, bf16[1024,384]{1,0:T(8,128)(2,1)S(1)} %copy-done.3, ...), custom_call_target="tpu_custom_call" | custom-call | flops 1000000000 | bytes 3000000 | tf_op jit(solution)/shard_map/time/pallas_call | solution.py:432
  76.1 1.6 %finish.1 = (f32[16,4096]{1,0:T(8,128)}, f32[16,4096]{1,0:T(8,128)}) custom-call(f32[16,256]{1,0:T(8,128)S(1)} %time.5.force, bf16[4096,256]{1,0:T(8,128)(2,1)S(1)} %get-tuple-element.45.refs_7_.refs_9_.hot.refs_6_.refs_8_, f32[16,2048]{1,0:T(8,128)S(1)} %inside.5._.lin_a, f32[16,2048]{1,0:T(8,128)S(1)} %edges.5.lin_b, ...), custom_call_target="tpu_custom_call" | custom-call | tf_op jit(solution)/shard_map/finish/pallas_call | solution.py:443
  (35 shorter events, 2.1 us)
Async XLA Ops:
  2.0 4.9 %copy-start = (bf16[32,8,128,128]{3,2,1,0:T(8,128)(2,1)S(1)}, bf16[32,8,128,128]{3,2,1,0:T(8,128)(2,1)}, u32[]{:S(2)}) copy-start(bf16[32,8,128,128]{3,2,1,0:T(8,128)(2,1)} %refs_6_.2) | copy-start | bytes 25165828
  2.0 6.6 %copy-start.1 = (bf16[32,8,128,128]{3,2,1,0:T(8,128)(2,1)S(1)}, bf16[32,8,128,128]{3,2,1,0:T(8,128)(2,1)}, u32[]{:S(2)}) copy-start(bf16[32,8,128,128]{3,2,1,0:T(8,128)(2,1)} %refs_7_.2) | copy-start | bytes 25165828
  2.0 6.6 %copy-start.2 = (f32[16,4096]{1,0:T(8,128)S(1)}, f32[16,4096]{1,0:T(8,128)}, u32[]{:S(2)}) copy-start(f32[16,4096]{1,0:T(8,128)} %refs_7_.4) | copy-start | bytes 786436
  5.5 6.4 %collective-permute-start = (f32[16,256]{1,0:T(8,128)S(1)}, f32[16,256]{1,0:T(8,128)S(1)}, u32[]{:S(2)}, u32[]{:S(2)}) collective-permute-start(f32[16,256]{1,0:T(8,128)S(1)} %get-tuple-element.38.own), channel_id=1, source_target_pairs={{0,128},{8,136},{16,144},{24,152},{32,160},{40,168},{48,176},{56,1... | collective-permute-start | bytes 49160 | tf_op jit(solution)/shard_map/ppermute | solution.py:387
  12.1 3.8 %collective-permute-start.1 = (f32[16,256]{1,0:T(8,128)S(1)}, f32[16,256]{1,0:T(8,128)S(1)}, u32[]{:S(2)}, u32[]{:S(2)}) collective-permute-start(f32[16,256]{1,0:T(8,128)S(1)} %relative.3), channel_id=1, source_target_pairs={{0,2},{1,3},{2,0},{3,1},{4,6},{5,7},{6,4},{7,5},{8,10},{9,11},{10,... | collective-permute-start | bytes 49160 | tf_op jit(solution)/shard_map/ppermute | solution.py:382
  15.9 11.7 %collective-permute-start.2 = (f32[32,256]{1,0:T(8,128)S(1)}, f32[32,256]{1,0:T(8,128)S(1)}, u32[]{:S(2)}, u32[]{:S(2)}) collective-permute-start(f32[32,256]{1,0:T(8,128)S(1)} %pad_maximum_fusion.3.near), channel_id=1, source_target_pairs={{0,6},{1,7},{2,4},{3,5},{4,2},{5,3},{6,0},{7,1},{8,14},{9,15},{10,... | collective-permute-start | bytes 98312 | tf_op jit(solution)/shard_map/ppermute | solution.py:382
  18.6 9.1 %collective-permute-start.4 = (bf16[8,16,128]{2,1,0:T(8,128)(2,1)S(1)}, bf16[8,16,128]{2,1,0:T(8,128)(2,1)S(1)}, u32[]{:S(2)}, u32[]{:S(2)}) collective-permute-start(bf16[8,16,128]{2,1,0:T(8,128)(2,1)S(1)} %get-tuple-element.49), channel_id=1, source_target_pairs={{0,8},{8,0},{16,24},{24,16},{32,40},{40,32},{48,56},{56,48},{64,72... | collective-permute-start | bytes 98312 | tf_op jit(solution)/shard_map/ppermute | solution.py:388
  20.5 8.9 %collective-permute-start.5 = (bf16[8,16,128]{2,1,0:T(8,128)(2,1)S(1)}, bf16[8,16,128]{2,1,0:T(8,128)(2,1)S(1)}, u32[]{:S(2)}, u32[]{:S(2)}) collective-permute-start(bf16[8,16,128]{2,1,0:T(8,128)(2,1)S(1)} %get-tuple-element.50), channel_id=1, source_target_pairs={{8,16},{16,8},{24,32},{32,24},{40,48},{48,40},{56,64},{64,56},{72,... | collective-permute-start | bytes 98312 | tf_op jit(solution)/shard_map/ppermute | solution.py:389
  27.6 5.4 %collective-permute-start.3 = (f32[64,256]{1,0:T(8,128)S(1)}, f32[64,256]{1,0:T(8,128)S(1)}, u32[]{:S(2)}, u32[]{:S(2)}) collective-permute-start(f32[64,256]{1,0:T(8,128)S(1)} %pad_maximum_fusion), channel_id=1, source_target_pairs={{0,1},{1,0},{2,3},{3,2},{4,5},{5,4},{6,7},{7,6},{8,9},{9,8},{10,11... | collective-permute-start | bytes 196616 | tf_op jit(solution)/shard_map/ppermute | solution.py:382
  29.4 3.5 %copy-start.3 = (bf16[1024,384]{1,0:T(8,128)(2,1)S(1)}, bf16[1024,384]{1,0:T(8,128)(2,1)}, u32[]{:S(2)}) copy-start(bf16[1024,384]{1,0:T(8,128)(2,1)} %constant.13.clone.forward) | copy-start | bytes 2359300
  33.9 5.3 %collective-permute-start.6 = (f32[16,256]{1,0:T(8,128)S(1)}, f32[16,256]{1,0:T(8,128)S(1)}, u32[]{:S(2)}, u32[]{:S(2)}) collective-permute-start(f32[16,256]{1,0:T(8,128)S(1)} %get-tuple-element.53.own), channel_id=1, source_target_pairs={{0,128},{8,136},{16,144},{24,152},{32,160},{40,168},{48,176},{56,1... | collective-permute-start | bytes 49160 | tf_op jit(solution)/shard_map/ppermute | solution.py:387
  39.3 3.9 %collective-permute-start.7 = (f32[16,256]{1,0:T(8,128)S(1)}, f32[16,256]{1,0:T(8,128)S(1)}, u32[]{:S(2)}, u32[]{:S(2)}) collective-permute-start(f32[16,256]{1,0:T(8,128)S(1)} %relative.4), channel_id=1, source_target_pairs={{0,2},{1,3},{2,0},{3,1},{4,6},{5,7},{6,4},{7,5},{8,10},{9,11},{10,... | collective-permute-start | bytes 49160 | tf_op jit(solution)/shard_map/ppermute | solution.py:382
  43.2 6.5 %collective-permute-start.8 = (f32[32,256]{1,0:T(8,128)S(1)}, f32[32,256]{1,0:T(8,128)S(1)}, u32[]{:S(2)}, u32[]{:S(2)}) collective-permute-start(f32[32,256]{1,0:T(8,128)S(1)} %pad_maximum_fusion.4.near), channel_id=1, source_target_pairs={{0,6},{1,7},{2,4},{3,5},{4,2},{5,3},{6,0},{7,1},{8,14},{9,15},{10,... | collective-permute-start | bytes 98312 | tf_op jit(solution)/shard_map/ppermute | solution.py:382
  43.7 6.2 %collective-permute-start.10 = (bf16[8,16,128]{2,1,0:T(8,128)(2,1)S(1)}, bf16[8,16,128]{2,1,0:T(8,128)(2,1)S(1)}, u32[]{:S(2)}, u32[]{:S(2)}) collective-permute-start(bf16[8,16,128]{2,1,0:T(8,128)(2,1)S(1)} %get-tuple-element.59), channel_id=1, source_target_pairs={{0,8},{8,0},{16,24},{24,16},{32,40},{40,32},{48,56},{56,48},{64,72... | collective-permute-start | bytes 98312 | tf_op jit(solution)/shard_map/ppermute | solution.py:388
  43.7 7.9 %collective-permute-start.11 = (bf16[8,16,128]{2,1,0:T(8,128)(2,1)S(1)}, bf16[8,16,128]{2,1,0:T(8,128)(2,1)S(1)}, u32[]{:S(2)}, u32[]{:S(2)}) collective-permute-start(bf16[8,16,128]{2,1,0:T(8,128)(2,1)S(1)} %get-tuple-element.60), channel_id=1, source_target_pairs={{8,16},{16,8},{24,32},{32,24},{40,48},{48,40},{56,64},{64,56},{72,... | collective-permute-start | bytes 98312 | tf_op jit(solution)/shard_map/ppermute | solution.py:389
  49.7 3.5 %collective-permute-start.9 = (f32[64,256]{1,0:T(8,128)S(1)}, f32[64,256]{1,0:T(8,128)S(1)}, u32[]{:S(2)}, u32[]{:S(2)}) collective-permute-start(f32[64,256]{1,0:T(8,128)S(1)} %pad_maximum_fusion.1), channel_id=1, source_target_pairs={{0,1},{1,0},{2,3},{3,2},{4,5},{5,4},{6,7},{7,6},{8,9},{9,8},{10,11... | collective-permute-start | bytes 196616 | tf_op jit(solution)/shard_map/ppermute | solution.py:382
  54.2 5.3 %collective-permute-start.12 = (f32[16,256]{1,0:T(8,128)S(1)}, f32[16,256]{1,0:T(8,128)S(1)}, u32[]{:S(2)}, u32[]{:S(2)}) collective-permute-start(f32[16,256]{1,0:T(8,128)S(1)} %get-tuple-element.64.own), channel_id=1, source_target_pairs={{0,128},{8,136},{16,144},{24,152},{32,160},{40,168},{48,176},{56,1... | collective-permute-start | bytes 49160 | tf_op jit(solution)/shard_map/ppermute | solution.py:387
  59.5 3.8 %collective-permute-start.13 = (f32[16,256]{1,0:T(8,128)S(1)}, f32[16,256]{1,0:T(8,128)S(1)}, u32[]{:S(2)}, u32[]{:S(2)}) collective-permute-start(f32[16,256]{1,0:T(8,128)S(1)} %relative.5), channel_id=1, source_target_pairs={{0,2},{1,3},{2,0},{3,1},{4,6},{5,7},{6,4},{7,5},{8,10},{9,11},{10,... | collective-permute-start | bytes 49160 | tf_op jit(solution)/shard_map/ppermute | solution.py:382
  63.3 8.8 %collective-permute-start.14 = (f32[32,256]{1,0:T(8,128)S(1)}, f32[32,256]{1,0:T(8,128)S(1)}, u32[]{:S(2)}, u32[]{:S(2)}) collective-permute-start(f32[32,256]{1,0:T(8,128)S(1)} %pad_maximum_fusion.5.near), channel_id=1, source_target_pairs={{0,6},{1,7},{2,4},{3,5},{4,2},{5,3},{6,0},{7,1},{8,14},{9,15},{10,... | collective-permute-start | bytes 98312 | tf_op jit(solution)/shard_map/ppermute | solution.py:382
  66.1 6.2 %collective-permute-start.16 = (bf16[8,16,128]{2,1,0:T(8,128)(2,1)S(1)}, bf16[8,16,128]{2,1,0:T(8,128)(2,1)S(1)}, u32[]{:S(2)}, u32[]{:S(2)}) collective-permute-start(bf16[8,16,128]{2,1,0:T(8,128)(2,1)S(1)} %get-tuple-element.70), channel_id=1, source_target_pairs={{0,8},{8,0},{16,24},{24,16},{32,40},{40,32},{48,56},{56,48},{64,72... | collective-permute-start | bytes 98312 | tf_op jit(solution)/shard_map/ppermute | solution.py:388
  66.1 7.9 %collective-permute-start.17 = (bf16[8,16,128]{2,1,0:T(8,128)(2,1)S(1)}, bf16[8,16,128]{2,1,0:T(8,128)(2,1)S(1)}, u32[]{:S(2)}, u32[]{:S(2)}) collective-permute-start(bf16[8,16,128]{2,1,0:T(8,128)(2,1)S(1)} %get-tuple-element.71), channel_id=1, source_target_pairs={{8,16},{16,8},{24,32},{32,24},{40,48},{48,40},{56,64},{64,56},{72,... | collective-permute-start | bytes 98312 | tf_op jit(solution)/shard_map/ppermute | solution.py:389
  72.1 3.1 %collective-permute-start.15 = (f32[64,256]{1,0:T(8,128)S(1)}, f32[64,256]{1,0:T(8,128)S(1)}, u32[]{:S(2)}, u32[]{:S(2)}) collective-permute-start(f32[64,256]{1,0:T(8,128)S(1)} %pad_maximum_fusion.2), channel_id=1, source_target_pairs={{0,1},{1,0},{2,3},{3,2},{4,5},{5,4},{6,7},{7,6},{8,9},{9,8},{10,11... | collective-permute-start | bytes 196616 | tf_op jit(solution)/shard_map/ppermute | solution.py:382

commit v4 on v3

--- a/solution.py
+++ b/solution.py
@@ -19,8 +19,11 @@
 OWN = 16
 ROWS = 32
 HALF = ROWS // 2
-RATIO = 16
-LIMIT = 24
+INV = OWN
+RATIO = 32
+LIMIT = 33
+FACING = 34
+MINE = 48
 CMAX = 256
 DOFS = ROWS * BLK
 F32 = jnp.float32
@@ -40,11 +43,19 @@
     table = np.where(j[None, :] <= H // 2, np.cos(angle), np.sin(angle)).astype(np.float32)
     high = table.astype(ml_dtypes.bfloat16)
     low = (table - high.astype(np.float32)).astype(ml_dtypes.bfloat16)
-    forward = np.concatenate([high, high, low], axis=1)
+    half = TIME_POINTS // 2
+    forward = np.stack(
+        [
+            np.concatenate([high[:half, p::2], high[:half, p::2], low[:half, p::2]], axis=1)
+            for p in range(2)
+        ]
+    )
     weights = (np.where(j == 0, 1.0, 2.0) / TIME_POINTS).astype(np.float32)
     back = (table * weights[None, :]).T
     back_high = back.astype(ml_dtypes.bfloat16)
     back_low = (back - back_high.astype(np.float32)).astype(ml_dtypes.bfloat16)
+    order = np.arange(TIME_POINTS).reshape(2, -1, BLK).transpose(1, 0, 2).reshape(-1)
+    back_high, back_low = back_high[:, order], back_low[:, order]
     backward = np.concatenate(
         [
             back_high.reshape(H // OWN, OWN, TIME_POINTS),
@@ -102,9 +113,14 @@
         odd_o[...] = inner[high]
 
 
+def one_hot(wanted):
+    row = lax.broadcasted_iota(jnp.int32, (CMAX, CMAX), 0)
+    return jnp.where(row == wanted, 1.0, 0.0).astype(BF16)
+
+
 def init_kernel(
     freq, place, count, load, stiff, mass, rows, pslot, normal, tangent, backward, cols,
-    inner_o, even_o, odd_o, dyn_o, inv_o, hot_o, swap_o, listed_o, aux_o, backward_o, place_o, cols_o,
+    inner_o, even_o, odd_o, dyn_o, inv_o, hot_o, swap_o, mine_o, backward_o, place_o, cols_o,
     s_buf, m_buf, l_buf, small_i, small_f, parts, sems,
 ):
     moves = [
@@ -127,12 +143,12 @@
     wanted = small_i[0]
     for r in range(ROWS):
         hot_o[r * BLK : (r + 1) * BLK, :] = jnp.where(in_block + r * BLK == wanted, 1.0, 0.0).astype(BF16)
-    swap_o[...] = jnp.where(
-        lax.broadcasted_iota(jnp.int32, (CMAX, CMAX), 0) == small_i[1], 1.0, 0.0
-    ).astype(BF16)
+    swap_o[...] = one_hot(small_i[1])
     live = lax.broadcasted_iota(jnp.int32, (1, CMAX), 1) < count[0]
-    aux_o[RATIO : RATIO + 1, :] = small_f[1] / small_f[0]
-    aux_o[LIMIT : LIMIT + 1, :] = jnp.where(live, small_f[0], 0.0)
+    mine_o[2 * OWN :, :] = jnp.zeros((MINE - 2 * OWN, CMAX), F32)
+    mine_o[RATIO : RATIO + 1, :] = small_f[1] / small_f[0]
+    mine_o[LIMIT : LIMIT + 1, :] = jnp.where(live, small_f[0], 0.0)
+    mine_o[FACING : FACING + 1, :] = small_i[1].astype(F32)
     eye = lax.broadcasted_iota(jnp.int32, (BLK, BLK), 0) == lax.broadcasted_iota(
         jnp.int32, (BLK, BLK), 1
     )
@@ -152,25 +168,45 @@
         parts[: 3 * OWN, at] = split3(disp)
         parts[3 * OWN :, at] = split3(dynamic)
     listed = dot(parts[...], hot_o[...])
-    listed_o[...] = sum3(listed[: 3 * OWN])
-    aux_o[:OWN, :] = 1.0 / sum3(listed[3 * OWN :])
+    mine_o[:OWN, :] = sum3(listed[: 3 * OWN])
+    mine_o[INV : INV + OWN, :] = 1.0 / sum3(listed[3 * OWN :])
     put_edges(place, inner_o, even_o, odd_o)
     place_o[0] = place[0]
     place_o[1] = place[1]
+    place_o[2] = place[2]
     moves[7].wait()
     moves[8].wait()
 
 
-def relative_kernel(own, far, swap, aux, _, out):
-    facing = dot(split3(far[...]), swap[...])
-    out[...] = (own[...] - sum3(facing)) * aux[RATIO : RATIO + 1, :]
+def relative_kernel(mine, far, swap, *refs, first, final):
+    if first:
+        out, swap_far = refs[-2:]
+        wanted = far[FACING : FACING + 1, :].astype(jnp.int32)
+        swap_far[...] = one_hot(wanted)
+        near_disp, far_disp = mine[:OWN, :], far[:OWN, :]
+    else:
+        swap_far, force, near_lin, far_lin, out = refs
+        near_disp = near_lin[...] - force[:, :CMAX] * mine[INV : INV + OWN, :]
+        far_disp = far_lin[...] - force[:, CMAX:] * far[INV : INV + OWN, :]
+    facing = sum3(dot(split3(far_disp), swap[...]))
+    out[:, :CMAX] = (near_disp - facing) * mine[RATIO : RATIO + 1, :]
+    if not final:
+        facing = sum3(dot(split3(near_disp), swap_far[...]))
+        out[:, CMAX:] = (far_disp - facing) * far[RATIO : RATIO + 1, :]
+
+
+def join_kernel(a, b, *rest):
+    out = rest[-1]
+    n = a.shape[0]
+    out[:n, :] = a[...]
+    out[n:, :] = b[...]
 
 
 INSIDE = tuple(range(BAND, ROWS - BAND))
 OUTSIDE = tuple(range(BAND)) + tuple(range(ROWS - BAND, ROWS))
 
 
-def product_kernel(*refs, edges, first, final, more):
+def product_kernel(*refs, edges, first, final, more, after):
     refs = list(refs)
     cols, freq, place, inner = refs[:4]
     del refs[:4]
@@ -188,6 +224,7 @@
         disp = refs.pop(0)
     if more:
         earlier = refs.pop(0)
+    del refs[:after]
     lin_o = refs.pop(0)
     if not final:
         listed_o = refs.pop(0)
@@ -200,7 +237,8 @@
         far_end = BAND + ROWS
         field[BAND:far_end] = inner[...]
         field[pl.ds((1 - side) * far_end, BAND)] = even[...]
-        field[pl.ds(side * far_end, BAND)] = odd[...]
+        alone = (place[1] == 0) | (place[1] == place[2] - 1)
+        field[pl.ds(side * far_end, BAND)] = jnp.where(alone, jnp.zeros(odd.shape, BF16), odd[...])
         source, offset = field, own - BAND
     else:
         source, offset = inner, own
@@ -241,31 +279,33 @@
     return outside[:, i * BLK : (i + 1) * BLK]
 
 
-def time_kernel(place, near, opposite, across, forward, backward, aux, *rest, final):
-    rel = rest[-1]
-    me = place[0]
+def time_kernel(place, near, opposite, across, forward, backward, mine, far, *rest, final):
+    force_o, rel = rest[-2:]
+    me, width = place[0], near.shape[1]
     for ref, at, other in (
         (near, 0, 0), (near, 1, 2), (opposite, 0, 6), (opposite, 1, 4),
         (across, 0, 1), (across, 1, 3), (across, 2, 7), (across, 3, 5),
     ):
         to = pl.multiple_of(jnp.bitwise_xor(me, other) * OWN, OWN)
-        rel[pl.ds(to, OWN), :] = ref[at * OWN : (at + 1) * OWN, :]
-    whole = rel[...]
-    high = whole.astype(BF16)
-    low = (whole - high.astype(F32)).astype(BF16)
-    stacked = jnp.concatenate([high, low, high], axis=0)
-    step = 256
-    total = jnp.zeros((2 * OWN, CMAX), F32)
-    for n in range(0, TIME_POINTS, step):
-        values = jnp.tanh(dot(forward[n : n + step, :], stacked)).astype(BF16)
-        total = total + dot(backward[:, n : n + step], values)
-    force = (total[:OWN] + total[OWN:]) * aux[LIMIT : LIMIT + 1, :]
-    if final:
-        rest[0][...] = force
-        return
-    lin_rows, force_o, listed_o, _ = rest
-    force_o[...] = force
-    listed_o[...] = lin_rows[...] - force * aux[:OWN, :]
+        for c in range(width // BLK):
+            rel[c, pl.ds(to, OWN), :] = ref[at * OWN : (at + 1) * OWN, c * BLK : (c + 1) * BLK]
+    for first_col in range(0, width, CMAX):
+        stacked = []
+        for parity in range(2):
+            part = jnp.concatenate(
+                [rel[first_col // BLK + c, pl.ds(parity, H // 2, stride=2), :] for c in range(CMAX // BLK)], axis=1
+            )
+            high = part.astype(BF16)
+            low = (part - high.astype(F32)).astype(BF16)
+            stacked.append(jnp.concatenate([high, low, high], axis=0))
+        total = jnp.zeros((2 * OWN, CMAX), F32)
+        for n in range(0, TIME_POINTS // 2, BLK):
+            even = dot(forward[0, n : n + BLK, :], stacked[0])
+            odd = dot(forward[1, n : n + BLK, :], stacked[1])
+            values = jnp.concatenate([jnp.tanh(even + odd).astype(BF16), jnp.tanh(even - odd).astype(BF16)], axis=0)
+            total = total + dot(backward[:, 2 * n : 2 * n + 2 * BLK], values)
+        limit = (far if first_col else mine)[LIMIT : LIMIT + 1, :]
+        force_o[:, first_col : first_col + CMAX] = (total[:OWN] + total[OWN:]) * limit
 
 
 def spread(force, hot_block):
@@ -276,7 +316,7 @@
 
 
 def update_kernel(place, force, hot, lin_a, lin_b, inv, inner_o, even_o, odd_o, *rest):
-    add = force[...]
+    add = force[:, :CMAX]
     for r in range(ROWS):
         at = slice(r * BLK, (r + 1) * BLK)
         lin = lin_block(lin_a, lin_b, r)
@@ -287,14 +327,22 @@
     put_edges(place, inner_o, even_o, odd_o)
 
 
-def finish_kernel(force, hot, lin_a, lin_b, inv, disp, disp_o, residual_o):
-    add = force[...]
+def finish_kernel(force, hot, lin_a, lin_b, inv, disp, disp_o, residual_o, disp_b, residual_b, sems):
+    add = force[:, :CMAX]
+    moves = []
     for r in range(ROWS):
         at = slice(r * BLK, (r + 1) * BLK)
-        lin = lin_block(lin_a, lin_b, r)
-        residual = lin - spread(add, hot[at, :])
-        residual_o[:, at] = residual
-        disp_o[:, at] = disp[:, at] + residual * inv[:, at]
+        residual = lin_block(lin_a, lin_b, r) - spread(add, hot[at, :])
+        residual_b[:, at] = residual
+        disp_b[:, at] = disp[:, at] + residual * inv[:, at]
+        if r % BAND == BAND - 1:
+            part, ready = r // BAND, pl.ds((r + 1 - BAND) * BLK, BAND * BLK)
+            moves.append(pltpu.make_async_copy(disp_b.at[:, ready], disp_o.at[:, ready], sems.at[0, part]))
+            moves.append(pltpu.make_async_copy(residual_b.at[:, ready], residual_o.at[:, ready], sems.at[1, part]))
+            for move in moves[-2:]:
+                move.start()
+    for move in moves:
+        move.wait()
 
 
 def shape(dims, dtype=F32):
@@ -335,21 +383,21 @@
 ):
     harm = lax.axis_index("harm").astype(jnp.int32)
     comp = lax.axis_index("comp").astype(jnp.int32)
-    place = jnp.stack([harm, comp])
+    place = jnp.stack([harm, comp, jnp.int32(lax.axis_size("comp"))])
     groups = lax.axis_size("comp")
     devices = lax.axis_size("harm")
     cols = block_cols.T
     forward, backward = (jnp.asarray(t) for t in tables())
-    inner, even, odd, dyn, inv, hot, swap, listed, aux, backward, place, cols = pl.pallas_call(
+    inner, even, odd, dyn, inv, hot, swap, mine, backward, place, cols = pl.pallas_call(
         init_kernel,
         out_shape=(
             shape(BLOCKED, BF16), shape(EDGE, BF16), shape(EDGE, BF16),
             shape(FULL), shape(FULL), shape((DOFS, CMAX), BF16), shape((CMAX, CMAX), BF16),
-            shape(LIST), shape((32, CMAX)), shape((2 * OWN, TIME_POINTS), BF16),
-            pltpu.SMEM((2,), jnp.int32), pltpu.SMEM((SLOTS, ROWS), jnp.int32),
+            shape((MINE, CMAX)), shape((2 * OWN, TIME_POINTS), BF16),
+            pltpu.SMEM((3,), jnp.int32), pltpu.SMEM((SLOTS, ROWS), jnp.int32),
         ),
         in_specs=[SM, SM, SM] + [FAR] * 9,
-        out_specs=(VM,) * 10 + (SM,) * 2,
+        out_specs=(VM,) * 9 + (SM,) * 2,
         scratch_shapes=[
             pltpu.VMEM((ROWS, BLK, BLK), BF16),
             pltpu.VMEM((ROWS, BLK, BLK), BF16),
@@ -369,36 +417,49 @@
         )
     )
 
-    stiff_late, mass_late, _ = lax.optimization_barrier((stiff_blocks, mass_blocks, listed))
+    stiff_late, mass_late, _ = lax.optimization_barrier((stiff_blocks, mass_blocks, mine))
     stiff_near = pltpu.with_memory_space_constraint(stiff_late, pltpu.VMEM)
     mass_near = pltpu.with_memory_space_constraint(mass_late, pltpu.VMEM)
 
     across = groups // 2
-    far = [(i, i ^ across) for i in range(groups)]
+    facing = [(i, i ^ across) for i in range(groups)]
     evens = [(i, i ^ 1) for i in range(groups)]
-    odds = [(i, j) for i in range(groups) if 0 <= (j := i - 1 + 2 * (i % 2)) < groups]
+    odds = [(i, (i - 1 + 2 * (i % 2)) % groups) for i in range(groups)]
 
     def flipped(x, bits):
         return lax.ppermute(x, "harm", [(i, i ^ bits) for i in range(devices)])
 
-    wides = []
+    far = lax.ppermute(mine, "comp", facing)
+    def join(a, b, *after):
+        return pl.pallas_call(
+            join_kernel,
+            out_shape=shape((2 * a.shape[0], a.shape[1])),
+            in_specs=[VM] * (2 + len(after)),
+            out_specs=VM,
+            compiler_params=params(),
+            cost_estimate=cost(0.1),
+            name="join",
+        )(a, b, *after)
+
+    wides = {}
     for sweep in range(ITERS):
         first, final = sweep == 0, sweep == ITERS - 1
-        own_far = lax.ppermute(listed, "comp", far)
         even_in = lax.ppermute(even, "comp", evens)
         odd_in = lax.ppermute(odd, "comp", odds)
 
-        def product(edges, extra):
+        def product(edges, extra, after=()):
             take = [cols, frequency, place, inner] + ([even_in, odd_in] if edges else [])
             if first:
                 take += [stiff_near, mass_near]
             else:
-                take += [pltpu.with_memory_space_constraint(wides[int(edges)], pltpu.VMEM)]
+                take += [pltpu.with_memory_space_constraint(wides[edges], pltpu.VMEM)]
             take += [load, hot, dyn if final else inv]
-            take += ([kept] if final else []) + extra
+            take += ([kept] if final else []) + [*extra, *after]
             give = [shape(PART)] + ([] if final else [shape(LIST)]) + ([held(WIDE, BF16)] if first else [])
             outs = pl.pallas_call(
-                functools.partial(product_kernel, edges=edges, first=first, final=final, more=bool(extra)),
+                functools.partial(
+                    product_kernel, edges=edges, first=first, final=final, more=bool(extra), after=len(after)
+                ),
                 out_shape=tuple(give),
                 in_specs=[SM] * 3 + [VM] * (len(take) - 3),
                 out_specs=(VM,) * len(give),
@@ -411,44 +472,65 @@
                 name="edges" if edges else "inside",
             )(*take)
             if first:
-                wides.append(outs[-1])
+                wides[edges] = outs[-1]
             return outs[:1] if final else outs[:2]
 
-        inside = product(False, [])
-        relative = pl.pallas_call(
-            relative_kernel,
-            out_shape=shape(LIST),
-            in_specs=[VM] * 5,
-            out_specs=VM,
+        wide_list = LIST if final else (OWN, 2 * CMAX)
+        given = [mine, far, swap] + ([even_in, odd_in] if first else [swap_far, force, near_lin, far_lin])
+        made = pl.pallas_call(
+            functools.partial(relative_kernel, first=first, final=final),
+            out_shape=(shape(wide_list),) + ((shape((CMAX, CMAX), BF16),) if first else ()),
+            in_specs=[VM] * len(given),
+            out_specs=(VM,) * (2 if first else 1),
             compiler_params=params(),
             cost_estimate=cost(0.2),
             name="relative",
-        )(listed, own_far, swap, aux, inside[0])
-        near = jnp.concatenate([relative, flipped(relative, 2)], axis=0)
+        )(*given)
+        relative = made[0]
+        if first:
+            swap_far = made[1]
+        beside = flipped(relative, 2)
+        if first:
+            outside = product(True, [])
+            near = join(relative, beside, outside[0])
+            inside = product(False, outside[1:], [near])
+            added = inside
+        else:
+            near = join(relative, beside)
+            inside = product(False, [], [near])
+            outside = product(True, inside[1:])
+            added = outside
         opposite = flipped(near, 6)
-        across_core = flipped(jnp.concatenate([near, opposite], axis=0), 1)
-        outside = product(True, [] if final else [inside[1]])
+        across_core = flipped(join(near, opposite, inside[0], outside[0]), 1)
         lins = [inside[0], outside[0]]
-        timed = pl.pallas_call(
+        if not final:
+            near_lin = added[1]
+            far_lin = lax.ppermute(near_lin, "comp", facing)
+        given = [near, opposite, across_core, forward, backward, mine, far]
+        force = pl.pallas_call(
             functools.partial(time_kernel, final=final),
-            out_shape=(shape(LIST),) * (1 if final else 2),
-            in_specs=[SM] + [VM] * (6 if final else 7),
-            out_specs=(VM,) * (1 if final else 2),
-            scratch_shapes=[pltpu.VMEM((H, CMAX), F32)],
+            out_shape=shape(wide_list),
+            in_specs=[SM] + [VM] * len(given),
+            out_specs=VM,
+            scratch_shapes=[pltpu.VMEM((wide_list[1] // BLK, H, BLK), F32)],
             compiler_params=params(),
-            cost_estimate=cost(1.0),
+            cost_estimate=cost(1.0 if final else 1.8),
             name="time",
-        )(place, near, opposite, across_core, forward, backward, aux, *([] if final else [outside[1]]))
+        )(place, *given)
         if final:
             return pl.pallas_call(
                 finish_kernel,
                 out_shape=(shape(FULL), shape(FULL)),
                 in_specs=[VM] * 6,
-                out_specs=(VM, VM),
+                out_specs=(FAR, FAR),
+                scratch_shapes=[
+                    pltpu.VMEM(FULL, F32),
+                    pltpu.VMEM(FULL, F32),
+                    pltpu.SemaphoreType.DMA((2, ROWS // BAND)),
+                ],
                 compiler_params=params(),
                 name="finish",
-            )(timed[0], hot, *lins, inv, kept)
-        force, listed = timed
+            )(force, hot, *lins, inv, kept)
         keep = (shape(FULL),) if sweep == ITERS - 2 else ()
         inner, even, odd, *rest = pl.pallas_call(
             update_kernel,

time: 77.9 us -> 68.5 us (0.88)
  the two profiles are of different devices: /device:TPU:24 before, /device:TPU:1 now
where the time goes in v4:
time: 68.5 us; the launch traced here: 68.4 us
  starting transfers between devices  37.1 us (54%)
  Pallas kernels  22.4 us (33%)
  waiting for transfers between devices  6.55 us (10%)
  between operations  2.2 us (3%)
    ppermute x9, starting transfers between devices, flipped(): return lax.ppermute(x, 'harm', [(i, i ^ bits) for i in range(devices)])  15.5 us
    ppermute x3, starting transfers between devices, local(): odd_in = lax.ppermute(odd, 'comp', odds)  14.3 us
    pallas_call x6, Pallas kernels, product(): pl.pallas_call(functools.partial(product_kernel, edges=edges, first=first...  12.4 us
    ppermute x1, starting transfers between devices, local(): far = lax.ppermute(mine, 'comp', facing)  3.83 us
    ppermute x2, waiting for transfers between devices, local(): far_lin = lax.ppermute(near_lin, 'comp', facing)  3.54 us
    pallas_call x1, Pallas kernels, local(): pl.pallas_call(init_kernel, out_shape=(shape(BLOCKED, BF16), shape(EDGE,...  3.52 us
    pallas_call x3, Pallas kernels, local(): pl.pallas_call(functools.partial(time_kernel, final=final), out_shape=sha...  2.93 us
    ppermute x3, starting transfers between devices, local(): even_in = lax.ppermute(even, 'comp', evens)  1.82 us
  transfers between devices with their start and end apart: 18, of which 5 were waited for; matrix products, arithmetic and copies ran while one was open for 0% of the time, Pallas kernels for 24%

profile of v4, /device:TPU:1, one launch (start us, length us, event | category | flops | bytes accessed | tf_op | source)
XLA Modules:
  0.0 68.4 jit_solution(9943350484341769901)
XLA Ops:
  2.0 3.5 %init.1 = (bf16[32,16,128]{2,1,0:T(8,128)(2,1)S(1)}, bf16[8,16,128]{2,1,0:T(8,128)(2,1)S(1)}, bf16[8,16,128]{2,1,0:T(8,128)(2,1)S(1)}, f32[16,4096]{1,0:T(8,128)...) custom-call(f32[1]{0:T(128)S(6)} %copy.15.freq.refs_1_, ...), custom_call_target="tpu_custom_call" | custom-call | flops 3000000000 | bytes 9000000 | tf_op jit(solution)/shard_map/init/pallas_call | solution.py:391
  5.5 3.8 %collective-permute-start = (f32[48,256]{1,0:T(8,128)S(1)}, f32[48,256]{1,0:T(8,128)S(1)}, u32[]{:S(2)}, u32[]{:S(2)}) collective-permute-start(f32[48,256]{1,0:T(8,128)S(1)} %get-tuple-element.35.mine), channel_id=1, source_target_pairs={{0,128},{8,136},{16,144},{24,152},{32,160},{40,168},{48,176},{56,1... | collective-permute-start | bytes 147464 | tf_op jit(solution)/shard_map/ppermute | solution.py:432
  9.4 1.6 %collective-permute-start.1 = (bf16[8,16,128]{2,1,0:T(8,128)(2,1)S(1)}, bf16[8,16,128]{2,1,0:T(8,128)(2,1)S(1)}, u32[]{:S(2)}, u32[]{:S(2)}) collective-permute-start(bf16[8,16,128]{2,1,0:T(8,128)(2,1)S(1)} %get-tuple-element.37), channel_id=1, source_target_pairs={{0,8},{8,0},{16,24},{24,16},{32,40},{40,32},{48,56},{56,48},{64,72... | collective-permute-start | bytes 98312 | tf_op jit(solution)/shard_map/ppermute | solution.py:447
  11.0 5.2 %collective-permute-start.2 = (bf16[8,16,128]{2,1,0:T(8,128)(2,1)S(1)}, bf16[8,16,128]{2,1,0:T(8,128)(2,1)S(1)}, u32[]{:S(2)}, u32[]{:S(2)}) collective-permute-start(bf16[8,16,128]{2,1,0:T(8,128)(2,1)S(1)} %get-tuple-element.38), channel_id=1, source_target_pairs={{0,248},{8,16},{16,8},{24,32},{32,24},{40,48},{48,40},{56,64},{64,... | collective-permute-start | bytes 98312 | tf_op jit(solution)/shard_map/ppermute | solution.py:448
  16.2 1.3 %collective-permute-done.2.refs_1_.refs_5_ = bf16[8,16,128]{2,1,0:T(8,128)(2,1)S(1)} collective-permute-done((bf16[8,16,128]{2,1,0:T(8,128)(2,1)S(1)}, bf16[8,16,128]{2,1,0:T(8,128)(2,1)S(1)}, u32[]{:S(2)}, u32[]{:S(2)}) %collective-permute-start.2) | collective-permute-done | bytes 32800 | tf_op jit(solution)/shard_map/ppermute | solution.py:448
  17.6 1.3 %collective-permute-start.3 = (f32[16,512]{1,0:T(8,128)S(1)}, f32[16,512]{1,0:T(8,128)S(1)}, u32[]{:S(2)}, u32[]{:S(2)}) collective-permute-start(f32[16,512]{1,0:T(8,128)S(1)} %get-tuple-element.40.a), channel_id=1, source_target_pairs={{0,2},{1,3},{2,0},{3,1},{4,6},{5,7},{6,4},{7,5},{8,10},{9,11},{10,... | collective-permute-start | bytes 98312 | tf_op jit(solution)/shard_map/ppermute | solution.py:430
  18.9 3.5 %edges.3 = (f32[16,2048]{1,0:T(8,128)S(1)}, f32[16,256]{1,0:T(8,128)S(1)}, bf16[16,1024,256]{2,1,0:T(8,128)(2,1)S(1)}) custom-call(s32[8,32]{1,0:T(8,128)S(4)} %get-tuple-element.41.refs_0_, f32[1]{0:T(128)S(6)} %copy.15.freq.refs_1_, s32[3]{0:T(128)S(4)} %get-tuple-element.34.refs_2_.place, bf16[32,16,128]{2,1,0:T(8,128)(2,1)S(1)} %get-tuple-element.42.refs_3_, ...), custom_call_target="tpu_custom_call" | custom-call | flops 3000000000 | bytes 9000000 | tf_op jit(solution)/shard_map/edges/pallas_call | solution.py:459
  22.5 1.9 %collective-permute-start.4 = (f32[32,512]{1,0:T(8,128)S(1)}, f32[32,512]{1,0:T(8,128)S(1)}, u32[]{:S(2)}, u32[]{:S(2)}) collective-permute-start(f32[32,512]{1,0:T(8,128)S(1)} %join.6.refs_10_.a.near), channel_id=1, source_target_pairs={{0,6},{1,7},{2,4},{3,5},{4,2},{5,3},{6,0},{7,1},{8,14},{9,15},{10,... | collective-permute-start | bytes 196616 | tf_op jit(solution)/shard_map/ppermute | solution.py:430
  24.4 3.4 %inside.3 = (f32[16,2048]{1,0:T(8,128)S(1)}, f32[16,256]{1,0:T(8,128)S(1)}, bf16[16,1024,256]{2,1,0:T(8,128)(2,1)S(1)}) custom-call(s32[8,32]{1,0:T(8,128)S(4)} %get-tuple-element.41.refs_0_, f32[1]{0:T(128)S(6)} %copy.15.freq.refs_1_, s32[3]{0:T(128)S(4)} %get-tuple-element.34.refs_2_.place, bf16[32,16,128]{2,1,0:T(8,128)(2,1)S(1)} %get-tuple-element.42.refs_3_, ...), custom_call_target="tpu_custom_call" | custom-call | flops 3000000000 | bytes 9000000 | tf_op jit(solution)/shard_map/inside/pallas_call | solution.py:459
  27.8 2.8 %collective-permute-start.5 = (f32[64,512]{1,0:T(8,128)S(1)}, f32[64,512]{1,0:T(8,128)S(1)}, u32[]{:S(2)}, u32[]{:S(2)}) collective-permute-start(f32[64,512]{1,0:T(8,128)S(1)} %join.7), channel_id=1, source_target_pairs={{0,1},{1,0},{2,3},{3,2},{4,5},{5,4},{6,7},{7,6},{8,9},{9,8},{10,11... | collective-permute-start | bytes 393224 | tf_op jit(solution)/shard_map/ppermute | solution.py:430
  30.5 1.4 %collective-permute-start.6 = (f32[16,256]{1,0:T(8,128)S(1)}, f32[16,256]{1,0:T(8,128)S(1)}, u32[]{:S(2)}, u32[]{:S(2)}) collective-permute-start(f32[16,256]{1,0:T(8,128)S(1)} %get-tuple-element.51.refs_2_), channel_id=1, source_target_pairs={{0,128},{8,136},{16,144},{24,152},{32,160},{40,168},{48,176},{56,1... | collective-permute-start | bytes 49160 | tf_op jit(solution)/shard_map/ppermute | solution.py:508
  32.0 1.1 %time.3.refs_1_.force = f32[16,512]{1,0:T(8,128)S(1)} custom-call(s32[3]{0:T(128)S(4)} %get-tuple-element.34.refs_2_.place, f32[32,512]{1,0:T(8,128)S(1)} %join.6.refs_10_.a.near, f32[32,512]{1,0:T(8,128)S(1)} %collective-permute-done.4.b.opposite, f32[64,512]{1,0:T(8,128)S(1)} %collective-permute-done.5.across, bf16[2,512,192]{2,1,0:T(8,128)(2,1)S(1)} %copy-done.3, ...), custom_call_target="tpu_custom_call" | custom-call | flops 1800000000 | bytes 5400000 | tf_op jit(solution)/shard_map/time/pallas_call | solution.py:510
  33.1 1.5 %collective-permute-done.6.refs_3_ = f32[16,256]{1,0:T(8,128)S(1)} collective-permute-done((f32[16,256]{1,0:T(8,128)S(1)}, f32[16,256]{1,0:T(8,128)S(1)}, u32[]{:S(2)}, u32[]{:S(2)}) %collective-permute-start.6) | collective-permute-done | bytes 16416 | tf_op jit(solution)/shard_map/ppermute | solution.py:508
  34.8 0.5 collective-permute-start.7
  35.3 0.8 %update.2 = (bf16[32,16,128]{2,1,0:T(8,128)(2,1)S(1)}, bf16[8,16,128]{2,1,0:T(8,128)(2,1)S(1)}, bf16[8,16,128]{2,1,0:T(8,128)(2,1)S(1)}) custom-call(s32[3]{0:T(128)S(4)} %get-tuple-element.34.refs_2_.place, f32[16,512]{1,0:T(8,128)S(1)} %time.3.refs_1_.force, bf16[4096,256]{1,0:T(8,128)(2,1)S(1)} %get-tuple-element.45.refs_9_.refs_7_.hot.refs_6_.refs_8_, ...), custom_call_target="tpu_custom_call" | custom-call | flops 800000000 | bytes 2400000 | tf_op jit(solution)/shard_map/update/pallas_call | solution.py:535
  36.1 5.2 %collective-permute-start.10 = (bf16[8,16,128]{2,1,0:T(8,128)(2,1)S(1)}, bf16[8,16,128]{2,1,0:T(8,128)(2,1)S(1)}, u32[]{:S(2)}, u32[]{:S(2)}) collective-permute-start(bf16[8,16,128]{2,1,0:T(8,128)(2,1)S(1)} %get-tuple-element.56), channel_id=1, source_target_pairs={{0,248},{8,16},{16,8},{24,32},{32,24},{40,48},{48,40},{56,64},{64,... | collective-permute-start | bytes 98312 | tf_op jit(solution)/shard_map/ppermute | solution.py:448
  41.3 1.6 %collective-permute-start.8 = (f32[32,512]{1,0:T(8,128)S(1)}, f32[32,512]{1,0:T(8,128)S(1)}, u32[]{:S(2)}, u32[]{:S(2)}) collective-permute-start(f32[32,512]{1,0:T(8,128)S(1)} %join.8.refs_8_.a.near), channel_id=1, source_target_pairs={{0,6},{1,7},{2,4},{3,5},{4,2},{5,3},{6,0},{7,1},{8,14},{9,15},{10,... | collective-permute-start | bytes 196616 | tf_op jit(solution)/shard_map/ppermute | solution.py:430
  42.9 1.5 %inside.4 = (f32[16,2048]{1,0:T(8,128)S(1)}, f32[16,256]{1,0:T(8,128)S(1)}) custom-call(s32[8,32]{1,0:T(8,128)S(4)} %get-tuple-element.41.refs_0_, f32[1]{0:T(128)S(6)} %copy.15.freq.refs_1_, s32[3]{0:T(128)S(4)} %get-tuple-element.34.refs_2_.place, bf16[32,16,128]{2,1,0:T(8,128)(2,1)S(1)} %get-tuple-element.52.refs_3_, ...), custom_call_target="tpu_custom_call" | custom-call | flops 1500000000 | bytes 4500000 | tf_op jit(solution)/shard_map/inside/pallas_call | solution.py:459
  44.4 1.6 %edges.4 = (f32[16,2048]{1,0:T(8,128)S(1)}, f32[16,256]{1,0:T(8,128)S(1)}) custom-call(s32[8,32]{1,0:T(8,128)S(4)} %get-tuple-element.41.refs_0_, f32[1]{0:T(128)S(6)} %copy.15.freq.refs_1_, s32[3]{0:T(128)S(4)} %get-tuple-element.34.refs_2_.place, bf16[32,16,128]{2,1,0:T(8,128)(2,1)S(1)} %get-tuple-element.52.refs_3_, ...), custom_call_target="tpu_custom_call" | custom-call | flops 1500000000 | bytes 4500000 | tf_op jit(solution)/shard_map/edges/pallas_call | solution.py:459
  46.1 2.7 %collective-permute-start.11 = (f32[64,512]{1,0:T(8,128)S(1)}, f32[64,512]{1,0:T(8,128)S(1)}, u32[]{:S(2)}, u32[]{:S(2)}) collective-permute-start(f32[64,512]{1,0:T(8,128)S(1)} %join.9), channel_id=1, source_target_pairs={{0,1},{1,0},{2,3},{3,2},{4,5},{5,4},{6,7},{7,6},{8,9},{9,8},{10,11... | collective-permute-start | bytes 393224 | tf_op jit(solution)/shard_map/ppermute | solution.py:430
  49.0 0.8 %collective-permute-done.11.across = f32[64,512]{1,0:T(8,128)S(1)} collective-permute-done((f32[64,512]{1,0:T(8,128)S(1)}, f32[64,512]{1,0:T(8,128)S(1)}, u32[]{:S(2)}, u32[]{:S(2)}) %collective-permute-start.11) | collective-permute-done | bytes 131104 | tf_op jit(solution)/shard_map/ppermute | solution.py:430
  49.7 1.1 %time.4.refs_1_.force = f32[16,512]{1,0:T(8,128)S(1)} custom-call(s32[3]{0:T(128)S(4)} %get-tuple-element.34.refs_2_.place, f32[32,512]{1,0:T(8,128)S(1)} %join.8.refs_8_.a.near, f32[32,512]{1,0:T(8,128)S(1)} %collective-permute-done.8.b.opposite, f32[64,512]{1,0:T(8,128)S(1)} %collective-permute-done.11.across, bf16[2,512,192]{2,1,0:T(8,128)(2,1)S(1)} %copy-done.3, ...), custom_call_target="tpu_custom_call" | custom-call | flops 1800000000 | bytes 5400000 | tf_op jit(solution)/shard_map/time/pallas_call | solution.py:510
  50.9 2.0 %collective-permute-done.12.refs_3_ = f32[16,256]{1,0:T(8,128)S(1)} collective-permute-done((f32[16,256]{1,0:T(8,128)S(1)}, f32[16,256]{1,0:T(8,128)S(1)}, u32[]{:S(2)}, u32[]{:S(2)}) %collective-permute-start.12) | collective-permute-done | bytes 16416 | tf_op jit(solution)/shard_map/ppermute | solution.py:508
  53.4 0.8 %update.3 = (bf16[32,16,128]{2,1,0:T(8,128)(2,1)S(1)}, bf16[8,16,128]{2,1,0:T(8,128)(2,1)S(1)}, bf16[8,16,128]{2,1,0:T(8,128)(2,1)S(1)}, f32[16,4096]{1,0:T(8,128)S(1)}) custom-call(s32[3]{0:T(128)S(4)} %get-tuple-element.34.refs_2_.place, f32[16,512]{1,0:T(8,128)S(1)} %time.4.refs_1_.force, ...), custom_call_target="tpu_custom_call" | custom-call | flops 800000000 | bytes 2400000 | tf_op jit(solution)/shard_map/update/pallas_call | solution.py:535
  54.2 4.0 %collective-permute-start.16 = (bf16[8,16,128]{2,1,0:T(8,128)(2,1)S(1)}, bf16[8,16,128]{2,1,0:T(8,128)(2,1)S(1)}, u32[]{:S(2)}, u32[]{:S(2)}) collective-permute-start(bf16[8,16,128]{2,1,0:T(8,128)(2,1)S(1)} %get-tuple-element.65), channel_id=1, source_target_pairs={{0,248},{8,16},{16,8},{24,32},{32,24},{40,48},{48,40},{56,64},{64,... | collective-permute-start | bytes 98312 | tf_op jit(solution)/shard_map/ppermute | solution.py:448
  58.2 1.8 %collective-permute-start.14 = (f32[32,256]{1,0:T(8,128)S(1)}, f32[32,256]{1,0:T(8,128)S(1)}, u32[]{:S(2)}, u32[]{:S(2)}) collective-permute-start(f32[32,256]{1,0:T(8,128)S(1)} %join.10.refs_9_.a.near), channel_id=1, source_target_pairs={{0,6},{1,7},{2,4},{3,5},{4,2},{5,3},{6,0},{7,1},{8,14},{9,15},{10,... | collective-permute-start | bytes 98312 | tf_op jit(solution)/shard_map/ppermute | solution.py:430
  60.0 1.2 %inside.5.rest_0_.lin_a = f32[16,2048]{1,0:T(8,128)S(1)} custom-call(s32[8,32]{1,0:T(8,128)S(4)} %get-tuple-element.41.refs_0_, f32[1]{0:T(128)S(6)} %copy.15.freq.refs_1_, s32[3]{0:T(128)S(4)} %get-tuple-element.34.refs_2_.place, bf16[32,16,128]{2,1,0:T(8,128)(2,1)S(1)} %get-tuple-element.61.refs_3_, bf16[16,1024,256]{2,1,0:T(8,128)(2,1)S(1)} %get-tuple-element.53.refs_4_, ...), custom_call_target="tpu_custom_call" | custom-call | flops 1500000000 | bytes 4500000 | tf_op jit(solution)/shard_map/inside/pallas_call | solution.py:459
  61.2 1.2 %edges.5.rest_1_.lin_b = f32[16,2048]{1,0:T(8,128)S(1)} custom-call(s32[8,32]{1,0:T(8,128)S(4)} %get-tuple-element.41.refs_0_, f32[1]{0:T(128)S(6)} %copy.15.freq.refs_1_, s32[3]{0:T(128)S(4)} %get-tuple-element.34.refs_2_.place, bf16[32,16,128]{2,1,0:T(8,128)(2,1)S(1)} %get-tuple-element.61.refs_3_, ...), custom_call_target="tpu_custom_call" | custom-call | flops 1500000000 | bytes 4500000 | tf_op jit(solution)/shard_map/edges/pallas_call | solution.py:459
  62.5 2.6 %collective-permute-start.17 = (f32[64,256]{1,0:T(8,128)S(1)}, f32[64,256]{1,0:T(8,128)S(1)}, u32[]{:S(2)}, u32[]{:S(2)}) collective-permute-start(f32[64,256]{1,0:T(8,128)S(1)} %join.11), channel_id=1, source_target_pairs={{0,1},{1,0},{2,3},{3,2},{4,5},{5,4},{6,7},{7,6},{8,9},{9,8},{10,11... | collective-permute-start | bytes 196616 | tf_op jit(solution)/shard_map/ppermute | solution.py:430
  65.1 0.9 %collective-permute-done.17.across = f32[64,256]{1,0:T(8,128)S(1)} collective-permute-done((f32[64,256]{1,0:T(8,128)S(1)}, f32[64,256]{1,0:T(8,128)S(1)}, u32[]{:S(2)}, u32[]{:S(2)}) %collective-permute-start.17) | collective-permute-done | bytes 65568 | tf_op jit(solution)/shard_map/ppermute | solution.py:430
  66.0 0.7 time.5.force
  66.7 1.5 %finish.1 = (f32[16,4096]{1,0:T(8,128)}, f32[16,4096]{1,0:T(8,128)}) custom-call(f32[16,256]{1,0:T(8,128)S(1)} %time.5.force, bf16[4096,256]{1,0:T(8,128)(2,1)S(1)} %get-tuple-element.45.refs_9_.refs_7_.hot.refs_6_.refs_8_, f32[16,2048]{1,0:T(8,128)S(1)} %inside.5.rest_0_.lin_a, f32[16,2048]{1,0:T(8,128)S(1)} %edges.5.rest_1_.lin_b, ...), custom_call_target="tpu_custom_call" | custom-call | tf_op jit(solution)/shard_map/finish/pallas_call | solution.py:521
  (35 shorter events, 1.4 us)
Async XLA Ops:
  2.0 16.9 %copy-start = (bf16[32,8,128,128]{3,2,1,0:T(8,128)(2,1)S(1)}, bf16[32,8,128,128]{3,2,1,0:T(8,128)(2,1)}, u32[]{:S(2)}) copy-start(bf16[32,8,128,128]{3,2,1,0:T(8,128)(2,1)} %refs_4_) | copy-start | bytes 25165828
  2.0 16.9 %copy-start.1 = (bf16[32,8,128,128]{3,2,1,0:T(8,128)(2,1)S(1)}, bf16[32,8,128,128]{3,2,1,0:T(8,128)(2,1)}, u32[]{:S(2)}) copy-start(bf16[32,8,128,128]{3,2,1,0:T(8,128)(2,1)} %refs_5_.2) | copy-start | bytes 25165828
  2.0 16.9 %copy-start.2 = (f32[16,4096]{1,0:T(8,128)S(1)}, f32[16,4096]{1,0:T(8,128)}, u32[]{:S(2)}) copy-start(f32[16,4096]{1,0:T(8,128)} %refs_7_.4) | copy-start | bytes 786436
  5.5 11.9 %collective-permute-start = (f32[48,256]{1,0:T(8,128)S(1)}, f32[48,256]{1,0:T(8,128)S(1)}, u32[]{:S(2)}, u32[]{:S(2)}) collective-permute-start(f32[48,256]{1,0:T(8,128)S(1)} %get-tuple-element.35.mine), channel_id=1, source_target_pairs={{0,128},{8,136},{16,144},{24,152},{32,160},{40,168},{48,176},{56,1... | collective-permute-start | bytes 147464 | tf_op jit(solution)/shard_map/ppermute | solution.py:432
  9.4 6.8 %collective-permute-start.1 = (bf16[8,16,128]{2,1,0:T(8,128)(2,1)S(1)}, bf16[8,16,128]{2,1,0:T(8,128)(2,1)S(1)}, u32[]{:S(2)}, u32[]{:S(2)}) collective-permute-start(bf16[8,16,128]{2,1,0:T(8,128)(2,1)S(1)} %get-tuple-element.37), channel_id=1, source_target_pairs={{0,8},{8,0},{16,24},{24,16},{32,40},{40,32},{48,56},{56,48},{64,72... | collective-permute-start | bytes 98312 | tf_op jit(solution)/shard_map/ppermute | solution.py:447
  11.0 6.5 %collective-permute-start.2 = (bf16[8,16,128]{2,1,0:T(8,128)(2,1)S(1)}, bf16[8,16,128]{2,1,0:T(8,128)(2,1)S(1)}, u32[]{:S(2)}, u32[]{:S(2)}) collective-permute-start(bf16[8,16,128]{2,1,0:T(8,128)(2,1)S(1)} %get-tuple-element.38), channel_id=1, source_target_pairs={{0,248},{8,16},{16,8},{24,32},{32,24},{40,48},{48,40},{56,64},{64,... | collective-permute-start | bytes 98312 | tf_op jit(solution)/shard_map/ppermute | solution.py:448
  17.6 4.8 %collective-permute-start.3 = (f32[16,512]{1,0:T(8,128)S(1)}, f32[16,512]{1,0:T(8,128)S(1)}, u32[]{:S(2)}, u32[]{:S(2)}) collective-permute-start(f32[16,512]{1,0:T(8,128)S(1)} %get-tuple-element.40.a), channel_id=1, source_target_pairs={{0,2},{1,3},{2,0},{3,1},{4,6},{5,7},{6,4},{7,5},{8,10},{9,11},{10,... | collective-permute-start | bytes 98312 | tf_op jit(solution)/shard_map/ppermute | solution.py:430
  22.5 5.3 %collective-permute-start.4 = (f32[32,512]{1,0:T(8,128)S(1)}, f32[32,512]{1,0:T(8,128)S(1)}, u32[]{:S(2)}, u32[]{:S(2)}) collective-permute-start(f32[32,512]{1,0:T(8,128)S(1)} %join.6.refs_10_.a.near), channel_id=1, source_target_pairs={{0,6},{1,7},{2,4},{3,5},{4,2},{5,3},{6,0},{7,1},{8,14},{9,15},{10,... | collective-permute-start | bytes 196616 | tf_op jit(solution)/shard_map/ppermute | solution.py:430
  24.4 7.6 %copy-start.3 = (bf16[2,512,192]{2,1,0:T(8,128)(2,1)S(1)}, bf16[2,512,192]{2,1,0:T(8,128)(2,1)}, u32[]{:S(2)}) copy-start(bf16[2,512,192]{2,1,0:T(8,128)(2,1)} %constant.15.clone.forward) | copy-start | bytes 1179652
  27.8 4.2 %collective-permute-start.5 = (f32[64,512]{1,0:T(8,128)S(1)}, f32[64,512]{1,0:T(8,128)S(1)}, u32[]{:S(2)}, u32[]{:S(2)}) collective-permute-start(f32[64,512]{1,0:T(8,128)S(1)} %join.7), channel_id=1, source_target_pairs={{0,1},{1,0},{2,3},{3,2},{4,5},{5,4},{6,7},{7,6},{8,9},{9,8},{10,11... | collective-permute-start | bytes 393224 | tf_op jit(solution)/shard_map/ppermute | solution.py:430
  30.5 4.1 %collective-permute-start.6 = (f32[16,256]{1,0:T(8,128)S(1)}, f32[16,256]{1,0:T(8,128)S(1)}, u32[]{:S(2)}, u32[]{:S(2)}) collective-permute-start(f32[16,256]{1,0:T(8,128)S(1)} %get-tuple-element.51.refs_2_), channel_id=1, source_target_pairs={{0,128},{8,136},{16,144},{24,152},{32,160},{40,168},{48,176},{56,1... | collective-permute-start | bytes 49160 | tf_op jit(solution)/shard_map/ppermute | solution.py:508
  34.8 6.5 %collective-permute-start.7 = (f32[16,512]{1,0:T(8,128)S(1)}, f32[16,512]{1,0:T(8,128)S(1)}, u32[]{:S(2)}, u32[]{:S(2)}) collective-permute-start(f32[16,512]{1,0:T(8,128)S(1)} %relative.4.a), channel_id=1, source_target_pairs={{0,2},{1,3},{2,0},{3,1},{4,6},{5,7},{6,4},{7,5},{8,10},{9,11},{10,... | collective-permute-start | bytes 98312 | tf_op jit(solution)/shard_map/ppermute | solution.py:430
  36.0 8.4 %collective-permute-start.9 = (bf16[8,16,128]{2,1,0:T(8,128)(2,1)S(1)}, bf16[8,16,128]{2,1,0:T(8,128)(2,1)S(1)}, u32[]{:S(2)}, u32[]{:S(2)}) collective-permute-start(bf16[8,16,128]{2,1,0:T(8,128)(2,1)S(1)} %get-tuple-element.55), channel_id=1, source_target_pairs={{0,8},{8,0},{16,24},{24,16},{32,40},{40,32},{48,56},{56,48},{64,72... | collective-permute-start | bytes 98312 | tf_op jit(solution)/shard_map/ppermute | solution.py:447
  36.1 8.3 %collective-permute-start.10 = (bf16[8,16,128]{2,1,0:T(8,128)(2,1)S(1)}, bf16[8,16,128]{2,1,0:T(8,128)(2,1)S(1)}, u32[]{:S(2)}, u32[]{:S(2)}) collective-permute-start(bf16[8,16,128]{2,1,0:T(8,128)(2,1)S(1)} %get-tuple-element.56), channel_id=1, source_target_pairs={{0,248},{8,16},{16,8},{24,32},{32,24},{40,48},{48,40},{56,64},{64,... | collective-permute-start | bytes 98312 | tf_op jit(solution)/shard_map/ppermute | solution.py:448
  41.3 4.7 %collective-permute-start.8 = (f32[32,512]{1,0:T(8,128)S(1)}, f32[32,512]{1,0:T(8,128)S(1)}, u32[]{:S(2)}, u32[]{:S(2)}) collective-permute-start(f32[32,512]{1,0:T(8,128)S(1)} %join.8.refs_8_.a.near), channel_id=1, source_target_pairs={{0,6},{1,7},{2,4},{3,5},{4,2},{5,3},{6,0},{7,1},{8,14},{9,15},{10,... | collective-permute-start | bytes 196616 | tf_op jit(solution)/shard_map/ppermute | solution.py:430
  46.1 3.7 %collective-permute-start.11 = (f32[64,512]{1,0:T(8,128)S(1)}, f32[64,512]{1,0:T(8,128)S(1)}, u32[]{:S(2)}, u32[]{:S(2)}) collective-permute-start(f32[64,512]{1,0:T(8,128)S(1)} %join.9), channel_id=1, source_target_pairs={{0,1},{1,0},{2,3},{3,2},{4,5},{5,4},{6,7},{7,6},{8,9},{9,8},{10,11... | collective-permute-start | bytes 393224 | tf_op jit(solution)/shard_map/ppermute | solution.py:430
  48.8 4.1 %collective-permute-start.12 = (f32[16,256]{1,0:T(8,128)S(1)}, f32[16,256]{1,0:T(8,128)S(1)}, u32[]{:S(2)}, u32[]{:S(2)}) collective-permute-start(f32[16,256]{1,0:T(8,128)S(1)} %get-tuple-element.60.refs_2_), channel_id=1, source_target_pairs={{0,128},{8,136},{16,144},{24,152},{32,160},{40,168},{48,176},{56,1... | collective-permute-start | bytes 49160 | tf_op jit(solution)/shard_map/ppermute | solution.py:508
  53.0 5.2 %collective-permute-start.13 = (f32[16,256]{1,0:T(8,128)S(1)}, f32[16,256]{1,0:T(8,128)S(1)}, u32[]{:S(2)}, u32[]{:S(2)}) collective-permute-start(f32[16,256]{1,0:T(8,128)S(1)} %relative.5.a), channel_id=1, source_target_pairs={{0,2},{1,3},{2,0},{3,1},{4,6},{5,7},{6,4},{7,5},{8,10},{9,11},{10,... | collective-permute-start | bytes 49160 | tf_op jit(solution)/shard_map/ppermute | solution.py:430
  54.1 7.1 %collective-permute-start.15 = (bf16[8,16,128]{2,1,0:T(8,128)(2,1)S(1)}, bf16[8,16,128]{2,1,0:T(8,128)(2,1)S(1)}, u32[]{:S(2)}, u32[]{:S(2)}) collective-permute-start(bf16[8,16,128]{2,1,0:T(8,128)(2,1)S(1)} %get-tuple-element.64), channel_id=1, source_target_pairs={{0,8},{8,0},{16,24},{24,16},{32,40},{40,32},{48,56},{56,48},{64,72... | collective-permute-start | bytes 98312 | tf_op jit(solution)/shard_map/ppermute | solution.py:447
  54.2 7.0 %collective-permute-start.16 = (bf16[8,16,128]{2,1,0:T(8,128)(2,1)S(1)}, bf16[8,16,128]{2,1,0:T(8,128)(2,1)S(1)}, u32[]{:S(2)}, u32[]{:S(2)}) collective-permute-start(bf16[8,16,128]{2,1,0:T(8,128)(2,1)S(1)} %get-tuple-element.65), channel_id=1, source_target_pairs={{0,248},{8,16},{16,8},{24,32},{32,24},{40,48},{48,40},{56,64},{64,... | collective-permute-start | bytes 98312 | tf_op jit(solution)/shard_map/ppermute | solution.py:448
  58.2 4.3 %collective-permute-start.14 = (f32[32,256]{1,0:T(8,128)S(1)}, f32[32,256]{1,0:T(8,128)S(1)}, u32[]{:S(2)}, u32[]{:S(2)}) collective-permute-start(f32[32,256]{1,0:T(8,128)S(1)} %join.10.refs_9_.a.near), channel_id=1, source_target_pairs={{0,6},{1,7},{2,4},{3,5},{4,2},{5,3},{6,0},{7,1},{8,14},{9,15},{10,... | collective-permute-start | bytes 98312 | tf_op jit(solution)/shard_map/ppermute | solution.py:430
  62.5 3.5 %collective-permute-start.17 = (f32[64,256]{1,0:T(8,128)S(1)}, f32[64,256]{1,0:T(8,128)S(1)}, u32[]{:S(2)}, u32[]{:S(2)}) collective-permute-start(f32[64,256]{1,0:T(8,128)S(1)} %join.11), channel_id=1, source_target_pairs={{0,1},{1,0},{2,3},{3,2},{4,5},{5,4},{6,7},{7,6},{8,9},{9,8},{10,11... | collective-permute-start | bytes 196616 | tf_op jit(solution)/shard_map/ppermute | solution.py:430

commit v5 on v4

--- a/solution.py
+++ b/solution.py
@@ -161,9 +161,10 @@
         m_diag = dot(ones, jnp.where(eye, m_buf[r], zero))
         dynamic = s_diag - factor * m_diag
         at = slice(r * BLK, (r + 1) * BLK)
-        disp = l_buf[:, at] / dynamic
+        inverse = 1.0 / dynamic
+        disp = l_buf[:, at] * inverse
         dyn_o[:, at] = dynamic
-        inv_o[:, at] = 1.0 / dynamic
+        inv_o[:, at] = inverse
         inner_o[r] = disp.astype(BF16)
         parts[: 3 * OWN, at] = split3(disp)
         parts[3 * OWN :, at] = split3(dynamic)
@@ -185,7 +186,7 @@
         swap_far[...] = one_hot(wanted)
         near_disp, far_disp = mine[:OWN, :], far[:OWN, :]
     else:
-        swap_far, force, near_lin, far_lin, out = refs
+        swap_far, force, near_lin, far_lin, _, out = refs
         near_disp = near_lin[...] - force[:, :CMAX] * mine[INV : INV + OWN, :]
         far_disp = far_lin[...] - force[:, CMAX:] * far[INV : INV + OWN, :]
     facing = sum3(dot(split3(far_disp), swap[...]))
@@ -476,7 +477,7 @@
             return outs[:1] if final else outs[:2]
 
         wide_list = LIST if final else (OWN, 2 * CMAX)
-        given = [mine, far, swap] + ([even_in, odd_in] if first else [swap_far, force, near_lin, far_lin])
+        given = [mine, far, swap] + ([even_in] if first else [swap_far, force, near_lin, far_lin, inner])
         made = pl.pallas_call(
             functools.partial(relative_kernel, first=first, final=final),
             out_shape=(shape(wide_list),) + ((shape((CMAX, CMAX), BF16),) if first else ()),
@@ -491,15 +492,14 @@
             swap_far = made[1]
         beside = flipped(relative, 2)
         if first:
-            outside = product(True, [])
-            near = join(relative, beside, outside[0])
-            inside = product(False, outside[1:], [near])
-            added = inside
+            inside = product(False, [])
+            near = join(relative, beside, inside[0])
+            outside = product(True, inside[1:], [near])
         else:
             near = join(relative, beside)
             inside = product(False, [], [near])
             outside = product(True, inside[1:])
-            added = outside
+        added = outside
         opposite = flipped(near, 6)
         across_core = flipped(join(near, opposite, inside[0], outside[0]), 1)
         lins = [inside[0], outside[0]]
@@ -514,7 +514,7 @@
             out_specs=VM,
             scratch_shapes=[pltpu.VMEM((wide_list[1] // BLK, H, BLK), F32)],
             compiler_params=params(),
-            cost_estimate=cost(1.0 if final else 1.8),
+            cost_estimate=cost(0.01),
             name="time",
         )(place, *given)
         if final:
@@ -538,7 +538,7 @@
             in_specs=[SM] + [VM] * 5,
             out_specs=(VM,) * (3 + len(keep)),
             compiler_params=params(),
-            cost_estimate=cost(0.8),
+            cost_estimate=cost(0.01),
             name="update",
         )(place, force, hot, *lins, inv)
         if rest:

time: 68.5 us -> 63.8 us (0.931)
  waiting for transfers between devices: 6.55 us -> 3.57 us
  starting transfers between devices: 37.1 us -> 35.4 us
    ppermute x3, starting transfers between devices: 14.3 us -> 10.5 us  [local(): odd_in = lax.ppermute(odd, 'comp', odds)]
    ppermute x2, waiting for transfers between devices: 3.54 us -> 1.67 us  [local(): far_lin = lax.ppermute(near_lin, 'comp', facing)]
    ppermute x2, starting transfers between devices: 1.65 us -> 2.74 us  [local(): far_lin = lax.ppermute(near_lin, 'comp', facing)]
    ppermute x9, waiting for transfers between devices: 1.69 us -> 0.95 us  [flipped(): return lax.ppermute(x, 'harm', [(i, i ^ bits) for i in range(devices)])]
  transfers between devices with their start and end apart: 18 -> 18, of which waited for: 5 -> 4; matrix products, arithmetic and copies ran while one was open for 0% -> 0% of each run, Pallas kernels for 24% -> 26%
where the time goes in v5:
time: 63.8 us; the launch traced here: 63.7 us
  starting transfers between devices  35.4 us (55%)
  Pallas kernels  22.4 us (35%)
  waiting for transfers between devices  3.57 us (6%)
  between operations  2.18 us (3%)
    ppermute x9, starting transfers between devices, flipped(): return lax.ppermute(x, 'harm', [(i, i ^ bits) for i in range(devices)])  16 us
    pallas_call x6, Pallas kernels, product(): pl.pallas_call(functools.partial(product_kernel, edges=edges, first=first...  12.4 us
    ppermute x3, starting transfers between devices, local(): odd_in = lax.ppermute(odd, 'comp', odds)  10.5 us
    ppermute x1, starting transfers between devices, local(): far = lax.ppermute(mine, 'comp', facing)  3.83 us
    pallas_call x1, Pallas kernels, local(): pl.pallas_call(init_kernel, out_shape=(shape(BLOCKED, BF16), shape(EDGE,...  3.52 us
    pallas_call x3, Pallas kernels, local(): pl.pallas_call(functools.partial(time_kernel, final=final), out_shape=sha...  2.93 us
    ppermute x2, starting transfers between devices, local(): far_lin = lax.ppermute(near_lin, 'comp', facing)  2.74 us
    ppermute x3, starting transfers between devices, local(): even_in = lax.ppermute(even, 'comp', evens)  2.42 us
  transfers between devices with their start and end apart: 18, of which 4 were waited for; matrix products, arithmetic and copies ran while one was open for 0% of the time, Pallas kernels for 26%

profile of v5, /device:TPU:1, one launch (start us, length us, event | category | flops | bytes accessed | tf_op | source)
XLA Modules:
  0.0 63.7 jit_solution(3135645831819201894)
XLA Ops:
  2.0 3.5 %init.1 = (bf16[32,16,128]{2,1,0:T(8,128)(2,1)S(1)}, bf16[8,16,128]{2,1,0:T(8,128)(2,1)S(1)}, bf16[8,16,128]{2,1,0:T(8,128)(2,1)S(1)}, f32[16,4096]{1,0:T(8,128)...) custom-call(f32[1]{0:T(128)S(6)} %copy.15.freq.refs_1_, ...), custom_call_target="tpu_custom_call" | custom-call | flops 3000000000 | bytes 9000000 | tf_op jit(solution)/shard_map/init/pallas_call | solution.py:392
  5.5 3.8 %collective-permute-start = (f32[48,256]{1,0:T(8,128)S(1)}, f32[48,256]{1,0:T(8,128)S(1)}, u32[]{:S(2)}, u32[]{:S(2)}) collective-permute-start(f32[48,256]{1,0:T(8,128)S(1)} %get-tuple-element.35.mine), channel_id=1, source_target_pairs={{0,128},{8,136},{16,144},{24,152},{32,160},{40,168},{48,176},{56,1... | collective-permute-start | bytes 147464 | tf_op jit(solution)/shard_map/ppermute | solution.py:433
  9.4 1.6 %collective-permute-start.1 = (bf16[8,16,128]{2,1,0:T(8,128)(2,1)S(1)}, bf16[8,16,128]{2,1,0:T(8,128)(2,1)S(1)}, u32[]{:S(2)}, u32[]{:S(2)}) collective-permute-start(bf16[8,16,128]{2,1,0:T(8,128)(2,1)S(1)} %get-tuple-element.37), channel_id=1, source_target_pairs={{0,8},{8,0},{16,24},{24,16},{32,40},{40,32},{48,56},{56,48},{64,72... | collective-permute-start | bytes 98312 | tf_op jit(solution)/shard_map/ppermute | solution.py:448
  11.0 5.2 %collective-permute-start.4 = (bf16[8,16,128]{2,1,0:T(8,128)(2,1)S(1)}, bf16[8,16,128]{2,1,0:T(8,128)(2,1)S(1)}, u32[]{:S(2)}, u32[]{:S(2)}) collective-permute-start(bf16[8,16,128]{2,1,0:T(8,128)(2,1)S(1)} %get-tuple-element.47), channel_id=1, source_target_pairs={{0,248},{8,16},{16,8},{24,32},{32,24},{40,48},{48,40},{56,64},{64,... | collective-permute-start | bytes 98312 | tf_op jit(solution)/shard_map/ppermute | solution.py:449
  16.3 1.3 %collective-permute-start.2 = (f32[16,512]{1,0:T(8,128)S(1)}, f32[16,512]{1,0:T(8,128)S(1)}, u32[]{:S(2)}, u32[]{:S(2)}) collective-permute-start(f32[16,512]{1,0:T(8,128)S(1)} %get-tuple-element.39.a), channel_id=1, source_target_pairs={{0,2},{1,3},{2,0},{3,1},{4,6},{5,7},{6,4},{7,5},{8,10},{9,11},{10,... | collective-permute-start | bytes 98312 | tf_op jit(solution)/shard_map/ppermute | solution.py:431
  17.6 3.4 %inside.3 = (f32[16,2048]{1,0:T(8,128)S(1)}, f32[16,256]{1,0:T(8,128)S(1)}, bf16[16,1024,256]{2,1,0:T(8,128)(2,1)S(1)}) custom-call(s32[8,32]{1,0:T(8,128)S(4)} %get-tuple-element.40.refs_0_, f32[1]{0:T(128)S(6)} %copy.15.freq.refs_1_, s32[3]{0:T(128)S(4)} %get-tuple-element.34.refs_2_.place, bf16[32,16,128]{2,1,0:T(8,128)(2,1)S(1)} %get-tuple-element.41.refs_3_, ...), custom_call_target="tpu_custom_call" | custom-call | flops 3000000000 | bytes 9000000 | tf_op jit(solution)/shard_map/inside/pallas_call | solution.py:460
  21.0 1.9 %collective-permute-start.3 = (f32[32,512]{1,0:T(8,128)S(1)}, f32[32,512]{1,0:T(8,128)S(1)}, u32[]{:S(2)}, u32[]{:S(2)}) collective-permute-start(f32[32,512]{1,0:T(8,128)S(1)} %join.6.refs_12_.a.near), channel_id=1, source_target_pairs={{0,6},{1,7},{2,4},{3,5},{4,2},{5,3},{6,0},{7,1},{8,14},{9,15},{10,... | collective-permute-start | bytes 196616 | tf_op jit(solution)/shard_map/ppermute | solution.py:431
  22.9 3.5 %edges.3 = (f32[16,2048]{1,0:T(8,128)S(1)}, f32[16,256]{1,0:T(8,128)S(1)}, bf16[16,1024,256]{2,1,0:T(8,128)(2,1)S(1)}) custom-call(s32[8,32]{1,0:T(8,128)S(4)} %get-tuple-element.40.refs_0_, f32[1]{0:T(128)S(6)} %copy.15.freq.refs_1_, s32[3]{0:T(128)S(4)} %get-tuple-element.34.refs_2_.place, bf16[32,16,128]{2,1,0:T(8,128)(2,1)S(1)} %get-tuple-element.41.refs_3_, ...), custom_call_target="tpu_custom_call" | custom-call | flops 3000000000 | bytes 9000000 | tf_op jit(solution)/shard_map/edges/pallas_call | solution.py:460
  26.5 2.2 %collective-permute-start.5 = (f32[64,512]{1,0:T(8,128)S(1)}, f32[64,512]{1,0:T(8,128)S(1)}, u32[]{:S(2)}, u32[]{:S(2)}) collective-permute-start(f32[64,512]{1,0:T(8,128)S(1)} %join.7), channel_id=1, source_target_pairs={{0,1},{1,0},{2,3},{3,2},{4,5},{5,4},{6,7},{7,6},{8,9},{9,8},{10,11... | collective-permute-start | bytes 393224 | tf_op jit(solution)/shard_map/ppermute | solution.py:431
  28.6 1.4 %collective-permute-start.6 = (f32[16,256]{1,0:T(8,128)S(1)}, f32[16,256]{1,0:T(8,128)S(1)}, u32[]{:S(2)}, u32[]{:S(2)}) collective-permute-start(f32[16,256]{1,0:T(8,128)S(1)} %get-tuple-element.51.refs_2_), channel_id=1, source_target_pairs={{0,128},{8,136},{16,144},{24,152},{32,160},{40,168},{48,176},{56,1... | collective-permute-start | bytes 49160 | tf_op jit(solution)/shard_map/ppermute | solution.py:508
  30.1 1.1 %time.3.force.refs_1_ = f32[16,512]{1,0:T(8,128)S(1)} custom-call(s32[3]{0:T(128)S(4)} %get-tuple-element.34.refs_2_.place, f32[32,512]{1,0:T(8,128)S(1)} %join.6.refs_12_.a.near, f32[32,512]{1,0:T(8,128)S(1)} %collective-permute-done.3.b.opposite, f32[64,512]{1,0:T(8,128)S(1)} %collective-permute-done.5.across, bf16[2,512,192]{2,1,0:T(8,128)(2,1)S(1)} %copy-done.3, ...), custom_call_target="tpu_custom_call" | custom-call | flops 10000000 | bytes 30000 | tf_op jit(solution)/shard_map/time/pallas_call | solution.py:510
  31.2 0.8 %update.2 = (bf16[32,16,128]{2,1,0:T(8,128)(2,1)S(1)}, bf16[8,16,128]{2,1,0:T(8,128)(2,1)S(1)}, bf16[8,16,128]{2,1,0:T(8,128)(2,1)S(1)}) custom-call(s32[3]{0:T(128)S(4)} %get-tuple-element.34.refs_2_.place, f32[16,512]{1,0:T(8,128)S(1)} %time.3.force.refs_1_, bf16[4096,256]{1,0:T(8,128)(2,1)S(1)} %get-tuple-element.44.refs_7_.refs_9_.hot.refs_6_.refs_8_, ...), custom_call_target="tpu_custom_call" | custom-call | flops 10000000 | bytes 30000 | tf_op jit(solution)/shard_map/update/pallas_call | solution.py:535
  32.0 0.8 %collective-permute-done.6.refs_3_ = f32[16,256]{1,0:T(8,128)S(1)} collective-permute-done((f32[16,256]{1,0:T(8,128)S(1)}, f32[16,256]{1,0:T(8,128)S(1)}, u32[]{:S(2)}, u32[]{:S(2)}) %collective-permute-start.6) | collective-permute-done | bytes 16416 | tf_op jit(solution)/shard_map/ppermute | solution.py:508
  33.4 3.1 %collective-permute-start.10 = (bf16[8,16,128]{2,1,0:T(8,128)(2,1)S(1)}, bf16[8,16,128]{2,1,0:T(8,128)(2,1)S(1)}, u32[]{:S(2)}, u32[]{:S(2)}) collective-permute-start(bf16[8,16,128]{2,1,0:T(8,128)(2,1)S(1)} %get-tuple-element.56), channel_id=1, source_target_pairs={{0,248},{8,16},{16,8},{24,32},{32,24},{40,48},{48,40},{56,64},{64,... | collective-permute-start | bytes 98312 | tf_op jit(solution)/shard_map/ppermute | solution.py:449
  36.5 1.5 %collective-permute-start.8 = (f32[32,512]{1,0:T(8,128)S(1)}, f32[32,512]{1,0:T(8,128)S(1)}, u32[]{:S(2)}, u32[]{:S(2)}) collective-permute-start(f32[32,512]{1,0:T(8,128)S(1)} %join.8.refs_8_.a.near), channel_id=1, source_target_pairs={{0,6},{1,7},{2,4},{3,5},{4,2},{5,3},{6,0},{7,1},{8,14},{9,15},{10,... | collective-permute-start | bytes 196616 | tf_op jit(solution)/shard_map/ppermute | solution.py:431
  38.0 1.5 %inside.4 = (f32[16,2048]{1,0:T(8,128)S(1)}, f32[16,256]{1,0:T(8,128)S(1)}) custom-call(s32[8,32]{1,0:T(8,128)S(4)} %get-tuple-element.40.refs_0_, f32[1]{0:T(128)S(6)} %copy.15.freq.refs_1_, s32[3]{0:T(128)S(4)} %get-tuple-element.34.refs_2_.place, bf16[32,16,128]{2,1,0:T(8,128)(2,1)S(1)} %get-tuple-element.52.refs_4_.refs_3_, ...), custom_call_target="tpu_custom_call" | custom-call | flops 1500000000 | bytes 4500000 | tf_op jit(solution)/shard_map/inside/pallas_call | solution.py:460
  39.5 1.6 %edges.4 = (f32[16,2048]{1,0:T(8,128)S(1)}, f32[16,256]{1,0:T(8,128)S(1)}) custom-call(s32[8,32]{1,0:T(8,128)S(4)} %get-tuple-element.40.refs_0_, f32[1]{0:T(128)S(6)} %copy.15.freq.refs_1_, s32[3]{0:T(128)S(4)} %get-tuple-element.34.refs_2_.place, bf16[32,16,128]{2,1,0:T(8,128)(2,1)S(1)} %get-tuple-element.52.refs_4_.refs_3_, ...), custom_call_target="tpu_custom_call" | custom-call | flops 1500000000 | bytes 4500000 | tf_op jit(solution)/shard_map/edges/pallas_call | solution.py:460
  41.2 2.7 %collective-permute-start.11 = (f32[64,512]{1,0:T(8,128)S(1)}, f32[64,512]{1,0:T(8,128)S(1)}, u32[]{:S(2)}, u32[]{:S(2)}) collective-permute-start(f32[64,512]{1,0:T(8,128)S(1)} %join.9), channel_id=1, source_target_pairs={{0,1},{1,0},{2,3},{3,2},{4,5},{5,4},{6,7},{7,6},{8,9},{9,8},{10,11... | collective-permute-start | bytes 393224 | tf_op jit(solution)/shard_map/ppermute | solution.py:431
  43.9 1.3 %collective-permute-start.12 = (f32[16,256]{1,0:T(8,128)S(1)}, f32[16,256]{1,0:T(8,128)S(1)}, u32[]{:S(2)}, u32[]{:S(2)}) collective-permute-start(f32[16,256]{1,0:T(8,128)S(1)} %get-tuple-element.60.refs_2_), channel_id=1, source_target_pairs={{0,128},{8,136},{16,144},{24,152},{32,160},{40,168},{48,176},{56,1... | collective-permute-start | bytes 49160 | tf_op jit(solution)/shard_map/ppermute | solution.py:508
  45.2 1.1 %time.4.force.refs_1_ = f32[16,512]{1,0:T(8,128)S(1)} custom-call(s32[3]{0:T(128)S(4)} %get-tuple-element.34.refs_2_.place, f32[32,512]{1,0:T(8,128)S(1)} %join.8.refs_8_.a.near, f32[32,512]{1,0:T(8,128)S(1)} %collective-permute-done.8.b.opposite, f32[64,512]{1,0:T(8,128)S(1)} %collective-permute-done.11.across, bf16[2,512,192]{2,1,0:T(8,128)(2,1)S(1)} %copy-done.3, ...), custom_call_target="tpu_custom_call" | custom-call | flops 10000000 | bytes 30000 | tf_op jit(solution)/shard_map/time/pallas_call | solution.py:510
  46.4 0.8 %update.3 = (bf16[32,16,128]{2,1,0:T(8,128)(2,1)S(1)}, bf16[8,16,128]{2,1,0:T(8,128)(2,1)S(1)}, bf16[8,16,128]{2,1,0:T(8,128)(2,1)S(1)}, f32[16,4096]{1,0:T(8,128)S(1)}) custom-call(s32[3]{0:T(128)S(4)} %get-tuple-element.34.refs_2_.place, f32[16,512]{1,0:T(8,128)S(1)} %time.4.force.refs_1_, ...), custom_call_target="tpu_custom_call" | custom-call | flops 10000000 | bytes 30000 | tf_op jit(solution)/shard_map/update/pallas_call | solution.py:535
  47.1 0.9 %collective-permute-done.12.refs_3_ = f32[16,256]{1,0:T(8,128)S(1)} collective-permute-done((f32[16,256]{1,0:T(8,128)S(1)}, f32[16,256]{1,0:T(8,128)S(1)}, u32[]{:S(2)}, u32[]{:S(2)}) %collective-permute-start.12) | collective-permute-done | bytes 16416 | tf_op jit(solution)/shard_map/ppermute | solution.py:508
  48.2 1.2 %collective-permute-start.13 = (f32[16,256]{1,0:T(8,128)S(1)}, f32[16,256]{1,0:T(8,128)S(1)}, u32[]{:S(2)}, u32[]{:S(2)}) collective-permute-start(f32[16,256]{1,0:T(8,128)S(1)} %relative.5.a), channel_id=1, source_target_pairs={{0,2},{1,3},{2,0},{3,1},{4,6},{5,7},{6,4},{7,5},{8,10},{9,11},{10,... | collective-permute-start | bytes 49160 | tf_op jit(solution)/shard_map/ppermute | solution.py:431
  49.3 0.8 %collective-permute-start.15 = (bf16[8,16,128]{2,1,0:T(8,128)(2,1)S(1)}, bf16[8,16,128]{2,1,0:T(8,128)(2,1)S(1)}, u32[]{:S(2)}, u32[]{:S(2)}) collective-permute-start(bf16[8,16,128]{2,1,0:T(8,128)(2,1)S(1)} %get-tuple-element.64), channel_id=1, source_target_pairs={{0,8},{8,0},{16,24},{24,16},{32,40},{40,32},{48,56},{56,48},{64,72... | collective-permute-start | bytes 98312 | tf_op jit(solution)/shard_map/ppermute | solution.py:448
  50.1 2.3 %collective-permute-start.16 = (bf16[8,16,128]{2,1,0:T(8,128)(2,1)S(1)}, bf16[8,16,128]{2,1,0:T(8,128)(2,1)S(1)}, u32[]{:S(2)}, u32[]{:S(2)}) collective-permute-start(bf16[8,16,128]{2,1,0:T(8,128)(2,1)S(1)} %get-tuple-element.65), channel_id=1, source_target_pairs={{0,248},{8,16},{16,8},{24,32},{32,24},{40,48},{48,40},{56,64},{64,... | collective-permute-start | bytes 98312 | tf_op jit(solution)/shard_map/ppermute | solution.py:449
  52.4 1.7 %collective-permute-start.14 = (f32[32,256]{1,0:T(8,128)S(1)}, f32[32,256]{1,0:T(8,128)S(1)}, u32[]{:S(2)}, u32[]{:S(2)}) collective-permute-start(f32[32,256]{1,0:T(8,128)S(1)} %join.10.refs_9_.a.near), channel_id=1, source_target_pairs={{0,6},{1,7},{2,4},{3,5},{4,2},{5,3},{6,0},{7,1},{8,14},{9,15},{10,... | collective-permute-start | bytes 98312 | tf_op jit(solution)/shard_map/ppermute | solution.py:431
  54.1 1.2 %inside.5.rest_0_.lin_a = f32[16,2048]{1,0:T(8,128)S(1)} custom-call(s32[8,32]{1,0:T(8,128)S(4)} %get-tuple-element.40.refs_0_, f32[1]{0:T(128)S(6)} %copy.15.freq.refs_1_, s32[3]{0:T(128)S(4)} %get-tuple-element.34.refs_2_.place, bf16[32,16,128]{2,1,0:T(8,128)(2,1)S(1)} %get-tuple-element.61.refs_4_.refs_3_, ...), custom_call_target="tpu_custom_call" | custom-call | flops 1500000000 | bytes 4500000 | tf_op jit(solution)/shard_map/inside/pallas_call | solution.py:460
  55.3 0.9 %collective-permute-done.16.refs_5_ = bf16[8,16,128]{2,1,0:T(8,128)(2,1)S(1)} collective-permute-done((bf16[8,16,128]{2,1,0:T(8,128)(2,1)S(1)}, bf16[8,16,128]{2,1,0:T(8,128)(2,1)S(1)}, u32[]{:S(2)}, u32[]{:S(2)}) %collective-permute-start.16) | collective-permute-done | bytes 32800 | tf_op jit(solution)/shard_map/ppermute | solution.py:449
  56.2 1.2 %edges.5.rest_1_.lin_b = f32[16,2048]{1,0:T(8,128)S(1)} custom-call(s32[8,32]{1,0:T(8,128)S(4)} %get-tuple-element.40.refs_0_, f32[1]{0:T(128)S(6)} %copy.15.freq.refs_1_, s32[3]{0:T(128)S(4)} %get-tuple-element.34.refs_2_.place, bf16[32,16,128]{2,1,0:T(8,128)(2,1)S(1)} %get-tuple-element.61.refs_4_.refs_3_, ...), custom_call_target="tpu_custom_call" | custom-call | flops 1500000000 | bytes 4500000 | tf_op jit(solution)/shard_map/edges/pallas_call | solution.py:460
  57.4 3.0 %collective-permute-start.17 = (f32[64,256]{1,0:T(8,128)S(1)}, f32[64,256]{1,0:T(8,128)S(1)}, u32[]{:S(2)}, u32[]{:S(2)}) collective-permute-start(f32[64,256]{1,0:T(8,128)S(1)} %join.11), channel_id=1, source_target_pairs={{0,1},{1,0},{2,3},{3,2},{4,5},{5,4},{6,7},{7,6},{8,9},{9,8},{10,11... | collective-permute-start | bytes 196616 | tf_op jit(solution)/shard_map/ppermute | solution.py:431
  60.5 0.9 %collective-permute-done.17.across = f32[64,256]{1,0:T(8,128)S(1)} collective-permute-done((f32[64,256]{1,0:T(8,128)S(1)}, f32[64,256]{1,0:T(8,128)S(1)}, u32[]{:S(2)}, u32[]{:S(2)}) %collective-permute-start.17) | collective-permute-done | bytes 65568 | tf_op jit(solution)/shard_map/ppermute | solution.py:431
  62.0 1.5 %finish.1 = (f32[16,4096]{1,0:T(8,128)}, f32[16,4096]{1,0:T(8,128)}) custom-call(f32[16,256]{1,0:T(8,128)S(1)} %time.5.force, bf16[4096,256]{1,0:T(8,128)(2,1)S(1)} %get-tuple-element.44.refs_7_.refs_9_.hot.refs_6_.refs_8_, f32[16,2048]{1,0:T(8,128)S(1)} %inside.5.rest_0_.lin_a, f32[16,2048]{1,0:T(8,128)S(1)} %edges.5.rest_1_.lin_b, ...), custom_call_target="tpu_custom_call" | custom-call | tf_op jit(solution)/shard_map/finish/pallas_call | solution.py:521
  (35 shorter events, 1.8 us)
Async XLA Ops:
  2.0 15.6 %copy-start = (bf16[32,8,128,128]{3,2,1,0:T(8,128)(2,1)S(1)}, bf16[32,8,128,128]{3,2,1,0:T(8,128)(2,1)}, u32[]{:S(2)}) copy-start(bf16[32,8,128,128]{3,2,1,0:T(8,128)(2,1)} %refs_6_.2) | copy-start | bytes 25165828
  2.0 15.6 %copy-start.1 = (bf16[32,8,128,128]{3,2,1,0:T(8,128)(2,1)S(1)}, bf16[32,8,128,128]{3,2,1,0:T(8,128)(2,1)}, u32[]{:S(2)}) copy-start(bf16[32,8,128,128]{3,2,1,0:T(8,128)(2,1)} %refs_7_.2) | copy-start | bytes 25165828
  2.0 15.6 %copy-start.2 = (f32[16,4096]{1,0:T(8,128)S(1)}, f32[16,4096]{1,0:T(8,128)}, u32[]{:S(2)}) copy-start(f32[16,4096]{1,0:T(8,128)} %refs_7_.4) | copy-start | bytes 786436
  5.5 10.6 %collective-permute-start = (f32[48,256]{1,0:T(8,128)S(1)}, f32[48,256]{1,0:T(8,128)S(1)}, u32[]{:S(2)}, u32[]{:S(2)}) collective-permute-start(f32[48,256]{1,0:T(8,128)S(1)} %get-tuple-element.35.mine), channel_id=1, source_target_pairs={{0,128},{8,136},{16,144},{24,152},{32,160},{40,168},{48,176},{56,1... | collective-permute-start | bytes 147464 | tf_op jit(solution)/shard_map/ppermute | solution.py:433
  9.4 6.8 %collective-permute-start.1 = (bf16[8,16,128]{2,1,0:T(8,128)(2,1)S(1)}, bf16[8,16,128]{2,1,0:T(8,128)(2,1)S(1)}, u32[]{:S(2)}, u32[]{:S(2)}) collective-permute-start(bf16[8,16,128]{2,1,0:T(8,128)(2,1)S(1)} %get-tuple-element.37), channel_id=1, source_target_pairs={{0,8},{8,0},{16,24},{24,16},{32,40},{40,32},{48,56},{56,48},{64,72... | collective-permute-start | bytes 98312 | tf_op jit(solution)/shard_map/ppermute | solution.py:448
  11.0 11.9 %collective-permute-start.4 = (bf16[8,16,128]{2,1,0:T(8,128)(2,1)S(1)}, bf16[8,16,128]{2,1,0:T(8,128)(2,1)S(1)}, u32[]{:S(2)}, u32[]{:S(2)}) collective-permute-start(bf16[8,16,128]{2,1,0:T(8,128)(2,1)S(1)} %get-tuple-element.47), channel_id=1, source_target_pairs={{0,248},{8,16},{16,8},{24,32},{32,24},{40,48},{48,40},{56,64},{64,... | collective-permute-start | bytes 98312 | tf_op jit(solution)/shard_map/ppermute | solution.py:449
  16.3 4.7 %collective-permute-start.2 = (f32[16,512]{1,0:T(8,128)S(1)}, f32[16,512]{1,0:T(8,128)S(1)}, u32[]{:S(2)}, u32[]{:S(2)}) collective-permute-start(f32[16,512]{1,0:T(8,128)S(1)} %get-tuple-element.39.a), channel_id=1, source_target_pairs={{0,2},{1,3},{2,0},{3,1},{4,6},{5,7},{6,4},{7,5},{8,10},{9,11},{10,... | collective-permute-start | bytes 98312 | tf_op jit(solution)/shard_map/ppermute | solution.py:431
  21.0 5.4 %collective-permute-start.3 = (f32[32,512]{1,0:T(8,128)S(1)}, f32[32,512]{1,0:T(8,128)S(1)}, u32[]{:S(2)}, u32[]{:S(2)}) collective-permute-start(f32[32,512]{1,0:T(8,128)S(1)} %join.6.refs_12_.a.near), channel_id=1, source_target_pairs={{0,6},{1,7},{2,4},{3,5},{4,2},{5,3},{6,0},{7,1},{8,14},{9,15},{10,... | collective-permute-start | bytes 196616 | tf_op jit(solution)/shard_map/ppermute | solution.py:431
  22.9 7.1 %copy-start.3 = (bf16[2,512,192]{2,1,0:T(8,128)(2,1)S(1)}, bf16[2,512,192]{2,1,0:T(8,128)(2,1)}, u32[]{:S(2)}) copy-start(bf16[2,512,192]{2,1,0:T(8,128)(2,1)} %constant.15.clone.forward) | copy-start | bytes 1179652
  26.5 3.6 %collective-permute-start.5 = (f32[64,512]{1,0:T(8,128)S(1)}, f32[64,512]{1,0:T(8,128)S(1)}, u32[]{:S(2)}, u32[]{:S(2)}) collective-permute-start(f32[64,512]{1,0:T(8,128)S(1)} %join.7), channel_id=1, source_target_pairs={{0,1},{1,0},{2,3},{3,2},{4,5},{5,4},{6,7},{7,6},{8,9},{9,8},{10,11... | collective-permute-start | bytes 393224 | tf_op jit(solution)/shard_map/ppermute | solution.py:431
  28.6 4.1 %collective-permute-start.6 = (f32[16,256]{1,0:T(8,128)S(1)}, f32[16,256]{1,0:T(8,128)S(1)}, u32[]{:S(2)}, u32[]{:S(2)}) collective-permute-start(f32[16,256]{1,0:T(8,128)S(1)} %get-tuple-element.51.refs_2_), channel_id=1, source_target_pairs={{0,128},{8,136},{16,144},{24,152},{32,160},{40,168},{48,176},{56,1... | collective-permute-start | bytes 49160 | tf_op jit(solution)/shard_map/ppermute | solution.py:508
  32.9 3.6 %collective-permute-start.7 = (f32[16,512]{1,0:T(8,128)S(1)}, f32[16,512]{1,0:T(8,128)S(1)}, u32[]{:S(2)}, u32[]{:S(2)}) collective-permute-start(f32[16,512]{1,0:T(8,128)S(1)} %relative.4.a), channel_id=1, source_target_pairs={{0,2},{1,3},{2,0},{3,1},{4,6},{5,7},{6,4},{7,5},{8,10},{9,11},{10,... | collective-permute-start | bytes 98312 | tf_op jit(solution)/shard_map/ppermute | solution.py:431
  33.4 6.1 %collective-permute-start.10 = (bf16[8,16,128]{2,1,0:T(8,128)(2,1)S(1)}, bf16[8,16,128]{2,1,0:T(8,128)(2,1)S(1)}, u32[]{:S(2)}, u32[]{:S(2)}) collective-permute-start(bf16[8,16,128]{2,1,0:T(8,128)(2,1)S(1)} %get-tuple-element.56), channel_id=1, source_target_pairs={{0,248},{8,16},{16,8},{24,32},{32,24},{40,48},{48,40},{56,64},{64,... | collective-permute-start | bytes 98312 | tf_op jit(solution)/shard_map/ppermute | solution.py:449
  36.4 3.1 %collective-permute-start.9 = (bf16[8,16,128]{2,1,0:T(8,128)(2,1)S(1)}, bf16[8,16,128]{2,1,0:T(8,128)(2,1)S(1)}, u32[]{:S(2)}, u32[]{:S(2)}) collective-permute-start(bf16[8,16,128]{2,1,0:T(8,128)(2,1)S(1)} %get-tuple-element.55), channel_id=1, source_target_pairs={{0,8},{8,0},{16,24},{24,16},{32,40},{40,32},{48,56},{56,48},{64,72... | collective-permute-start | bytes 98312 | tf_op jit(solution)/shard_map/ppermute | solution.py:448
  36.5 4.7 %collective-permute-start.8 = (f32[32,512]{1,0:T(8,128)S(1)}, f32[32,512]{1,0:T(8,128)S(1)}, u32[]{:S(2)}, u32[]{:S(2)}) collective-permute-start(f32[32,512]{1,0:T(8,128)S(1)} %join.8.refs_8_.a.near), channel_id=1, source_target_pairs={{0,6},{1,7},{2,4},{3,5},{4,2},{5,3},{6,0},{7,1},{8,14},{9,15},{10,... | collective-permute-start | bytes 196616 | tf_op jit(solution)/shard_map/ppermute | solution.py:431
  41.2 4.0 %collective-permute-start.11 = (f32[64,512]{1,0:T(8,128)S(1)}, f32[64,512]{1,0:T(8,128)S(1)}, u32[]{:S(2)}, u32[]{:S(2)}) collective-permute-start(f32[64,512]{1,0:T(8,128)S(1)} %join.9), channel_id=1, source_target_pairs={{0,1},{1,0},{2,3},{3,2},{4,5},{5,4},{6,7},{7,6},{8,9},{9,8},{10,11... | collective-permute-start | bytes 393224 | tf_op jit(solution)/shard_map/ppermute | solution.py:431
  43.9 4.1 %collective-permute-start.12 = (f32[16,256]{1,0:T(8,128)S(1)}, f32[16,256]{1,0:T(8,128)S(1)}, u32[]{:S(2)}, u32[]{:S(2)}) collective-permute-start(f32[16,256]{1,0:T(8,128)S(1)} %get-tuple-element.60.refs_2_), channel_id=1, source_target_pairs={{0,128},{8,136},{16,144},{24,152},{32,160},{40,168},{48,176},{56,1... | collective-permute-start | bytes 49160 | tf_op jit(solution)/shard_map/ppermute | solution.py:508
  48.2 4.2 %collective-permute-start.13 = (f32[16,256]{1,0:T(8,128)S(1)}, f32[16,256]{1,0:T(8,128)S(1)}, u32[]{:S(2)}, u32[]{:S(2)}) collective-permute-start(f32[16,256]{1,0:T(8,128)S(1)} %relative.5.a), channel_id=1, source_target_pairs={{0,2},{1,3},{2,0},{3,1},{4,6},{5,7},{6,4},{7,5},{8,10},{9,11},{10,... | collective-permute-start | bytes 49160 | tf_op jit(solution)/shard_map/ppermute | solution.py:431
  49.3 5.9 %collective-permute-start.15 = (bf16[8,16,128]{2,1,0:T(8,128)(2,1)S(1)}, bf16[8,16,128]{2,1,0:T(8,128)(2,1)S(1)}, u32[]{:S(2)}, u32[]{:S(2)}) collective-permute-start(bf16[8,16,128]{2,1,0:T(8,128)(2,1)S(1)} %get-tuple-element.64), channel_id=1, source_target_pairs={{0,8},{8,0},{16,24},{24,16},{32,40},{40,32},{48,56},{56,48},{64,72... | collective-permute-start | bytes 98312 | tf_op jit(solution)/shard_map/ppermute | solution.py:448
  50.1 6.1 %collective-permute-start.16 = (bf16[8,16,128]{2,1,0:T(8,128)(2,1)S(1)}, bf16[8,16,128]{2,1,0:T(8,128)(2,1)S(1)}, u32[]{:S(2)}, u32[]{:S(2)}) collective-permute-start(bf16[8,16,128]{2,1,0:T(8,128)(2,1)S(1)} %get-tuple-element.65), channel_id=1, source_target_pairs={{0,248},{8,16},{16,8},{24,32},{32,24},{40,48},{48,40},{56,64},{64,... | collective-permute-start | bytes 98312 | tf_op jit(solution)/shard_map/ppermute | solution.py:449
  52.4 5.0 %collective-permute-start.14 = (f32[32,256]{1,0:T(8,128)S(1)}, f32[32,256]{1,0:T(8,128)S(1)}, u32[]{:S(2)}, u32[]{:S(2)}) collective-permute-start(f32[32,256]{1,0:T(8,128)S(1)} %join.10.refs_9_.a.near), channel_id=1, source_target_pairs={{0,6},{1,7},{2,4},{3,5},{4,2},{5,3},{6,0},{7,1},{8,14},{9,15},{10,... | collective-permute-start | bytes 98312 | tf_op jit(solution)/shard_map/ppermute | solution.py:431
  57.4 3.9 %collective-permute-start.17 = (f32[64,256]{1,0:T(8,128)S(1)}, f32[64,256]{1,0:T(8,128)S(1)}, u32[]{:S(2)}, u32[]{:S(2)}) collective-permute-start(f32[64,256]{1,0:T(8,128)S(1)} %join.11), channel_id=1, source_target_pairs={{0,1},{1,0},{2,3},{3,2},{4,5},{5,4},{6,7},{7,6},{8,9},{9,8},{10,11... | collective-permute-start | bytes 196616 | tf_op jit(solution)/shard_map/ppermute | solution.py:431

commit v6 on v5

--- a/solution.py
+++ b/solution.py
@@ -501,7 +501,7 @@
             outside = product(True, inside[1:])
         added = outside
         opposite = flipped(near, 6)
-        across_core = flipped(join(near, opposite, inside[0], outside[0]), 1)
+        across_core = flipped(join(near, opposite, inside[0], *([] if final else outside[:1])), 1)
         lins = [inside[0], outside[0]]
         if not final:
             near_lin = added[1]

time: 63.8 us -> 63 us (0.987)
  waiting for transfers between devices: 3.57 us -> 2.84 us
    ppermute x3, waiting for transfers between devices: 0.93 us -> 0.01 us  [local(): odd_in = lax.ppermute(odd, 'comp', odds)]
  transfers between devices with their start and end apart: 18 -> 18, of which waited for: 4 -> 3; matrix products, arithmetic and copies ran while one was open for 0% -> 0% of each run, Pallas kernels for 26% -> 26%
where the time goes in v6:
time: 63 us; the launch traced here: 62.9 us
  starting transfers between devices  35.4 us (56%)
  Pallas kernels  22.4 us (36%)
  waiting for transfers between devices  2.84 us (5%)
  between operations  2.16 us (3%)
    ppermute x9, starting transfers between devices, flipped(): return lax.ppermute(x, 'harm', [(i, i ^ bits) for i in range(devices)])  15.9 us
    pallas_call x6, Pallas kernels, product(): pl.pallas_call(functools.partial(product_kernel, edges=edges, first=first...  12.4 us
    ppermute x3, starting transfers between devices, local(): odd_in = lax.ppermute(odd, 'comp', odds)  10.5 us
    ppermute x1, starting transfers between devices, local(): far = lax.ppermute(mine, 'comp', facing)  3.83 us
    pallas_call x1, Pallas kernels, local(): pl.pallas_call(init_kernel, out_shape=(shape(BLOCKED, BF16), shape(EDGE,...  3.52 us
    pallas_call x3, Pallas kernels, local(): pl.pallas_call(functools.partial(time_kernel, final=final), out_shape=sha...  2.93 us
    ppermute x2, starting transfers between devices, local(): far_lin = lax.ppermute(near_lin, 'comp', facing)  2.75 us
    ppermute x3, starting transfers between devices, local(): even_in = lax.ppermute(even, 'comp', evens)  2.43 us
  transfers between devices with their start and end apart: 18, of which 3 were waited for; matrix products, arithmetic and copies ran while one was open for 0% of the time, Pallas kernels for 26%

profile of v6, /device:TPU:1, one launch (start us, length us, event | category | flops | bytes accessed | tf_op | source)
XLA Modules:
  0.0 62.9 jit_solution(18251400995425929569)
XLA Ops:
  2.0 3.5 %init.1 = (bf16[32,16,128]{2,1,0:T(8,128)(2,1)S(1)}, bf16[8,16,128]{2,1,0:T(8,128)(2,1)S(1)}, bf16[8,16,128]{2,1,0:T(8,128)(2,1)S(1)}, f32[16,4096]{1,0:T(8,128)...) custom-call(f32[1]{0:T(128)S(6)} %copy.15.freq.refs_1_, ...), custom_call_target="tpu_custom_call" | custom-call | flops 3000000000 | bytes 9000000 | tf_op jit(solution)/shard_map/init/pallas_call | solution.py:392
  5.5 3.8 %collective-permute-start = (f32[48,256]{1,0:T(8,128)S(1)}, f32[48,256]{1,0:T(8,128)S(1)}, u32[]{:S(2)}, u32[]{:S(2)}) collective-permute-start(f32[48,256]{1,0:T(8,128)S(1)} %get-tuple-element.35.mine), channel_id=1, source_target_pairs={{0,128},{8,136},{16,144},{24,152},{32,160},{40,168},{48,176},{56,1... | collective-permute-start | bytes 147464 | tf_op jit(solution)/shard_map/ppermute | solution.py:433
  9.4 1.6 %collective-permute-start.1 = (bf16[8,16,128]{2,1,0:T(8,128)(2,1)S(1)}, bf16[8,16,128]{2,1,0:T(8,128)(2,1)S(1)}, u32[]{:S(2)}, u32[]{:S(2)}) collective-permute-start(bf16[8,16,128]{2,1,0:T(8,128)(2,1)S(1)} %get-tuple-element.37), channel_id=1, source_target_pairs={{0,8},{8,0},{16,24},{24,16},{32,40},{40,32},{48,56},{56,48},{64,72... | collective-permute-start | bytes 98312 | tf_op jit(solution)/shard_map/ppermute | solution.py:448
  11.0 5.2 %collective-permute-start.4 = (bf16[8,16,128]{2,1,0:T(8,128)(2,1)S(1)}, bf16[8,16,128]{2,1,0:T(8,128)(2,1)S(1)}, u32[]{:S(2)}, u32[]{:S(2)}) collective-permute-start(bf16[8,16,128]{2,1,0:T(8,128)(2,1)S(1)} %get-tuple-element.47), channel_id=1, source_target_pairs={{0,248},{8,16},{16,8},{24,32},{32,24},{40,48},{48,40},{56,64},{64,... | collective-permute-start | bytes 98312 | tf_op jit(solution)/shard_map/ppermute | solution.py:449
  16.3 1.3 %collective-permute-start.2 = (f32[16,512]{1,0:T(8,128)S(1)}, f32[16,512]{1,0:T(8,128)S(1)}, u32[]{:S(2)}, u32[]{:S(2)}) collective-permute-start(f32[16,512]{1,0:T(8,128)S(1)} %get-tuple-element.39.a), channel_id=1, source_target_pairs={{0,2},{1,3},{2,0},{3,1},{4,6},{5,7},{6,4},{7,5},{8,10},{9,11},{10,... | collective-permute-start | bytes 98312 | tf_op jit(solution)/shard_map/ppermute | solution.py:431
  17.6 3.4 %inside.3 = (f32[16,2048]{1,0:T(8,128)S(1)}, f32[16,256]{1,0:T(8,128)S(1)}, bf16[16,1024,256]{2,1,0:T(8,128)(2,1)S(1)}) custom-call(s32[8,32]{1,0:T(8,128)S(4)} %get-tuple-element.40.refs_0_, f32[1]{0:T(128)S(6)} %copy.15.freq.refs_1_, s32[3]{0:T(128)S(4)} %get-tuple-element.34.refs_2_.place, bf16[32,16,128]{2,1,0:T(8,128)(2,1)S(1)} %get-tuple-element.41.refs_3_, ...), custom_call_target="tpu_custom_call" | custom-call | flops 3000000000 | bytes 9000000 | tf_op jit(solution)/shard_map/inside/pallas_call | solution.py:460
  21.0 1.9 %collective-permute-start.3 = (f32[32,512]{1,0:T(8,128)S(1)}, f32[32,512]{1,0:T(8,128)S(1)}, u32[]{:S(2)}, u32[]{:S(2)}) collective-permute-start(f32[32,512]{1,0:T(8,128)S(1)} %join.6.refs_12_.a.near), channel_id=1, source_target_pairs={{0,6},{1,7},{2,4},{3,5},{4,2},{5,3},{6,0},{7,1},{8,14},{9,15},{10,... | collective-permute-start | bytes 196616 | tf_op jit(solution)/shard_map/ppermute | solution.py:431
  22.9 3.5 %edges.3 = (f32[16,2048]{1,0:T(8,128)S(1)}, f32[16,256]{1,0:T(8,128)S(1)}, bf16[16,1024,256]{2,1,0:T(8,128)(2,1)S(1)}) custom-call(s32[8,32]{1,0:T(8,128)S(4)} %get-tuple-element.40.refs_0_, f32[1]{0:T(128)S(6)} %copy.15.freq.refs_1_, s32[3]{0:T(128)S(4)} %get-tuple-element.34.refs_2_.place, bf16[32,16,128]{2,1,0:T(8,128)(2,1)S(1)} %get-tuple-element.41.refs_3_, ...), custom_call_target="tpu_custom_call" | custom-call | flops 3000000000 | bytes 9000000 | tf_op jit(solution)/shard_map/edges/pallas_call | solution.py:460
  26.5 2.2 %collective-permute-start.5 = (f32[64,512]{1,0:T(8,128)S(1)}, f32[64,512]{1,0:T(8,128)S(1)}, u32[]{:S(2)}, u32[]{:S(2)}) collective-permute-start(f32[64,512]{1,0:T(8,128)S(1)} %join.7), channel_id=1, source_target_pairs={{0,1},{1,0},{2,3},{3,2},{4,5},{5,4},{6,7},{7,6},{8,9},{9,8},{10,11... | collective-permute-start | bytes 393224 | tf_op jit(solution)/shard_map/ppermute | solution.py:431
  28.6 1.4 %collective-permute-start.6 = (f32[16,256]{1,0:T(8,128)S(1)}, f32[16,256]{1,0:T(8,128)S(1)}, u32[]{:S(2)}, u32[]{:S(2)}) collective-permute-start(f32[16,256]{1,0:T(8,128)S(1)} %get-tuple-element.51.refs_2_), channel_id=1, source_target_pairs={{0,128},{8,136},{16,144},{24,152},{32,160},{40,168},{48,176},{56,1... | collective-permute-start | bytes 49160 | tf_op jit(solution)/shard_map/ppermute | solution.py:508
  30.1 1.1 %time.3.force.refs_1_ = f32[16,512]{1,0:T(8,128)S(1)} custom-call(s32[3]{0:T(128)S(4)} %get-tuple-element.34.refs_2_.place, f32[32,512]{1,0:T(8,128)S(1)} %join.6.refs_12_.a.near, f32[32,512]{1,0:T(8,128)S(1)} %collective-permute-done.3.b.opposite, f32[64,512]{1,0:T(8,128)S(1)} %collective-permute-done.5.across, bf16[2,512,192]{2,1,0:T(8,128)(2,1)S(1)} %copy-done.3, ...), custom_call_target="tpu_custom_call" | custom-call | flops 10000000 | bytes 30000 | tf_op jit(solution)/shard_map/time/pallas_call | solution.py:510
  31.2 0.8 %update.2 = (bf16[32,16,128]{2,1,0:T(8,128)(2,1)S(1)}, bf16[8,16,128]{2,1,0:T(8,128)(2,1)S(1)}, bf16[8,16,128]{2,1,0:T(8,128)(2,1)S(1)}) custom-call(s32[3]{0:T(128)S(4)} %get-tuple-element.34.refs_2_.place, f32[16,512]{1,0:T(8,128)S(1)} %time.3.force.refs_1_, bf16[4096,256]{1,0:T(8,128)(2,1)S(1)} %get-tuple-element.44.refs_7_.refs_9_.hot.refs_6_.refs_8_, ...), custom_call_target="tpu_custom_call" | custom-call | flops 10000000 | bytes 30000 | tf_op jit(solution)/shard_map/update/pallas_call | solution.py:535
  32.0 0.8 %collective-permute-done.6.refs_3_ = f32[16,256]{1,0:T(8,128)S(1)} collective-permute-done((f32[16,256]{1,0:T(8,128)S(1)}, f32[16,256]{1,0:T(8,128)S(1)}, u32[]{:S(2)}, u32[]{:S(2)}) %collective-permute-start.6) | collective-permute-done | bytes 16416 | tf_op jit(solution)/shard_map/ppermute | solution.py:508
  33.4 3.1 %collective-permute-start.10 = (bf16[8,16,128]{2,1,0:T(8,128)(2,1)S(1)}, bf16[8,16,128]{2,1,0:T(8,128)(2,1)S(1)}, u32[]{:S(2)}, u32[]{:S(2)}) collective-permute-start(bf16[8,16,128]{2,1,0:T(8,128)(2,1)S(1)} %get-tuple-element.56), channel_id=1, source_target_pairs={{0,248},{8,16},{16,8},{24,32},{32,24},{40,48},{48,40},{56,64},{64,... | collective-permute-start | bytes 98312 | tf_op jit(solution)/shard_map/ppermute | solution.py:449
  36.5 1.5 %collective-permute-start.8 = (f32[32,512]{1,0:T(8,128)S(1)}, f32[32,512]{1,0:T(8,128)S(1)}, u32[]{:S(2)}, u32[]{:S(2)}) collective-permute-start(f32[32,512]{1,0:T(8,128)S(1)} %join.8.refs_8_.a.near), channel_id=1, source_target_pairs={{0,6},{1,7},{2,4},{3,5},{4,2},{5,3},{6,0},{7,1},{8,14},{9,15},{10,... | collective-permute-start | bytes 196616 | tf_op jit(solution)/shard_map/ppermute | solution.py:431
  38.0 1.5 %inside.4 = (f32[16,2048]{1,0:T(8,128)S(1)}, f32[16,256]{1,0:T(8,128)S(1)}) custom-call(s32[8,32]{1,0:T(8,128)S(4)} %get-tuple-element.40.refs_0_, f32[1]{0:T(128)S(6)} %copy.15.freq.refs_1_, s32[3]{0:T(128)S(4)} %get-tuple-element.34.refs_2_.place, bf16[32,16,128]{2,1,0:T(8,128)(2,1)S(1)} %get-tuple-element.52.refs_4_.refs_3_, ...), custom_call_target="tpu_custom_call" | custom-call | flops 1500000000 | bytes 4500000 | tf_op jit(solution)/shard_map/inside/pallas_call | solution.py:460
  39.5 1.6 %edges.4 = (f32[16,2048]{1,0:T(8,128)S(1)}, f32[16,256]{1,0:T(8,128)S(1)}) custom-call(s32[8,32]{1,0:T(8,128)S(4)} %get-tuple-element.40.refs_0_, f32[1]{0:T(128)S(6)} %copy.15.freq.refs_1_, s32[3]{0:T(128)S(4)} %get-tuple-element.34.refs_2_.place, bf16[32,16,128]{2,1,0:T(8,128)(2,1)S(1)} %get-tuple-element.52.refs_4_.refs_3_, ...), custom_call_target="tpu_custom_call" | custom-call | flops 1500000000 | bytes 4500000 | tf_op jit(solution)/shard_map/edges/pallas_call | solution.py:460
  41.2 2.7 %collective-permute-start.11 = (f32[64,512]{1,0:T(8,128)S(1)}, f32[64,512]{1,0:T(8,128)S(1)}, u32[]{:S(2)}, u32[]{:S(2)}) collective-permute-start(f32[64,512]{1,0:T(8,128)S(1)} %join.9), channel_id=1, source_target_pairs={{0,1},{1,0},{2,3},{3,2},{4,5},{5,4},{6,7},{7,6},{8,9},{9,8},{10,11... | collective-permute-start | bytes 393224 | tf_op jit(solution)/shard_map/ppermute | solution.py:431
  43.9 1.3 %collective-permute-start.12 = (f32[16,256]{1,0:T(8,128)S(1)}, f32[16,256]{1,0:T(8,128)S(1)}, u32[]{:S(2)}, u32[]{:S(2)}) collective-permute-start(f32[16,256]{1,0:T(8,128)S(1)} %get-tuple-element.60.refs_2_), channel_id=1, source_target_pairs={{0,128},{8,136},{16,144},{24,152},{32,160},{40,168},{48,176},{56,1... | collective-permute-start | bytes 49160 | tf_op jit(solution)/shard_map/ppermute | solution.py:508
  45.2 1.1 %time.4.force.refs_1_ = f32[16,512]{1,0:T(8,128)S(1)} custom-call(s32[3]{0:T(128)S(4)} %get-tuple-element.34.refs_2_.place, f32[32,512]{1,0:T(8,128)S(1)} %join.8.refs_8_.a.near, f32[32,512]{1,0:T(8,128)S(1)} %collective-permute-done.8.b.opposite, f32[64,512]{1,0:T(8,128)S(1)} %collective-permute-done.11.across, bf16[2,512,192]{2,1,0:T(8,128)(2,1)S(1)} %copy-done.3, ...), custom_call_target="tpu_custom_call" | custom-call | flops 10000000 | bytes 30000 | tf_op jit(solution)/shard_map/time/pallas_call | solution.py:510
  46.4 0.8 %update.3 = (bf16[32,16,128]{2,1,0:T(8,128)(2,1)S(1)}, bf16[8,16,128]{2,1,0:T(8,128)(2,1)S(1)}, bf16[8,16,128]{2,1,0:T(8,128)(2,1)S(1)}, f32[16,4096]{1,0:T(8,128)S(1)}) custom-call(s32[3]{0:T(128)S(4)} %get-tuple-element.34.refs_2_.place, f32[16,512]{1,0:T(8,128)S(1)} %time.4.force.refs_1_, ...), custom_call_target="tpu_custom_call" | custom-call | flops 10000000 | bytes 30000 | tf_op jit(solution)/shard_map/update/pallas_call | solution.py:535
  47.1 0.9 %collective-permute-done.12.refs_3_ = f32[16,256]{1,0:T(8,128)S(1)} collective-permute-done((f32[16,256]{1,0:T(8,128)S(1)}, f32[16,256]{1,0:T(8,128)S(1)}, u32[]{:S(2)}, u32[]{:S(2)}) %collective-permute-start.12) | collective-permute-done | bytes 16416 | tf_op jit(solution)/shard_map/ppermute | solution.py:508
  48.2 1.2 %collective-permute-start.13 = (f32[16,256]{1,0:T(8,128)S(1)}, f32[16,256]{1,0:T(8,128)S(1)}, u32[]{:S(2)}, u32[]{:S(2)}) collective-permute-start(f32[16,256]{1,0:T(8,128)S(1)} %relative.5.a), channel_id=1, source_target_pairs={{0,2},{1,3},{2,0},{3,1},{4,6},{5,7},{6,4},{7,5},{8,10},{9,11},{10,... | collective-permute-start | bytes 49160 | tf_op jit(solution)/shard_map/ppermute | solution.py:431
  49.3 0.8 %collective-permute-start.16 = (bf16[8,16,128]{2,1,0:T(8,128)(2,1)S(1)}, bf16[8,16,128]{2,1,0:T(8,128)(2,1)S(1)}, u32[]{:S(2)}, u32[]{:S(2)}) collective-permute-start(bf16[8,16,128]{2,1,0:T(8,128)(2,1)S(1)} %get-tuple-element.64), channel_id=1, source_target_pairs={{0,8},{8,0},{16,24},{24,16},{32,40},{40,32},{48,56},{56,48},{64,72... | collective-permute-start | bytes 98312 | tf_op jit(solution)/shard_map/ppermute | solution.py:448
  50.1 2.3 %collective-permute-start.17 = (bf16[8,16,128]{2,1,0:T(8,128)(2,1)S(1)}, bf16[8,16,128]{2,1,0:T(8,128)(2,1)S(1)}, u32[]{:S(2)}, u32[]{:S(2)}) collective-permute-start(bf16[8,16,128]{2,1,0:T(8,128)(2,1)S(1)} %get-tuple-element.65), channel_id=1, source_target_pairs={{0,248},{8,16},{16,8},{24,32},{32,24},{40,48},{48,40},{56,64},{64,... | collective-permute-start | bytes 98312 | tf_op jit(solution)/shard_map/ppermute | solution.py:449
  52.4 1.7 %collective-permute-start.14 = (f32[32,256]{1,0:T(8,128)S(1)}, f32[32,256]{1,0:T(8,128)S(1)}, u32[]{:S(2)}, u32[]{:S(2)}) collective-permute-start(f32[32,256]{1,0:T(8,128)S(1)} %join.10.refs_9_.a.near), channel_id=1, source_target_pairs={{0,6},{1,7},{2,4},{3,5},{4,2},{5,3},{6,0},{7,1},{8,14},{9,15},{10,... | collective-permute-start | bytes 98312 | tf_op jit(solution)/shard_map/ppermute | solution.py:431
  54.1 1.2 %inside.5.rest_0_.lin_a = f32[16,2048]{1,0:T(8,128)S(1)} custom-call(s32[8,32]{1,0:T(8,128)S(4)} %get-tuple-element.40.refs_0_, f32[1]{0:T(128)S(6)} %copy.15.freq.refs_1_, s32[3]{0:T(128)S(4)} %get-tuple-element.34.refs_2_.place, bf16[32,16,128]{2,1,0:T(8,128)(2,1)S(1)} %get-tuple-element.61.refs_4_.refs_3_, ...), custom_call_target="tpu_custom_call" | custom-call | flops 1500000000 | bytes 4500000 | tf_op jit(solution)/shard_map/inside/pallas_call | solution.py:460
  55.3 1.1 %collective-permute-done.14.b.opposite = f32[32,256]{1,0:T(8,128)S(1)} collective-permute-done((f32[32,256]{1,0:T(8,128)S(1)}, f32[32,256]{1,0:T(8,128)S(1)}, u32[]{:S(2)}, u32[]{:S(2)}) %collective-permute-start.14) | collective-permute-done | bytes 32800 | tf_op jit(solution)/shard_map/ppermute | solution.py:431
  56.4 2.9 %collective-permute-start.15 = (f32[64,256]{1,0:T(8,128)S(1)}, f32[64,256]{1,0:T(8,128)S(1)}, u32[]{:S(2)}, u32[]{:S(2)}) collective-permute-start(f32[64,256]{1,0:T(8,128)S(1)} %join.11), channel_id=1, source_target_pairs={{0,1},{1,0},{2,3},{3,2},{4,5},{5,4},{6,7},{7,6},{8,9},{9,8},{10,11... | collective-permute-start | bytes 196616 | tf_op jit(solution)/shard_map/ppermute | solution.py:431
  59.3 1.2 %edges.5.lin_b = f32[16,2048]{1,0:T(8,128)S(1)} custom-call(s32[8,32]{1,0:T(8,128)S(4)} %get-tuple-element.40.refs_0_, f32[1]{0:T(128)S(6)} %copy.15.freq.refs_1_, s32[3]{0:T(128)S(4)} %get-tuple-element.34.refs_2_.place, bf16[32,16,128]{2,1,0:T(8,128)(2,1)S(1)} %get-tuple-element.61.refs_4_.refs_3_, ...), custom_call_target="tpu_custom_call" | custom-call | flops 1500000000 | bytes 4500000 | tf_op jit(solution)/shard_map/edges/pallas_call | solution.py:460
  60.5 0.7 %time.5.force = f32[16,256]{1,0:T(8,128)S(1)} custom-call(s32[3]{0:T(128)S(4)} %get-tuple-element.34.refs_2_.place, f32[32,256]{1,0:T(8,128)S(1)} %join.10.refs_9_.a.near, f32[32,256]{1,0:T(8,128)S(1)} %collective-permute-done.14.b.opposite, f32[64,256]{1,0:T(8,128)S(1)} %collective-permute-done.15.across, bf16[2,512,192]{2,1,0:T(8,128)(2,1)S(1)} %copy-done.3, ...), custom_call_target="tpu_custom_call" | custom-call | flops 10000000 | bytes 30000 | tf_op jit(solution)/shard_map/time/pallas_call | solution.py:510
  61.2 1.5 %finish.1 = (f32[16,4096]{1,0:T(8,128)}, f32[16,4096]{1,0:T(8,128)}) custom-call(f32[16,256]{1,0:T(8,128)S(1)} %time.5.force, bf16[4096,256]{1,0:T(8,128)(2,1)S(1)} %get-tuple-element.44.refs_7_.refs_9_.hot.refs_6_.refs_8_, f32[16,2048]{1,0:T(8,128)S(1)} %inside.5.rest_0_.lin_a, f32[16,2048]{1,0:T(8,128)S(1)} %edges.5.lin_b, ...), custom_call_target="tpu_custom_call" | custom-call | tf_op jit(solution)/shard_map/finish/pallas_call | solution.py:521
  (35 shorter events, 1.2 us)
Async XLA Ops:
  2.0 15.6 %copy-start = (bf16[32,8,128,128]{3,2,1,0:T(8,128)(2,1)S(1)}, bf16[32,8,128,128]{3,2,1,0:T(8,128)(2,1)}, u32[]{:S(2)}) copy-start(bf16[32,8,128,128]{3,2,1,0:T(8,128)(2,1)} %refs_6_.2) | copy-start | bytes 25165828
  2.0 15.6 %copy-start.1 = (bf16[32,8,128,128]{3,2,1,0:T(8,128)(2,1)S(1)}, bf16[32,8,128,128]{3,2,1,0:T(8,128)(2,1)}, u32[]{:S(2)}) copy-start(bf16[32,8,128,128]{3,2,1,0:T(8,128)(2,1)} %refs_7_.2) | copy-start | bytes 25165828
  2.0 15.6 %copy-start.2 = (f32[16,4096]{1,0:T(8,128)S(1)}, f32[16,4096]{1,0:T(8,128)}, u32[]{:S(2)}) copy-start(f32[16,4096]{1,0:T(8,128)} %refs_7_.4) | copy-start | bytes 786436
  5.5 10.6 %collective-permute-start = (f32[48,256]{1,0:T(8,128)S(1)}, f32[48,256]{1,0:T(8,128)S(1)}, u32[]{:S(2)}, u32[]{:S(2)}) collective-permute-start(f32[48,256]{1,0:T(8,128)S(1)} %get-tuple-element.35.mine), channel_id=1, source_target_pairs={{0,128},{8,136},{16,144},{24,152},{32,160},{40,168},{48,176},{56,1... | collective-permute-start | bytes 147464 | tf_op jit(solution)/shard_map/ppermute | solution.py:433
  9.4 6.8 %collective-permute-start.1 = (bf16[8,16,128]{2,1,0:T(8,128)(2,1)S(1)}, bf16[8,16,128]{2,1,0:T(8,128)(2,1)S(1)}, u32[]{:S(2)}, u32[]{:S(2)}) collective-permute-start(bf16[8,16,128]{2,1,0:T(8,128)(2,1)S(1)} %get-tuple-element.37), channel_id=1, source_target_pairs={{0,8},{8,0},{16,24},{24,16},{32,40},{40,32},{48,56},{56,48},{64,72... | collective-permute-start | bytes 98312 | tf_op jit(solution)/shard_map/ppermute | solution.py:448
  11.0 11.9 %collective-permute-start.4 = (bf16[8,16,128]{2,1,0:T(8,128)(2,1)S(1)}, bf16[8,16,128]{2,1,0:T(8,128)(2,1)S(1)}, u32[]{:S(2)}, u32[]{:S(2)}) collective-permute-start(bf16[8,16,128]{2,1,0:T(8,128)(2,1)S(1)} %get-tuple-element.47), channel_id=1, source_target_pairs={{0,248},{8,16},{16,8},{24,32},{32,24},{40,48},{48,40},{56,64},{64,... | collective-permute-start | bytes 98312 | tf_op jit(solution)/shard_map/ppermute | solution.py:449
  16.3 4.7 %collective-permute-start.2 = (f32[16,512]{1,0:T(8,128)S(1)}, f32[16,512]{1,0:T(8,128)S(1)}, u32[]{:S(2)}, u32[]{:S(2)}) collective-permute-start(f32[16,512]{1,0:T(8,128)S(1)} %get-tuple-element.39.a), channel_id=1, source_target_pairs={{0,2},{1,3},{2,0},{3,1},{4,6},{5,7},{6,4},{7,5},{8,10},{9,11},{10,... | collective-permute-start | bytes 98312 | tf_op jit(solution)/shard_map/ppermute | solution.py:431
  21.0 5.4 %collective-permute-start.3 = (f32[32,512]{1,0:T(8,128)S(1)}, f32[32,512]{1,0:T(8,128)S(1)}, u32[]{:S(2)}, u32[]{:S(2)}) collective-permute-start(f32[32,512]{1,0:T(8,128)S(1)} %join.6.refs_12_.a.near), channel_id=1, source_target_pairs={{0,6},{1,7},{2,4},{3,5},{4,2},{5,3},{6,0},{7,1},{8,14},{9,15},{10,... | collective-permute-start | bytes 196616 | tf_op jit(solution)/shard_map/ppermute | solution.py:431
  22.9 7.1 %copy-start.3 = (bf16[2,512,192]{2,1,0:T(8,128)(2,1)S(1)}, bf16[2,512,192]{2,1,0:T(8,128)(2,1)}, u32[]{:S(2)}) copy-start(bf16[2,512,192]{2,1,0:T(8,128)(2,1)} %constant.15.clone.forward) | copy-start | bytes 1179652
  26.5 3.6 %collective-permute-start.5 = (f32[64,512]{1,0:T(8,128)S(1)}, f32[64,512]{1,0:T(8,128)S(1)}, u32[]{:S(2)}, u32[]{:S(2)}) collective-permute-start(f32[64,512]{1,0:T(8,128)S(1)} %join.7), channel_id=1, source_target_pairs={{0,1},{1,0},{2,3},{3,2},{4,5},{5,4},{6,7},{7,6},{8,9},{9,8},{10,11... | collective-permute-start | bytes 393224 | tf_op jit(solution)/shard_map/ppermute | solution.py:431
  28.6 4.1 %collective-permute-start.6 = (f32[16,256]{1,0:T(8,128)S(1)}, f32[16,256]{1,0:T(8,128)S(1)}, u32[]{:S(2)}, u32[]{:S(2)}) collective-permute-start(f32[16,256]{1,0:T(8,128)S(1)} %get-tuple-element.51.refs_2_), channel_id=1, source_target_pairs={{0,128},{8,136},{16,144},{24,152},{32,160},{40,168},{48,176},{56,1... | collective-permute-start | bytes 49160 | tf_op jit(solution)/shard_map/ppermute | solution.py:508
  32.9 3.6 %collective-permute-start.7 = (f32[16,512]{1,0:T(8,128)S(1)}, f32[16,512]{1,0:T(8,128)S(1)}, u32[]{:S(2)}, u32[]{:S(2)}) collective-permute-start(f32[16,512]{1,0:T(8,128)S(1)} %relative.4.a), channel_id=1, source_target_pairs={{0,2},{1,3},{2,0},{3,1},{4,6},{5,7},{6,4},{7,5},{8,10},{9,11},{10,... | collective-permute-start | bytes 98312 | tf_op jit(solution)/shard_map/ppermute | solution.py:431
  33.4 6.1 %collective-permute-start.10 = (bf16[8,16,128]{2,1,0:T(8,128)(2,1)S(1)}, bf16[8,16,128]{2,1,0:T(8,128)(2,1)S(1)}, u32[]{:S(2)}, u32[]{:S(2)}) collective-permute-start(bf16[8,16,128]{2,1,0:T(8,128)(2,1)S(1)} %get-tuple-element.56), channel_id=1, source_target_pairs={{0,248},{8,16},{16,8},{24,32},{32,24},{40,48},{48,40},{56,64},{64,... | collective-permute-start | bytes 98312 | tf_op jit(solution)/shard_map/ppermute | solution.py:449
  36.4 3.1 %collective-permute-start.9 = (bf16[8,16,128]{2,1,0:T(8,128)(2,1)S(1)}, bf16[8,16,128]{2,1,0:T(8,128)(2,1)S(1)}, u32[]{:S(2)}, u32[]{:S(2)}) collective-permute-start(bf16[8,16,128]{2,1,0:T(8,128)(2,1)S(1)} %get-tuple-element.55), channel_id=1, source_target_pairs={{0,8},{8,0},{16,24},{24,16},{32,40},{40,32},{48,56},{56,48},{64,72... | collective-permute-start | bytes 98312 | tf_op jit(solution)/shard_map/ppermute | solution.py:448
  36.5 4.7 %collective-permute-start.8 = (f32[32,512]{1,0:T(8,128)S(1)}, f32[32,512]{1,0:T(8,128)S(1)}, u32[]{:S(2)}, u32[]{:S(2)}) collective-permute-start(f32[32,512]{1,0:T(8,128)S(1)} %join.8.refs_8_.a.near), channel_id=1, source_target_pairs={{0,6},{1,7},{2,4},{3,5},{4,2},{5,3},{6,0},{7,1},{8,14},{9,15},{10,... | collective-permute-start | bytes 196616 | tf_op jit(solution)/shard_map/ppermute | solution.py:431
  41.2 4.0 %collective-permute-start.11 = (f32[64,512]{1,0:T(8,128)S(1)}, f32[64,512]{1,0:T(8,128)S(1)}, u32[]{:S(2)}, u32[]{:S(2)}) collective-permute-start(f32[64,512]{1,0:T(8,128)S(1)} %join.9), channel_id=1, source_target_pairs={{0,1},{1,0},{2,3},{3,2},{4,5},{5,4},{6,7},{7,6},{8,9},{9,8},{10,11... | collective-permute-start | bytes 393224 | tf_op jit(solution)/shard_map/ppermute | solution.py:431
  43.9 4.1 %collective-permute-start.12 = (f32[16,256]{1,0:T(8,128)S(1)}, f32[16,256]{1,0:T(8,128)S(1)}, u32[]{:S(2)}, u32[]{:S(2)}) collective-permute-start(f32[16,256]{1,0:T(8,128)S(1)} %get-tuple-element.60.refs_2_), channel_id=1, source_target_pairs={{0,128},{8,136},{16,144},{24,152},{32,160},{40,168},{48,176},{56,1... | collective-permute-start | bytes 49160 | tf_op jit(solution)/shard_map/ppermute | solution.py:508
  48.2 4.2 %collective-permute-start.13 = (f32[16,256]{1,0:T(8,128)S(1)}, f32[16,256]{1,0:T(8,128)S(1)}, u32[]{:S(2)}, u32[]{:S(2)}) collective-permute-start(f32[16,256]{1,0:T(8,128)S(1)} %relative.5.a), channel_id=1, source_target_pairs={{0,2},{1,3},{2,0},{3,1},{4,6},{5,7},{6,4},{7,5},{8,10},{9,11},{10,... | collective-permute-start | bytes 49160 | tf_op jit(solution)/shard_map/ppermute | solution.py:431
  49.3 10.0 %collective-permute-start.16 = (bf16[8,16,128]{2,1,0:T(8,128)(2,1)S(1)}, bf16[8,16,128]{2,1,0:T(8,128)(2,1)S(1)}, u32[]{:S(2)}, u32[]{:S(2)}) collective-permute-start(bf16[8,16,128]{2,1,0:T(8,128)(2,1)S(1)} %get-tuple-element.64), channel_id=1, source_target_pairs={{0,8},{8,0},{16,24},{24,16},{32,40},{40,32},{48,56},{56,48},{64,72... | collective-permute-start | bytes 98312 | tf_op jit(solution)/shard_map/ppermute | solution.py:448
  50.1 9.2 %collective-permute-start.17 = (bf16[8,16,128]{2,1,0:T(8,128)(2,1)S(1)}, bf16[8,16,128]{2,1,0:T(8,128)(2,1)S(1)}, u32[]{:S(2)}, u32[]{:S(2)}) collective-permute-start(bf16[8,16,128]{2,1,0:T(8,128)(2,1)S(1)} %get-tuple-element.65), channel_id=1, source_target_pairs={{0,248},{8,16},{16,8},{24,32},{32,24},{40,48},{48,40},{56,64},{64,... | collective-permute-start | bytes 98312 | tf_op jit(solution)/shard_map/ppermute | solution.py:449
  52.4 4.0 %collective-permute-start.14 = (f32[32,256]{1,0:T(8,128)S(1)}, f32[32,256]{1,0:T(8,128)S(1)}, u32[]{:S(2)}, u32[]{:S(2)}) collective-permute-start(f32[32,256]{1,0:T(8,128)S(1)} %join.10.refs_9_.a.near), channel_id=1, source_target_pairs={{0,6},{1,7},{2,4},{3,5},{4,2},{5,3},{6,0},{7,1},{8,14},{9,15},{10,... | collective-permute-start | bytes 98312 | tf_op jit(solution)/shard_map/ppermute | solution.py:431
  56.4 4.2 %collective-permute-start.15 = (f32[64,256]{1,0:T(8,128)S(1)}, f32[64,256]{1,0:T(8,128)S(1)}, u32[]{:S(2)}, u32[]{:S(2)}) collective-permute-start(f32[64,256]{1,0:T(8,128)S(1)} %join.11), channel_id=1, source_target_pairs={{0,1},{1,0},{2,3},{3,2},{4,5},{5,4},{6,7},{7,6},{8,9},{9,8},{10,11... | collective-permute-start | bytes 196616 | tf_op jit(solution)/shard_map/ppermute | solution.py:431

commit v7 on v6

--- a/solution.py
+++ b/solution.py
@@ -19,11 +19,13 @@
 OWN = 16
 ROWS = 32
 HALF = ROWS // 2
-INV = OWN
-RATIO = 32
-LIMIT = 33
-FACING = 34
-MINE = 48
+RATIO = 16
+LIMIT = 17
+FACING = 18
+STIFF = 19
+MASS = 20
+MINE = 32
+STEP = 8
 CMAX = 256
 DOFS = ROWS * BLK
 F32 = jnp.float32
@@ -145,7 +147,7 @@
         hot_o[r * BLK : (r + 1) * BLK, :] = jnp.where(in_block + r * BLK == wanted, 1.0, 0.0).astype(BF16)
     swap_o[...] = one_hot(small_i[1])
     live = lax.broadcasted_iota(jnp.int32, (1, CMAX), 1) < count[0]
-    mine_o[2 * OWN :, :] = jnp.zeros((MINE - 2 * OWN, CMAX), F32)
+    mine_o[OWN:, :] = jnp.zeros((MINE - OWN, CMAX), F32)
     mine_o[RATIO : RATIO + 1, :] = small_f[1] / small_f[0]
     mine_o[LIMIT : LIMIT + 1, :] = jnp.where(live, small_f[0], 0.0)
     mine_o[FACING : FACING + 1, :] = small_i[1].astype(F32)
@@ -153,6 +155,7 @@
         jnp.int32, (BLK, BLK), 1
     )
     ones = jnp.ones((OWN, BLK), BF16)
+    upper = lax.broadcasted_iota(jnp.int32, (OWN, BLK), 0) < OWN // 2
     zero = jnp.zeros((BLK, BLK), BF16)
     for move in moves[4:7]:
         move.wait()
@@ -167,10 +170,11 @@
         inv_o[:, at] = inverse
         inner_o[r] = disp.astype(BF16)
         parts[: 3 * OWN, at] = split3(disp)
-        parts[3 * OWN :, at] = split3(dynamic)
+        parts[3 * OWN :, at] = jnp.where(upper, s_diag, m_diag).astype(BF16)
     listed = dot(parts[...], hot_o[...])
     mine_o[:OWN, :] = sum3(listed[: 3 * OWN])
-    mine_o[INV : INV + OWN, :] = 1.0 / sum3(listed[3 * OWN :])
+    mine_o[STIFF : STIFF + 1, :] = listed[3 * OWN : 3 * OWN + 1]
+    mine_o[MASS : MASS + 1, :] = listed[4 * OWN - 1 :]
     put_edges(place, inner_o, even_o, odd_o)
     place_o[0] = place[0]
     place_o[1] = place[1]
@@ -179,7 +183,7 @@
     moves[8].wait()
 
 
-def relative_kernel(mine, far, swap, *refs, first, final):
+def relative_kernel(freq, place, mine, far, swap, *refs, first, final):
     if first:
         out, swap_far = refs[-2:]
         wanted = far[FACING : FACING + 1, :].astype(jnp.int32)
@@ -187,8 +191,12 @@
         near_disp, far_disp = mine[:OWN, :], far[:OWN, :]
     else:
         swap_far, force, near_lin, far_lin, _, out = refs
-        near_disp = near_lin[...] - force[:, :CMAX] * mine[INV : INV + OWN, :]
-        far_disp = far_lin[...] - force[:, CMAX:] * far[INV : INV + OWN, :]
+        factor = own_factor(freq, place)
+        factor = jnp.concatenate([factor, factor], axis=1)
+        near_dyn = mine[STIFF : STIFF + 1, :] - factor * mine[MASS : MASS + 1, :]
+        far_dyn = far[STIFF : STIFF + 1, :] - factor * far[MASS : MASS + 1, :]
+        near_disp = near_lin[...] - force[:, :CMAX] / near_dyn
+        far_disp = far_lin[...] - force[:, CMAX:] / far_dyn
     facing = sum3(dot(split3(far_disp), swap[...]))
     out[:, :CMAX] = (near_disp - facing) * mine[RATIO : RATIO + 1, :]
     if not final:
@@ -336,8 +344,8 @@
         residual = lin_block(lin_a, lin_b, r) - spread(add, hot[at, :])
         residual_b[:, at] = residual
         disp_b[:, at] = disp[:, at] + residual * inv[:, at]
-        if r % BAND == BAND - 1:
-            part, ready = r // BAND, pl.ds((r + 1 - BAND) * BLK, BAND * BLK)
+        if r % STEP == STEP - 1:
+            part, ready = r // STEP, pl.ds((r + 1 - STEP) * BLK, STEP * BLK)
             moves.append(pltpu.make_async_copy(disp_b.at[:, ready], disp_o.at[:, ready], sems.at[0, part]))
             moves.append(pltpu.make_async_copy(residual_b.at[:, ready], residual_o.at[:, ready], sems.at[1, part]))
             for move in moves[-2:]:
@@ -405,7 +413,7 @@
             pltpu.VMEM(FULL, F32),
             pltpu.VMEM((2, 1, CMAX), jnp.int32),
             pltpu.VMEM((2, 1, CMAX), F32),
-            pltpu.VMEM((6 * OWN, DOFS), BF16),
+            pltpu.VMEM((4 * OWN, DOFS), BF16),
             pltpu.SemaphoreType.DMA((9,)),
         ],
         compiler_params=params(),
@@ -481,12 +489,12 @@
         made = pl.pallas_call(
             functools.partial(relative_kernel, first=first, final=final),
             out_shape=(shape(wide_list),) + ((shape((CMAX, CMAX), BF16),) if first else ()),
-            in_specs=[VM] * len(given),
+            in_specs=[SM, SM] + [VM] * len(given),
             out_specs=(VM,) * (2 if first else 1),
             compiler_params=params(),
             cost_estimate=cost(0.2),
             name="relative",
-        )(*given)
+        )(frequency, place, *given)
         relative = made[0]
         if first:
             swap_far = made[1]
@@ -526,7 +534,7 @@
                 scratch_shapes=[
                     pltpu.VMEM(FULL, F32),
                     pltpu.VMEM(FULL, F32),
-                    pltpu.SemaphoreType.DMA((2, ROWS // BAND)),
+                    pltpu.SemaphoreType.DMA((2, ROWS // STEP)),
                 ],
                 compiler_params=params(),
                 name="finish",

time: 63 us -> 62.8 us (level)
  transfers between devices with their start and end apart: 18 -> 18, of which waited for: 3 -> 4; matrix products, arithmetic and copies ran while one was open for 0% -> 0% of each run, Pallas kernels for 26% -> 26%
where the time goes in v7:
time: 62.8 us; the launch traced here: 62.7 us
  starting transfers between devices  35.1 us (56%)
  Pallas kernels  22.5 us (36%)
  waiting for transfers between devices  2.94 us (5%)
  between operations  2.17 us (3%)
    ppermute x9, starting transfers between devices, flipped(): return lax.ppermute(x, 'harm', [(i, i ^ bits) for i in range(devices)])  15.9 us
    pallas_call x6, Pallas kernels, product(): pl.pallas_call(functools.partial(product_kernel, edges=edges, first=first...  12.4 us
    ppermute x3, starting transfers between devices, local(): odd_in = lax.ppermute(odd, 'comp', odds)  10.3 us
    ppermute x1, starting transfers between devices, local(): far = lax.ppermute(mine, 'comp', facing)  3.83 us
    pallas_call x1, Pallas kernels, local(): pl.pallas_call(init_kernel, out_shape=(shape(BLOCKED, BF16), shape(EDGE,...  3.53 us
    pallas_call x3, Pallas kernels, local(): pl.pallas_call(functools.partial(time_kernel, final=final), out_shape=sha...  2.93 us
    ppermute x2, starting transfers between devices, local(): far_lin = lax.ppermute(near_lin, 'comp', facing)  2.77 us
    ppermute x3, starting transfers between devices, local(): even_in = lax.ppermute(even, 'comp', evens)  2.28 us
  transfers between devices with their start and end apart: 18, of which 4 were waited for; matrix products, arithmetic and copies ran while one was open for 0% of the time, Pallas kernels for 26%

profile of v7, /device:TPU:1, one launch (start us, length us, event | category | flops | bytes accessed | tf_op | source)
XLA Modules:
  0.0 62.7 jit_solution(8666198272778080029)
XLA Ops:
  2.0 3.5 %init.1 = (bf16[32,16,128]{2,1,0:T(8,128)(2,1)S(1)}, bf16[8,16,128]{2,1,0:T(8,128)(2,1)S(1)}, bf16[8,16,128]{2,1,0:T(8,128)(2,1)S(1)}, f32[16,4096]{1,0:T(8,128)...) custom-call(f32[1]{0:T(128)S(6)} %copy.15.freq.refs_1_, ...), custom_call_target="tpu_custom_call" | custom-call | flops 3000000000 | bytes 9000000 | tf_op jit(solution)/shard_map/init/pallas_call | solution.py:400
  5.5 3.8 %collective-permute-start = (f32[32,256]{1,0:T(8,128)S(1)}, f32[32,256]{1,0:T(8,128)S(1)}, u32[]{:S(2)}, u32[]{:S(2)}) collective-permute-start(f32[32,256]{1,0:T(8,128)S(1)} %get-tuple-element.35.mine), channel_id=1, source_target_pairs={{0,128},{8,136},{16,144},{24,152},{32,160},{40,168},{48,176},{56,1... | collective-permute-start | bytes 98312 | tf_op jit(solution)/shard_map/ppermute | solution.py:441
  9.4 1.6 %collective-permute-start.1 = (bf16[8,16,128]{2,1,0:T(8,128)(2,1)S(1)}, bf16[8,16,128]{2,1,0:T(8,128)(2,1)S(1)}, u32[]{:S(2)}, u32[]{:S(2)}) collective-permute-start(bf16[8,16,128]{2,1,0:T(8,128)(2,1)S(1)} %get-tuple-element.37), channel_id=1, source_target_pairs={{0,8},{8,0},{16,24},{24,16},{32,40},{40,32},{48,56},{56,48},{64,72... | collective-permute-start | bytes 98312 | tf_op jit(solution)/shard_map/ppermute | solution.py:456
  11.0 5.2 %collective-permute-start.4 = (bf16[8,16,128]{2,1,0:T(8,128)(2,1)S(1)}, bf16[8,16,128]{2,1,0:T(8,128)(2,1)S(1)}, u32[]{:S(2)}, u32[]{:S(2)}) collective-permute-start(bf16[8,16,128]{2,1,0:T(8,128)(2,1)S(1)} %get-tuple-element.47), channel_id=1, source_target_pairs={{0,248},{8,16},{16,8},{24,32},{32,24},{40,48},{48,40},{56,64},{64,... | collective-permute-start | bytes 98312 | tf_op jit(solution)/shard_map/ppermute | solution.py:457
  16.3 1.3 %collective-permute-start.2 = (f32[16,512]{1,0:T(8,128)S(1)}, f32[16,512]{1,0:T(8,128)S(1)}, u32[]{:S(2)}, u32[]{:S(2)}) collective-permute-start(f32[16,512]{1,0:T(8,128)S(1)} %get-tuple-element.39.a), channel_id=1, source_target_pairs={{0,2},{1,3},{2,0},{3,1},{4,6},{5,7},{6,4},{7,5},{8,10},{9,11},{10,... | collective-permute-start | bytes 98312 | tf_op jit(solution)/shard_map/ppermute | solution.py:439
  17.7 3.4 %inside.3 = (f32[16,2048]{1,0:T(8,128)S(1)}, f32[16,256]{1,0:T(8,128)S(1)}, bf16[16,1024,256]{2,1,0:T(8,128)(2,1)S(1)}) custom-call(s32[8,32]{1,0:T(8,128)S(4)} %get-tuple-element.40.refs_0_, f32[1]{0:T(128)S(6)} %copy.15.freq.refs_1_, s32[3]{0:T(128)S(4)} %get-tuple-element.34.place.refs_2_, bf16[32,16,128]{2,1,0:T(8,128)(2,1)S(1)} %get-tuple-element.41.refs_3_, ...), custom_call_target="tpu_custom_call" | custom-call | flops 3000000000 | bytes 9000000 | tf_op jit(solution)/shard_map/inside/pallas_call | solution.py:468
  21.1 1.9 %collective-permute-start.3 = (f32[32,512]{1,0:T(8,128)S(1)}, f32[32,512]{1,0:T(8,128)S(1)}, u32[]{:S(2)}, u32[]{:S(2)}) collective-permute-start(f32[32,512]{1,0:T(8,128)S(1)} %join.6.refs_12_.a.near), channel_id=1, source_target_pairs={{0,6},{1,7},{2,4},{3,5},{4,2},{5,3},{6,0},{7,1},{8,14},{9,15},{10,... | collective-permute-start | bytes 196616 | tf_op jit(solution)/shard_map/ppermute | solution.py:439
  23.0 3.5 %edges.3 = (f32[16,2048]{1,0:T(8,128)S(1)}, f32[16,256]{1,0:T(8,128)S(1)}, bf16[16,1024,256]{2,1,0:T(8,128)(2,1)S(1)}) custom-call(s32[8,32]{1,0:T(8,128)S(4)} %get-tuple-element.40.refs_0_, f32[1]{0:T(128)S(6)} %copy.15.freq.refs_1_, s32[3]{0:T(128)S(4)} %get-tuple-element.34.place.refs_2_, bf16[32,16,128]{2,1,0:T(8,128)(2,1)S(1)} %get-tuple-element.41.refs_3_, ...), custom_call_target="tpu_custom_call" | custom-call | flops 3000000000 | bytes 9000000 | tf_op jit(solution)/shard_map/edges/pallas_call | solution.py:468
  26.5 2.2 %collective-permute-start.5 = (f32[64,512]{1,0:T(8,128)S(1)}, f32[64,512]{1,0:T(8,128)S(1)}, u32[]{:S(2)}, u32[]{:S(2)}) collective-permute-start(f32[64,512]{1,0:T(8,128)S(1)} %join.7), channel_id=1, source_target_pairs={{0,1},{1,0},{2,3},{3,2},{4,5},{5,4},{6,7},{7,6},{8,9},{9,8},{10,11... | collective-permute-start | bytes 393224 | tf_op jit(solution)/shard_map/ppermute | solution.py:439
  28.7 1.4 %collective-permute-start.6 = (f32[16,256]{1,0:T(8,128)S(1)}, f32[16,256]{1,0:T(8,128)S(1)}, u32[]{:S(2)}, u32[]{:S(2)}) collective-permute-start(f32[16,256]{1,0:T(8,128)S(1)} %get-tuple-element.51.refs_2_), channel_id=1, source_target_pairs={{0,128},{8,136},{16,144},{24,152},{32,160},{40,168},{48,176},{56,1... | collective-permute-start | bytes 49160 | tf_op jit(solution)/shard_map/ppermute | solution.py:516
  30.1 1.1 %time.3.force.refs_1_ = f32[16,512]{1,0:T(8,128)S(1)} custom-call(s32[3]{0:T(128)S(4)} %get-tuple-element.34.place.refs_2_, f32[32,512]{1,0:T(8,128)S(1)} %join.6.refs_12_.a.near, f32[32,512]{1,0:T(8,128)S(1)} %collective-permute-done.3.b.opposite, f32[64,512]{1,0:T(8,128)S(1)} %collective-permute-done.5.across, bf16[2,512,192]{2,1,0:T(8,128)(2,1)S(1)} %copy-done.3, ...), custom_call_target="tpu_custom_call" | custom-call | flops 10000000 | bytes 30000 | tf_op jit(solution)/shard_map/time/pallas_call | solution.py:518
  31.2 0.8 %update.2 = (bf16[32,16,128]{2,1,0:T(8,128)(2,1)S(1)}, bf16[8,16,128]{2,1,0:T(8,128)(2,1)S(1)}, bf16[8,16,128]{2,1,0:T(8,128)(2,1)S(1)}) custom-call(s32[3]{0:T(128)S(4)} %get-tuple-element.34.place.refs_2_, f32[16,512]{1,0:T(8,128)S(1)} %time.3.force.refs_1_, bf16[4096,256]{1,0:T(8,128)(2,1)S(1)} %get-tuple-element.44.refs_7_.refs_9_.hot.refs_6_.refs_8_, ...), custom_call_target="tpu_custom_call" | custom-call | flops 10000000 | bytes 30000 | tf_op jit(solution)/shard_map/update/pallas_call | solution.py:543
  32.0 0.8 %collective-permute-done.6.refs_3_ = f32[16,256]{1,0:T(8,128)S(1)} collective-permute-done((f32[16,256]{1,0:T(8,128)S(1)}, f32[16,256]{1,0:T(8,128)S(1)}, u32[]{:S(2)}, u32[]{:S(2)}) %collective-permute-start.6) | collective-permute-done | bytes 16416 | tf_op jit(solution)/shard_map/ppermute | solution.py:516
  33.4 2.9 %collective-permute-start.10 = (bf16[8,16,128]{2,1,0:T(8,128)(2,1)S(1)}, bf16[8,16,128]{2,1,0:T(8,128)(2,1)S(1)}, u32[]{:S(2)}, u32[]{:S(2)}) collective-permute-start(bf16[8,16,128]{2,1,0:T(8,128)(2,1)S(1)} %get-tuple-element.56), channel_id=1, source_target_pairs={{0,248},{8,16},{16,8},{24,32},{32,24},{40,48},{48,40},{56,64},{64,... | collective-permute-start | bytes 98312 | tf_op jit(solution)/shard_map/ppermute | solution.py:457
  36.3 1.5 %collective-permute-start.8 = (f32[32,512]{1,0:T(8,128)S(1)}, f32[32,512]{1,0:T(8,128)S(1)}, u32[]{:S(2)}, u32[]{:S(2)}) collective-permute-start(f32[32,512]{1,0:T(8,128)S(1)} %join.8.refs_8_.a.near), channel_id=1, source_target_pairs={{0,6},{1,7},{2,4},{3,5},{4,2},{5,3},{6,0},{7,1},{8,14},{9,15},{10,... | collective-permute-start | bytes 196616 | tf_op jit(solution)/shard_map/ppermute | solution.py:439
  37.8 1.5 %inside.4 = (f32[16,2048]{1,0:T(8,128)S(1)}, f32[16,256]{1,0:T(8,128)S(1)}) custom-call(s32[8,32]{1,0:T(8,128)S(4)} %get-tuple-element.40.refs_0_, f32[1]{0:T(128)S(6)} %copy.15.freq.refs_1_, s32[3]{0:T(128)S(4)} %get-tuple-element.34.place.refs_2_, bf16[32,16,128]{2,1,0:T(8,128)(2,1)S(1)} %get-tuple-element.52.refs_4_.refs_3_, ...), custom_call_target="tpu_custom_call" | custom-call | flops 1500000000 | bytes 4500000 | tf_op jit(solution)/shard_map/inside/pallas_call | solution.py:468
  39.5 1.6 %edges.4 = (f32[16,2048]{1,0:T(8,128)S(1)}, f32[16,256]{1,0:T(8,128)S(1)}) custom-call(s32[8,32]{1,0:T(8,128)S(4)} %get-tuple-element.40.refs_0_, f32[1]{0:T(128)S(6)} %copy.15.freq.refs_1_, s32[3]{0:T(128)S(4)} %get-tuple-element.34.place.refs_2_, bf16[32,16,128]{2,1,0:T(8,128)(2,1)S(1)} %get-tuple-element.52.refs_4_.refs_3_, ...), custom_call_target="tpu_custom_call" | custom-call | flops 1500000000 | bytes 4500000 | tf_op jit(solution)/shard_map/edges/pallas_call | solution.py:468
  41.2 2.7 %collective-permute-start.11 = (f32[64,512]{1,0:T(8,128)S(1)}, f32[64,512]{1,0:T(8,128)S(1)}, u32[]{:S(2)}, u32[]{:S(2)}) collective-permute-start(f32[64,512]{1,0:T(8,128)S(1)} %join.9), channel_id=1, source_target_pairs={{0,1},{1,0},{2,3},{3,2},{4,5},{5,4},{6,7},{7,6},{8,9},{9,8},{10,11... | collective-permute-start | bytes 393224 | tf_op jit(solution)/shard_map/ppermute | solution.py:439
  43.9 1.3 %collective-permute-start.12 = (f32[16,256]{1,0:T(8,128)S(1)}, f32[16,256]{1,0:T(8,128)S(1)}, u32[]{:S(2)}, u32[]{:S(2)}) collective-permute-start(f32[16,256]{1,0:T(8,128)S(1)} %get-tuple-element.60.refs_2_), channel_id=1, source_target_pairs={{0,128},{8,136},{16,144},{24,152},{32,160},{40,168},{48,176},{56,1... | collective-permute-start | bytes 49160 | tf_op jit(solution)/shard_map/ppermute | solution.py:516
  45.2 1.1 %time.4.force.refs_1_ = f32[16,512]{1,0:T(8,128)S(1)} custom-call(s32[3]{0:T(128)S(4)} %get-tuple-element.34.place.refs_2_, f32[32,512]{1,0:T(8,128)S(1)} %join.8.refs_8_.a.near, f32[32,512]{1,0:T(8,128)S(1)} %collective-permute-done.8.b.opposite, f32[64,512]{1,0:T(8,128)S(1)} %collective-permute-done.11.across, bf16[2,512,192]{2,1,0:T(8,128)(2,1)S(1)} %copy-done.3, ...), custom_call_target="tpu_custom_call" | custom-call | flops 10000000 | bytes 30000 | tf_op jit(solution)/shard_map/time/pallas_call | solution.py:518
  46.4 0.8 %update.3 = (bf16[32,16,128]{2,1,0:T(8,128)(2,1)S(1)}, bf16[8,16,128]{2,1,0:T(8,128)(2,1)S(1)}, bf16[8,16,128]{2,1,0:T(8,128)(2,1)S(1)}, f32[16,4096]{1,0:T(8,128)S(1)}) custom-call(s32[3]{0:T(128)S(4)} %get-tuple-element.34.place.refs_2_, f32[16,512]{1,0:T(8,128)S(1)} %time.4.force.refs_1_, ...), custom_call_target="tpu_custom_call" | custom-call | flops 10000000 | bytes 30000 | tf_op jit(solution)/shard_map/update/pallas_call | solution.py:543
  47.1 0.9 %collective-permute-done.12.refs_3_ = f32[16,256]{1,0:T(8,128)S(1)} collective-permute-done((f32[16,256]{1,0:T(8,128)S(1)}, f32[16,256]{1,0:T(8,128)S(1)}, u32[]{:S(2)}, u32[]{:S(2)}) %collective-permute-start.12) | collective-permute-done | bytes 16416 | tf_op jit(solution)/shard_map/ppermute | solution.py:516
  48.2 1.2 %collective-permute-start.13 = (f32[16,256]{1,0:T(8,128)S(1)}, f32[16,256]{1,0:T(8,128)S(1)}, u32[]{:S(2)}, u32[]{:S(2)}) collective-permute-start(f32[16,256]{1,0:T(8,128)S(1)} %relative.5.a), channel_id=1, source_target_pairs={{0,2},{1,3},{2,0},{3,1},{4,6},{5,7},{6,4},{7,5},{8,10},{9,11},{10,... | collective-permute-start | bytes 49160 | tf_op jit(solution)/shard_map/ppermute | solution.py:439
  49.3 0.6 %collective-permute-start.16 = (bf16[8,16,128]{2,1,0:T(8,128)(2,1)S(1)}, bf16[8,16,128]{2,1,0:T(8,128)(2,1)S(1)}, u32[]{:S(2)}, u32[]{:S(2)}) collective-permute-start(bf16[8,16,128]{2,1,0:T(8,128)(2,1)S(1)} %get-tuple-element.64), channel_id=1, source_target_pairs={{0,8},{8,0},{16,24},{24,16},{32,40},{40,32},{48,56},{56,48},{64,72... | collective-permute-start | bytes 98312 | tf_op jit(solution)/shard_map/ppermute | solution.py:456
  50.0 2.3 %collective-permute-start.17 = (bf16[8,16,128]{2,1,0:T(8,128)(2,1)S(1)}, bf16[8,16,128]{2,1,0:T(8,128)(2,1)S(1)}, u32[]{:S(2)}, u32[]{:S(2)}) collective-permute-start(bf16[8,16,128]{2,1,0:T(8,128)(2,1)S(1)} %get-tuple-element.65), channel_id=1, source_target_pairs={{0,248},{8,16},{16,8},{24,32},{32,24},{40,48},{48,40},{56,64},{64,... | collective-permute-start | bytes 98312 | tf_op jit(solution)/shard_map/ppermute | solution.py:457
  52.2 1.7 %collective-permute-start.14 = (f32[32,256]{1,0:T(8,128)S(1)}, f32[32,256]{1,0:T(8,128)S(1)}, u32[]{:S(2)}, u32[]{:S(2)}) collective-permute-start(f32[32,256]{1,0:T(8,128)S(1)} %join.10.refs_9_.a.near), channel_id=1, source_target_pairs={{0,6},{1,7},{2,4},{3,5},{4,2},{5,3},{6,0},{7,1},{8,14},{9,15},{10,... | collective-permute-start | bytes 98312 | tf_op jit(solution)/shard_map/ppermute | solution.py:439
  53.9 1.2 %inside.5.rest_0_.lin_a = f32[16,2048]{1,0:T(8,128)S(1)} custom-call(s32[8,32]{1,0:T(8,128)S(4)} %get-tuple-element.40.refs_0_, f32[1]{0:T(128)S(6)} %copy.15.freq.refs_1_, s32[3]{0:T(128)S(4)} %get-tuple-element.34.place.refs_2_, bf16[32,16,128]{2,1,0:T(8,128)(2,1)S(1)} %get-tuple-element.61.refs_4_.refs_3_, ...), custom_call_target="tpu_custom_call" | custom-call | flops 1500000000 | bytes 4500000 | tf_op jit(solution)/shard_map/inside/pallas_call | solution.py:468
  55.1 1.1 %collective-permute-done.14.b.opposite = f32[32,256]{1,0:T(8,128)S(1)} collective-permute-done((f32[32,256]{1,0:T(8,128)S(1)}, f32[32,256]{1,0:T(8,128)S(1)}, u32[]{:S(2)}, u32[]{:S(2)}) %collective-permute-start.14) | collective-permute-done | bytes 32800 | tf_op jit(solution)/shard_map/ppermute | solution.py:439
  56.2 2.9 %collective-permute-start.15 = (f32[64,256]{1,0:T(8,128)S(1)}, f32[64,256]{1,0:T(8,128)S(1)}, u32[]{:S(2)}, u32[]{:S(2)}) collective-permute-start(f32[64,256]{1,0:T(8,128)S(1)} %join.11), channel_id=1, source_target_pairs={{0,1},{1,0},{2,3},{3,2},{4,5},{5,4},{6,7},{7,6},{8,9},{9,8},{10,11... | collective-permute-start | bytes 196616 | tf_op jit(solution)/shard_map/ppermute | solution.py:439
  59.1 1.2 %edges.5.lin_b = f32[16,2048]{1,0:T(8,128)S(1)} custom-call(s32[8,32]{1,0:T(8,128)S(4)} %get-tuple-element.40.refs_0_, f32[1]{0:T(128)S(6)} %copy.15.freq.refs_1_, s32[3]{0:T(128)S(4)} %get-tuple-element.34.place.refs_2_, bf16[32,16,128]{2,1,0:T(8,128)(2,1)S(1)} %get-tuple-element.61.refs_4_.refs_3_, ...), custom_call_target="tpu_custom_call" | custom-call | flops 1500000000 | bytes 4500000 | tf_op jit(solution)/shard_map/edges/pallas_call | solution.py:468
  60.4 0.7 %time.5.force = f32[16,256]{1,0:T(8,128)S(1)} custom-call(s32[3]{0:T(128)S(4)} %get-tuple-element.34.place.refs_2_, f32[32,256]{1,0:T(8,128)S(1)} %join.10.refs_9_.a.near, f32[32,256]{1,0:T(8,128)S(1)} %collective-permute-done.14.b.opposite, f32[64,256]{1,0:T(8,128)S(1)} %collective-permute-done.15.across, bf16[2,512,192]{2,1,0:T(8,128)(2,1)S(1)} %copy-done.3, ...), custom_call_target="tpu_custom_call" | custom-call | flops 10000000 | bytes 30000 | tf_op jit(solution)/shard_map/time/pallas_call | solution.py:518
  61.0 1.5 %finish.1 = (f32[16,4096]{1,0:T(8,128)}, f32[16,4096]{1,0:T(8,128)}) custom-call(f32[16,256]{1,0:T(8,128)S(1)} %time.5.force, bf16[4096,256]{1,0:T(8,128)(2,1)S(1)} %get-tuple-element.44.refs_7_.refs_9_.hot.refs_6_.refs_8_, f32[16,2048]{1,0:T(8,128)S(1)} %inside.5.rest_0_.lin_a, f32[16,2048]{1,0:T(8,128)S(1)} %edges.5.lin_b, ...), custom_call_target="tpu_custom_call" | custom-call | tf_op jit(solution)/shard_map/finish/pallas_call | solution.py:529
  (35 shorter events, 1.3 us)
Async XLA Ops:
  2.0 15.6 %copy-start = (bf16[32,8,128,128]{3,2,1,0:T(8,128)(2,1)S(1)}, bf16[32,8,128,128]{3,2,1,0:T(8,128)(2,1)}, u32[]{:S(2)}) copy-start(bf16[32,8,128,128]{3,2,1,0:T(8,128)(2,1)} %refs_6_.2) | copy-start | bytes 25165828
  2.0 15.6 %copy-start.1 = (bf16[32,8,128,128]{3,2,1,0:T(8,128)(2,1)S(1)}, bf16[32,8,128,128]{3,2,1,0:T(8,128)(2,1)}, u32[]{:S(2)}) copy-start(bf16[32,8,128,128]{3,2,1,0:T(8,128)(2,1)} %refs_7_.2) | copy-start | bytes 25165828
  2.0 15.6 %copy-start.2 = (f32[16,4096]{1,0:T(8,128)S(1)}, f32[16,4096]{1,0:T(8,128)}, u32[]{:S(2)}) copy-start(f32[16,4096]{1,0:T(8,128)} %refs_7_.4) | copy-start | bytes 786436
  5.5 10.6 %collective-permute-start = (f32[32,256]{1,0:T(8,128)S(1)}, f32[32,256]{1,0:T(8,128)S(1)}, u32[]{:S(2)}, u32[]{:S(2)}) collective-permute-start(f32[32,256]{1,0:T(8,128)S(1)} %get-tuple-element.35.mine), channel_id=1, source_target_pairs={{0,128},{8,136},{16,144},{24,152},{32,160},{40,168},{48,176},{56,1... | collective-permute-start | bytes 98312 | tf_op jit(solution)/shard_map/ppermute | solution.py:441
  9.4 6.8 %collective-permute-start.1 = (bf16[8,16,128]{2,1,0:T(8,128)(2,1)S(1)}, bf16[8,16,128]{2,1,0:T(8,128)(2,1)S(1)}, u32[]{:S(2)}, u32[]{:S(2)}) collective-permute-start(bf16[8,16,128]{2,1,0:T(8,128)(2,1)S(1)} %get-tuple-element.37), channel_id=1, source_target_pairs={{0,8},{8,0},{16,24},{24,16},{32,40},{40,32},{48,56},{56,48},{64,72... | collective-permute-start | bytes 98312 | tf_op jit(solution)/shard_map/ppermute | solution.py:456
  11.0 11.9 %collective-permute-start.4 = (bf16[8,16,128]{2,1,0:T(8,128)(2,1)S(1)}, bf16[8,16,128]{2,1,0:T(8,128)(2,1)S(1)}, u32[]{:S(2)}, u32[]{:S(2)}) collective-permute-start(bf16[8,16,128]{2,1,0:T(8,128)(2,1)S(1)} %get-tuple-element.47), channel_id=1, source_target_pairs={{0,248},{8,16},{16,8},{24,32},{32,24},{40,48},{48,40},{56,64},{64,... | collective-permute-start | bytes 98312 | tf_op jit(solution)/shard_map/ppermute | solution.py:457
  16.3 4.7 %collective-permute-start.2 = (f32[16,512]{1,0:T(8,128)S(1)}, f32[16,512]{1,0:T(8,128)S(1)}, u32[]{:S(2)}, u32[]{:S(2)}) collective-permute-start(f32[16,512]{1,0:T(8,128)S(1)} %get-tuple-element.39.a), channel_id=1, source_target_pairs={{0,2},{1,3},{2,0},{3,1},{4,6},{5,7},{6,4},{7,5},{8,10},{9,11},{10,... | collective-permute-start | bytes 98312 | tf_op jit(solution)/shard_map/ppermute | solution.py:439
  21.1 5.4 %collective-permute-start.3 = (f32[32,512]{1,0:T(8,128)S(1)}, f32[32,512]{1,0:T(8,128)S(1)}, u32[]{:S(2)}, u32[]{:S(2)}) collective-permute-start(f32[32,512]{1,0:T(8,128)S(1)} %join.6.refs_12_.a.near), channel_id=1, source_target_pairs={{0,6},{1,7},{2,4},{3,5},{4,2},{5,3},{6,0},{7,1},{8,14},{9,15},{10,... | collective-permute-start | bytes 196616 | tf_op jit(solution)/shard_map/ppermute | solution.py:439
  23.0 7.1 %copy-start.3 = (bf16[2,512,192]{2,1,0:T(8,128)(2,1)S(1)}, bf16[2,512,192]{2,1,0:T(8,128)(2,1)}, u32[]{:S(2)}) copy-start(bf16[2,512,192]{2,1,0:T(8,128)(2,1)} %constant.15.clone.forward) | copy-start | bytes 1179652
  26.5 3.6 %collective-permute-start.5 = (f32[64,512]{1,0:T(8,128)S(1)}, f32[64,512]{1,0:T(8,128)S(1)}, u32[]{:S(2)}, u32[]{:S(2)}) collective-permute-start(f32[64,512]{1,0:T(8,128)S(1)} %join.7), channel_id=1, source_target_pairs={{0,1},{1,0},{2,3},{3,2},{4,5},{5,4},{6,7},{7,6},{8,9},{9,8},{10,11... | collective-permute-start | bytes 393224 | tf_op jit(solution)/shard_map/ppermute | solution.py:439
  28.7 4.1 %collective-permute-start.6 = (f32[16,256]{1,0:T(8,128)S(1)}, f32[16,256]{1,0:T(8,128)S(1)}, u32[]{:S(2)}, u32[]{:S(2)}) collective-permute-start(f32[16,256]{1,0:T(8,128)S(1)} %get-tuple-element.51.refs_2_), channel_id=1, source_target_pairs={{0,128},{8,136},{16,144},{24,152},{32,160},{40,168},{48,176},{56,1... | collective-permute-start | bytes 49160 | tf_op jit(solution)/shard_map/ppermute | solution.py:516
  32.9 3.4 %collective-permute-start.7 = (f32[16,512]{1,0:T(8,128)S(1)}, f32[16,512]{1,0:T(8,128)S(1)}, u32[]{:S(2)}, u32[]{:S(2)}) collective-permute-start(f32[16,512]{1,0:T(8,128)S(1)} %relative.4.a), channel_id=1, source_target_pairs={{0,2},{1,3},{2,0},{3,1},{4,6},{5,7},{6,4},{7,5},{8,10},{9,11},{10,... | collective-permute-start | bytes 98312 | tf_op jit(solution)/shard_map/ppermute | solution.py:439
  33.4 6.1 %collective-permute-start.10 = (bf16[8,16,128]{2,1,0:T(8,128)(2,1)S(1)}, bf16[8,16,128]{2,1,0:T(8,128)(2,1)S(1)}, u32[]{:S(2)}, u32[]{:S(2)}) collective-permute-start(bf16[8,16,128]{2,1,0:T(8,128)(2,1)S(1)} %get-tuple-element.56), channel_id=1, source_target_pairs={{0,248},{8,16},{16,8},{24,32},{32,24},{40,48},{48,40},{56,64},{64,... | collective-permute-start | bytes 98312 | tf_op jit(solution)/shard_map/ppermute | solution.py:457
  36.3 3.2 %collective-permute-start.9 = (bf16[8,16,128]{2,1,0:T(8,128)(2,1)S(1)}, bf16[8,16,128]{2,1,0:T(8,128)(2,1)S(1)}, u32[]{:S(2)}, u32[]{:S(2)}) collective-permute-start(bf16[8,16,128]{2,1,0:T(8,128)(2,1)S(1)} %get-tuple-element.55), channel_id=1, source_target_pairs={{0,8},{8,0},{16,24},{24,16},{32,40},{40,32},{48,56},{56,48},{64,72... | collective-permute-start | bytes 98312 | tf_op jit(solution)/shard_map/ppermute | solution.py:456
  36.3 4.8 %collective-permute-start.8 = (f32[32,512]{1,0:T(8,128)S(1)}, f32[32,512]{1,0:T(8,128)S(1)}, u32[]{:S(2)}, u32[]{:S(2)}) collective-permute-start(f32[32,512]{1,0:T(8,128)S(1)} %join.8.refs_8_.a.near), channel_id=1, source_target_pairs={{0,6},{1,7},{2,4},{3,5},{4,2},{5,3},{6,0},{7,1},{8,14},{9,15},{10,... | collective-permute-start | bytes 196616 | tf_op jit(solution)/shard_map/ppermute | solution.py:439
  41.2 4.1 %collective-permute-start.11 = (f32[64,512]{1,0:T(8,128)S(1)}, f32[64,512]{1,0:T(8,128)S(1)}, u32[]{:S(2)}, u32[]{:S(2)}) collective-permute-start(f32[64,512]{1,0:T(8,128)S(1)} %join.9), channel_id=1, source_target_pairs={{0,1},{1,0},{2,3},{3,2},{4,5},{5,4},{6,7},{7,6},{8,9},{9,8},{10,11... | collective-permute-start | bytes 393224 | tf_op jit(solution)/shard_map/ppermute | solution.py:439
  43.9 4.1 %collective-permute-start.12 = (f32[16,256]{1,0:T(8,128)S(1)}, f32[16,256]{1,0:T(8,128)S(1)}, u32[]{:S(2)}, u32[]{:S(2)}) collective-permute-start(f32[16,256]{1,0:T(8,128)S(1)} %get-tuple-element.60.refs_2_), channel_id=1, source_target_pairs={{0,128},{8,136},{16,144},{24,152},{32,160},{40,168},{48,176},{56,1... | collective-permute-start | bytes 49160 | tf_op jit(solution)/shard_map/ppermute | solution.py:516
  48.2 4.1 %collective-permute-start.13 = (f32[16,256]{1,0:T(8,128)S(1)}, f32[16,256]{1,0:T(8,128)S(1)}, u32[]{:S(2)}, u32[]{:S(2)}) collective-permute-start(f32[16,256]{1,0:T(8,128)S(1)} %relative.5.a), channel_id=1, source_target_pairs={{0,2},{1,3},{2,0},{3,1},{4,6},{5,7},{6,4},{7,5},{8,10},{9,11},{10,... | collective-permute-start | bytes 49160 | tf_op jit(solution)/shard_map/ppermute | solution.py:439
  49.3 9.8 %collective-permute-start.16 = (bf16[8,16,128]{2,1,0:T(8,128)(2,1)S(1)}, bf16[8,16,128]{2,1,0:T(8,128)(2,1)S(1)}, u32[]{:S(2)}, u32[]{:S(2)}) collective-permute-start(bf16[8,16,128]{2,1,0:T(8,128)(2,1)S(1)} %get-tuple-element.64), channel_id=1, source_target_pairs={{0,8},{8,0},{16,24},{24,16},{32,40},{40,32},{48,56},{56,48},{64,72... | collective-permute-start | bytes 98312 | tf_op jit(solution)/shard_map/ppermute | solution.py:456
  50.0 9.2 %collective-permute-start.17 = (bf16[8,16,128]{2,1,0:T(8,128)(2,1)S(1)}, bf16[8,16,128]{2,1,0:T(8,128)(2,1)S(1)}, u32[]{:S(2)}, u32[]{:S(2)}) collective-permute-start(bf16[8,16,128]{2,1,0:T(8,128)(2,1)S(1)} %get-tuple-element.65), channel_id=1, source_target_pairs={{0,248},{8,16},{16,8},{24,32},{32,24},{40,48},{48,40},{56,64},{64,... | collective-permute-start | bytes 98312 | tf_op jit(solution)/shard_map/ppermute | solution.py:457
  52.2 4.0 %collective-permute-start.14 = (f32[32,256]{1,0:T(8,128)S(1)}, f32[32,256]{1,0:T(8,128)S(1)}, u32[]{:S(2)}, u32[]{:S(2)}) collective-permute-start(f32[32,256]{1,0:T(8,128)S(1)} %join.10.refs_9_.a.near), channel_id=1, source_target_pairs={{0,6},{1,7},{2,4},{3,5},{4,2},{5,3},{6,0},{7,1},{8,14},{9,15},{10,... | collective-permute-start | bytes 98312 | tf_op jit(solution)/shard_map/ppermute | solution.py:439
  56.2 4.2 %collective-permute-start.15 = (f32[64,256]{1,0:T(8,128)S(1)}, f32[64,256]{1,0:T(8,128)S(1)}, u32[]{:S(2)}, u32[]{:S(2)}) collective-permute-start(f32[64,256]{1,0:T(8,128)S(1)} %join.11), channel_id=1, source_target_pairs={{0,1},{1,0},{2,3},{3,2},{4,5},{5,4},{6,7},{7,6},{8,9},{9,8},{10,11... | collective-permute-start | bytes 196616 | tf_op jit(solution)/shard_map/ppermute | solution.py:439
